TPU v7x, 32 devices: a whole 2x2x4 slice. The times are simulated.
32 devices in a mesh: groups: 2 (over y), expert: 4 (over z), tensor: 4 (over x, core), sub: 1.
Axes of the slice: x: 2, y: 2, z: 4, core: 2. Of those that a mesh axis runs over, the one named last changes fastest.
Arguments:
- hidden_rows: bfloat16 [4, 320, 4096], P(None, ('groups', 'expert', 'tensor')), parts along dimension 1, may hold values from -6 to 6
- expert_ids: int32 [4, 320, 8], P(None, ('groups', 'expert', 'tensor')), parts along dimension 1, may hold values from 0 to 15, all different within a row; in each aligned block of 10 rows (0 to 9, 10 to 19, ..., all dimensions but the last counted through in order) at most 5 rows name the same one
- accepted: int32 [4, 64], P(None, ('groups', 'expert', 'tensor')), parts along dimension 1, may hold values from 0 to 4
- norm_gain: float32 [4096], replicated, may hold values from 0.5 to 1.5
- router: bfloat16 [4096, 16], replicated, may hold values from -0.0625 to 0.0625
- gate_weight: bfloat16 [16, 4096, 768], P(('expert', 'tensor'), None, 'sub'), may hold values from -0.09375 to 0.09375
- up_weight: bfloat16 [16, 4096, 768], P(('expert', 'tensor'), None, 'sub'), may hold values from -0.09375 to 0.09375
- down_weight: bfloat16 [16, 768, 4096], P(('expert', 'tensor'), 'sub'), may hold values from -0.21875 to 0.21875
- draft_gain: float32 [4096], replicated, may hold values from 0.5 to 1.5
- draft_gate: bfloat16 [4096, 6144], P(None, ('expert', 'tensor')), may hold values from -0.09375 to 0.09375
- draft_up: bfloat16 [4096, 6144], P(None, ('expert', 'tensor')), may hold values from -0.09375 to 0.09375
- draft_down: bfloat16 [6144, 4096], P(('expert', 'tensor')), may hold values from -0.078125 to 0.078125
- final_gain: float32 [4096], replicated, may hold values from 0.5 to 1.5
Outputs:
- verified: bfloat16 [4, 320, 4096], P(None, ('groups', 'expert', 'tensor')), parts along dimension 1
- draft_out: bfloat16 [4, 64, 4096], P(None, ('groups', 'expert', 'tensor')), parts along dimension 1
There are 2 independent parts, one for each index of `groups`. A program takes and returns all parts, laid end to end along the dimension named above; an argument that names none is the same for every part. Nothing has to cross between parts.
Inputs may be any that keep to these rules, and one draw needn't show every extreme that they name: `expert_ids`: the 8 ids of a row differ. In each aligned block of 10 rows no expert is named by more than 5 rows, and in some block one expert is named by exactly 5 rows.
All inputs are finite; a program needn't handle non-finite values.
Results may differ from a plain program's by a relative error of at most 0.0068.
Values may be sent and summed in bfloat16 or wider, within the bound.
No kernel may reach another device: no remote copies, remote signals or barrier semaphores. Data moves between devices by JAX's collectives and lax.ppermute only.
A program may use at most 128 MiB of HBM per device.

v0:
```python
import jax
import jax.numpy as jnp
from jax import lax
from jax.sharding import PartitionSpec as P

EPSILON = 1e-06


def rms_scale(values, weights):
    values = values.astype(jnp.float32)
    mean_square = jnp.mean(values * values, axis=-1, keepdims=True)
    return values * lax.rsqrt(mean_square + EPSILON) * weights


def local(
    hidden_rows,
    expert_ids,
    accepted,
    norm_gain,
    router,
    gate_weight,
    up_weight,
    down_weight,
    draft_gain,
    draft_gate,
    draft_up,
    draft_down,
    final_gain,
):
    rounds_total = hidden_rows.shape[0]
    rows_here = hidden_rows.shape[1]
    feature_width = hidden_rows.shape[2]
    top_count = expert_ids.shape[2]
    expert_count = router.shape[1]
    requests_here = accepted.shape[1]
    draft_rows = rows_here // requests_here
    capacity = max(2, (rows_here * top_count + expert_count - 1) // expert_count)
    expert_range = jnp.arange(expert_count, dtype=jnp.int32)
    slot_range = jnp.arange(capacity, dtype=jnp.float32)
    highest = lax.Precision.HIGHEST
    verified_list = []
    draft_list = []
    for round_index in range(rounds_total):
        rows = hidden_rows[round_index]
        chosen_ids = expert_ids[round_index]
        normed = rms_scale(rows, norm_gain).astype(jnp.bfloat16)
        logits = jnp.dot(normed, router, preferred_element_type=jnp.float32)
        expert_hot = (chosen_ids[:, :, None] == expert_range[None, None, :]).astype(jnp.float32)
        chosen = jnp.sum(expert_hot * logits[:, None, :], axis=2)
        exp_values = jnp.exp(chosen)
        gate_share = exp_values / jnp.sum(exp_values, axis=1, keepdims=True)
        flat_hot = expert_hot.reshape(rows_here * top_count, expert_count)
        rank_values = jnp.cumsum(flat_hot, axis=0) - 1.0
        positions = jnp.sum(rank_values * flat_hot, axis=1).reshape(rows_here, top_count)
        slot_hot = (positions[:, :, None] == slot_range[None, None, :]).astype(jnp.float32)
        send_table = jnp.einsum("rke,rkc->ecr", expert_hot, slot_hot)
        gate_table = jnp.einsum(
            "rke,rkc->ecr", expert_hot * gate_share[:, :, None], slot_hot, precision=highest
        )
        outgoing = jnp.einsum(
            "ecr,rd->ecd",
            send_table.astype(jnp.bfloat16),
            normed,
            preferred_element_type=jnp.float32,
        ).astype(jnp.bfloat16)
        received = lax.all_to_all(
            outgoing, ("expert", "tensor"), split_axis=0, concat_axis=0, tiled=True
        )
        sources = received.shape[0]
        item_count = received.shape[1]
        flat_rows = received.reshape(sources * item_count, feature_width)
        gate_values = jnp.dot(flat_rows, gate_weight[0], preferred_element_type=jnp.float32)
        up_values = jnp.dot(flat_rows, up_weight[0], preferred_element_type=jnp.float32)
        active = (jax.nn.silu(gate_values) * up_values).astype(jnp.bfloat16)
        partial_out = jnp.dot(active, down_weight[0], preferred_element_type=jnp.float32)
        partial_out = partial_out.reshape(sources, item_count, feature_width)
        processed = lax.psum(partial_out.astype(jnp.bfloat16), "sub")
        returned = lax.all_to_all(
            processed, ("expert", "tensor"), split_axis=0, concat_axis=0, tiled=True
        )
        mixed_rows = rows.astype(jnp.float32) + jnp.einsum(
            "ecr,ecd->rd", gate_table, returned.astype(jnp.float32), precision=highest
        )
        verified = mixed_rows.astype(jnp.bfloat16)
        wanted = jnp.arange(requests_here, dtype=jnp.int32) * draft_rows + accepted[round_index]
        select_table = (jnp.arange(rows_here, dtype=jnp.int32)[None, :] == wanted[:, None]).astype(
            jnp.bfloat16
        )
        features = jnp.dot(select_table, verified, preferred_element_type=jnp.float32).astype(
            jnp.bfloat16
        )
        draft_input = rms_scale(features, draft_gain).astype(jnp.bfloat16)
        piece_rows = lax.all_gather(draft_input, ("expert", "tensor"), axis=0, tiled=True)
        gate_part = jnp.dot(piece_rows, draft_gate, preferred_element_type=jnp.float32)
        up_part = jnp.dot(piece_rows, draft_up, preferred_element_type=jnp.float32)
        unit_rows = (jax.nn.silu(gate_part) * up_part).astype(jnp.bfloat16)
        summed = lax.psum_scatter(
            jnp.dot(unit_rows, draft_down, preferred_element_type=jnp.float32),
            ("expert", "tensor"),
            scatter_dimension=0,
            tiled=True,
        )
        draft_out = rms_scale(features.astype(jnp.float32) + summed, final_gain).astype(
            jnp.bfloat16
        )
        verified_list.append(verified)
        draft_list.append(draft_out)
    return (jnp.stack(verified_list, axis=0), jnp.stack(draft_list, axis=0))


def solution(mesh):
    placed = (
        P(None, ("groups", "expert", "tensor"), None),
        P(None, ("groups", "expert", "tensor"), None),
        P(None, ("groups", "expert", "tensor")),
        P(),
        P(),
        P(("expert", "tensor"), None, "sub"),
        P(("expert", "tensor"), None, "sub"),
        P(("expert", "tensor"), "sub", None),
        P(),
        P(None, ("expert", "tensor")),
        P(None, ("expert", "tensor")),
        P(("expert", "tensor"), None),
        P(),
    )
    return jax.shard_map(
        local,
        mesh=mesh,
        in_specs=placed,
        out_specs=(
            P(None, ("groups", "expert", "tensor"), None),
            P(None, ("groups", "expert", "tensor"), None),
        ),
        check_vma=False,
    )
```

profile of v0, /device:TPU:0, one launch (start us, length us, event | category | flops | bytes accessed | tf_op | source)
XLA Modules:
  0.0 500.1 jit_solution(5771111974080170452)
XLA Ops:
  15.2 7.4 %all-to-all-start.6 = ((bf16[16,5,4096]{2,1,0:T(8,128)(2,1)}), bf16[16,5,4096]{2,1,0:T(8,128)(2,1)}, u32[]{:S(2)}, u32[]{:S(2)}) async-start(bf16[16,5,4096]{2,1,0:T(8,128)(2,1)} %copy.76), calls=%async_computation.6 | async-start | bytes 2097152 | tf_op jit(solution)/shard_map/all_to_all | solution.py:66
  60.6 6.0 %all-to-all-start.4 = ((bf16[16,5,4096]{2,1,0:T(8,128)(2,1)}), bf16[16,5,4096]{2,1,0:T(8,128)(2,1)}, u32[]{:S(2)}, u32[]{:S(2)}) async-start(bf16[16,5,4096]{2,1,0:T(8,128)(2,1)} %copy.67), calls=%async_computation.4 | async-start | bytes 2097152 | tf_op jit(solution)/shard_map/all_to_all | solution.py:66
  71.2 18.4 %all-to-all-done.4 = bf16[16,5,4096]{2,1,0:T(8,128)(2,1)} async-done(((bf16[16,5,4096]{2,1,0:T(8,128)(2,1)}), bf16[16,5,4096]{2,1,0:T(8,128)(2,1)}, u32[]{:S(2)}, u32[]{:S(2)}) %all-to-all-start.4) | async-done | bytes 655392 | tf_op jit(solution)/shard_map/all_to_all | solution.py:66
  89.6 6.9 %all-to-all-start = ((bf16[16,5,4096]{2,1,0:T(8,128)(2,1)}), bf16[16,5,4096]{2,1,0:T(8,128)(2,1)}, u32[]{:S(2)}, u32[]{:S(2)}) async-start(bf16[16,5,4096]{2,1,0:T(8,128)(2,1)} %copy.49), calls=%async_computation | async-start | bytes 2097152 | tf_op jit(solution)/shard_map/all_to_all | solution.py:66
  104.6 14.9 %all-to-all-done = bf16[16,5,4096]{2,1,0:T(8,128)(2,1)} async-done(((bf16[16,5,4096]{2,1,0:T(8,128)(2,1)}), bf16[16,5,4096]{2,1,0:T(8,128)(2,1)}, u32[]{:S(2)}, u32[]{:S(2)}) %all-to-all-start) | async-done | bytes 655392 | tf_op jit(solution)/shard_map/all_to_all | solution.py:66
  119.5 6.9 %all-to-all-start.2 = ((bf16[16,5,4096]{2,1,0:T(8,128)(2,1)}), bf16[16,5,4096]{2,1,0:T(8,128)(2,1)}, u32[]{:S(2)}, u32[]{:S(2)}) async-start(bf16[16,5,4096]{2,1,0:T(8,128)(2,1)} %copy.58), calls=%async_computation.2 | async-start | bytes 2097152 | tf_op jit(solution)/shard_map/all_to_all | solution.py:66
  130.7 4.7 fusion.63
  144.9 4.6 all-to-all-done.2
  149.4 6.9 %all-to-all-start.5 = ((bf16[16,5,4096]{2,1,0:T(8,128)(2,1)}), bf16[16,5,4096]{2,1,0:T(8,128)(2,1)}, u32[]{:S(2)}, u32[]{:S(2)}) async-start(bf16[16,5,4096]{2,1,0:T(8,128)(2,1)} %copy.69), calls=%async_computation.5 | async-start | bytes 2097152 | tf_op jit(solution)/shard_map/all_to_all | solution.py:78
  160.6 4.6 fusion.69
  174.7 4.6 all-to-all-done.5
  179.4 6.9 %all-to-all-start.1 = ((bf16[16,5,4096]{2,1,0:T(8,128)(2,1)}), bf16[16,5,4096]{2,1,0:T(8,128)(2,1)}, u32[]{:S(2)}, u32[]{:S(2)}) async-start(bf16[16,5,4096]{2,1,0:T(8,128)(2,1)} %copy.51), calls=%async_computation.1 | async-start | bytes 2097152 | tf_op jit(solution)/shard_map/all_to_all | solution.py:78
  186.3 4.2 fusion.20
  190.6 4.7 fusion.66
  204.7 4.6 all-to-all-done.1
  209.3 6.9 %all-to-all-start.3 = ((bf16[16,5,4096]{2,1,0:T(8,128)(2,1)}), bf16[16,5,4096]{2,1,0:T(8,128)(2,1)}, u32[]{:S(2)}, u32[]{:S(2)}) async-start(bf16[16,5,4096]{2,1,0:T(8,128)(2,1)} %copy.60), calls=%async_computation.3 | async-start | bytes 2097152 | tf_op jit(solution)/shard_map/all_to_all | solution.py:78
  220.5 4.6 fusion.60
  239.2 6.9 %all-to-all-start.7 = ((bf16[16,5,4096]{2,1,0:T(8,128)(2,1)}), bf16[16,5,4096]{2,1,0:T(8,128)(2,1)}, u32[]{:S(2)}, u32[]{:S(2)}) async-start(bf16[16,5,4096]{2,1,0:T(8,128)(2,1)} %copy.78), calls=%async_computation.7 | async-start | bytes 2097152 | tf_op jit(solution)/shard_map/all_to_all | solution.py:78
  254.2 14.9 %all-to-all-done.7 = bf16[16,5,4096]{2,1,0:T(8,128)(2,1)} async-done(((bf16[16,5,4096]{2,1,0:T(8,128)(2,1)}), bf16[16,5,4096]{2,1,0:T(8,128)(2,1)}, u32[]{:S(2)}, u32[]{:S(2)}) %all-to-all-start.7) | async-done | bytes 655392 | tf_op jit(solution)/shard_map/all_to_all | solution.py:78
  273.3 24.7 %all-gather.3 = bf16[16,2,4096]{2,1,0:T(2,128)(2,1)} all-gather(bf16[1,2,4096]{2,1,0:T(2,128)(2,1)S(1)} %get-tuple-element.27), channel_id=1, replica_groups=mesh['groups'=2,'expert'=4,'tensor'=4,'sub'=1] {'expert','tensor'}, dimensions={0}, use_global_device_ids=true | all-gather | bytes 278528 | tf_op jit(solution)/shard_map/all_gather | solution.py:93
  299.0 19.8 %all-gather.2 = bf16[16,2,4096]{2,1,0:T(2,128)(2,1)} all-gather(bf16[1,2,4096]{2,1,0:T(2,128)(2,1)} %get-tuple-element.26), channel_id=1, replica_groups=mesh['groups'=2,'expert'=4,'tensor'=4,'sub'=1] {'expert','tensor'}, dimensions={0}, use_global_device_ids=true | all-gather | bytes 278528 | tf_op jit(solution)/shard_map/all_gather | solution.py:93
  333.2 20.8 %all-gather.1 = bf16[16,2,4096]{2,1,0:T(2,128)(2,1)} all-gather(bf16[1,2,4096]{2,1,0:T(2,128)(2,1)S(1)} %copy-done.13), channel_id=1, replica_groups=mesh['groups'=2,'expert'=4,'tensor'=4,'sub'=1] {'expert','tensor'}, dimensions={0}, use_global_device_ids=true | all-gather | bytes 278528 | tf_op jit(solution)/shard_map/all_gather | solution.py:93
  362.3 19.6 %all-gather = bf16[16,2,4096]{2,1,0:T(2,128)(2,1)} all-gather(bf16[1,2,4096]{2,1,0:T(2,128)(2,1)S(1)} %get-tuple-element.24), channel_id=1, replica_groups=mesh['groups'=2,'expert'=4,'tensor'=4,'sub'=1] {'expert','tensor'}, dimensions={0}, use_global_device_ids=true | all-gather | bytes 278528 | tf_op jit(solution)/shard_map/all_gather | solution.py:93
  393.5 93.5 %all-reduce.7.cloned.1.call-done = (f32[32,4096]{1,0:T(8,128)}, f32[32,4096]{1,0:T(8,128)}, f32[32,4096]{1,0:T(8,128)}, f32[32,4096]{1,0:T(8,128)}) async-done(((f32[32,4096]{1,0:T(8,128)}, f32[32,4096]{1,0:T(8,128)}, f32[32,4096]{1,0:T(8,128)}, f32[32,4096]{1,0:T(8,128)}), (f32[32,4096]{1,0:T(8,128)}, f32[32,4096]{1,0:T(8,128)}, f32[32,4096]{1,0:T(8,128)}, ...) | async-done | bytes 2097168
  (206 shorter events, 166.9 us)
Async XLA Ops:
  7.2 317.8 %copy-start = (bf16[384,4096]{1,0:T(8,128)(2,1)S(1)}, bf16[384,4096]{1,0:T(8,128)(2,1)}, u32[]{:S(2)}) copy-start(bf16[384,4096]{1,0:T(8,128)(2,1)} %param.24) | copy-start | bytes 9437188
  9.1 13.5 %copy-start.12 = (f32[4096]{0:T(1024)S(1)}, f32[4096]{0:T(1024)}, u32[]{:S(2)}) copy-start(f32[4096]{0:T(1024)} %param.16) | copy-start | bytes 49156
  9.4 14.4 %copy-start.21 = (f32[10,8]{1,0:T(8,128)}, f32[10,8]{1,0:T(8,128)S(1)}, u32[]{:S(2)}) copy-start(f32[10,8]{1,0:T(8,128)S(1)} %eq.248) | copy-start | bytes 964
  15.2 45.4 %all-to-all-start.6 = ((bf16[16,5,4096]{2,1,0:T(8,128)(2,1)}), bf16[16,5,4096]{2,1,0:T(8,128)(2,1)}, u32[]{:S(2)}, u32[]{:S(2)}) async-start(bf16[16,5,4096]{2,1,0:T(8,128)(2,1)} %copy.76), calls=%async_computation.6 | async-start | bytes 2097152 | tf_op jit(solution)/shard_map/all_to_all | solution.py:66
  28.2 7.6 %copy-start.18 = (s32[1,10,8]{1,2,0:T(8,128)S(1)}, s32[1,10,8]{1,2,0:T(8,128)}, u32[]{:S(2)}) copy-start(s32[1,10,8]{1,2,0:T(8,128)} %get-tuple-element.33) | copy-start | bytes 964
  50.5 8.4 %copy-start.16 = (s32[10,8]{1,0:T(8,128)S(1)}, s32[10,8]{1,0:T(8,128)}, u32[]{:S(2)}) copy-start(s32[10,8]{1,0:T(8,128)} %copy.56) | copy-start | bytes 964
  50.5 8.8 %copy-start.17 = (s32[10,8]{1,0:T(8,128)S(1)}, s32[10,8]{1,0:T(8,128)}, u32[]{:S(2)}) copy-start(s32[10,8]{1,0:T(8,128)} %copy.47) | copy-start | bytes 964
  51.3 7.8 %copy-start.7 = (bf16[1,10,4096]{2,0,1:T(2,128)(2,1)S(1)}, bf16[1,10,4096]{2,0,1:T(2,128)(2,1)}, u32[]{:S(2)}) copy-start(bf16[1,10,4096]{2,0,1:T(2,128)(2,1)} %get-tuple-element.16) | copy-start | bytes 245764
  51.3 7.8 %copy-start.33 = (bf16[4096,16]{0,1:T(8,128)(2,1)S(1)}, bf16[4096,16]{0,1:T(8,128)(2,1)}, u32[]{:S(2)}) copy-start(bf16[4096,16]{0,1:T(8,128)(2,1)} %param.17) | copy-start | bytes 393220
  54.7 43.6 %copy-start.15 = (s32[10,8]{1,0:T(8,128)S(1)}, s32[10,8]{1,0:T(8,128)}, u32[]{:S(2)}) copy-start(s32[10,8]{1,0:T(8,128)} %copy-done.14) | copy-start | bytes 964
  59.4 42.0 %copy-start.24 = (f32[10,8]{1,0:T(8,128)S(1)}, f32[10,8]{1,0:T(8,128)}, u32[]{:S(2)}) copy-start(f32[10,8]{1,0:T(8,128)} %copy-done.23) | copy-start | bytes 964
  60.6 29.0 %all-to-all-start.4 = ((bf16[16,5,4096]{2,1,0:T(8,128)(2,1)}), bf16[16,5,4096]{2,1,0:T(8,128)(2,1)}, u32[]{:S(2)}, u32[]{:S(2)}) async-start(bf16[16,5,4096]{2,1,0:T(8,128)(2,1)} %copy.67), calls=%async_computation.4 | async-start | bytes 2097152 | tf_op jit(solution)/shard_map/all_to_all | solution.py:66
  89.6 29.9 %all-to-all-start = ((bf16[16,5,4096]{2,1,0:T(8,128)(2,1)}), bf16[16,5,4096]{2,1,0:T(8,128)(2,1)}, u32[]{:S(2)}, u32[]{:S(2)}) async-start(bf16[16,5,4096]{2,1,0:T(8,128)(2,1)} %copy.49), calls=%async_computation | async-start | bytes 2097152 | tf_op jit(solution)/shard_map/all_to_all | solution.py:66
  119.5 29.9 %all-to-all-start.2 = ((bf16[16,5,4096]{2,1,0:T(8,128)(2,1)}), bf16[16,5,4096]{2,1,0:T(8,128)(2,1)}, u32[]{:S(2)}, u32[]{:S(2)}) async-start(bf16[16,5,4096]{2,1,0:T(8,128)(2,1)} %copy.58), calls=%async_computation.2 | async-start | bytes 2097152 | tf_op jit(solution)/shard_map/all_to_all | solution.py:66
  149.4 29.9 %all-to-all-start.5 = ((bf16[16,5,4096]{2,1,0:T(8,128)(2,1)}), bf16[16,5,4096]{2,1,0:T(8,128)(2,1)}, u32[]{:S(2)}, u32[]{:S(2)}) async-start(bf16[16,5,4096]{2,1,0:T(8,128)(2,1)} %copy.69), calls=%async_computation.5 | async-start | bytes 2097152 | tf_op jit(solution)/shard_map/all_to_all | solution.py:78
  179.4 29.9 %all-to-all-start.1 = ((bf16[16,5,4096]{2,1,0:T(8,128)(2,1)}), bf16[16,5,4096]{2,1,0:T(8,128)(2,1)}, u32[]{:S(2)}, u32[]{:S(2)}) async-start(bf16[16,5,4096]{2,1,0:T(8,128)(2,1)} %copy.51), calls=%async_computation.1 | async-start | bytes 2097152 | tf_op jit(solution)/shard_map/all_to_all | solution.py:78
  209.3 29.9 %all-to-all-start.3 = ((bf16[16,5,4096]{2,1,0:T(8,128)(2,1)}), bf16[16,5,4096]{2,1,0:T(8,128)(2,1)}, u32[]{:S(2)}, u32[]{:S(2)}) async-start(bf16[16,5,4096]{2,1,0:T(8,128)(2,1)} %copy.60), calls=%async_computation.3 | async-start | bytes 2097152 | tf_op jit(solution)/shard_map/all_to_all | solution.py:78
  230.9 15.5 %copy-start.31 = (s32[2]{0:T(128)S(1)}, s32[2]{0:T(128)}, u32[]{:S(2)}) copy-start(s32[2]{0:T(128)} %fusion.195) | copy-start | bytes 28
  230.9 19.1 %copy-start.29 = (s32[2]{0:T(128)S(1)}, s32[2]{0:T(128)}, u32[]{:S(2)}) copy-start(s32[2]{0:T(128)} %fusion.194) | copy-start | bytes 28
  232.3 21.6 %copy-start.30 = (s32[2]{0:T(128)S(1)}, s32[2]{0:T(128)}, u32[]{:S(2)}) copy-start(s32[2]{0:T(128)} %fusion.193) | copy-start | bytes 28
  235.2 36.2 %copy-start.28 = (s32[2]{0:T(128)S(1)}, s32[2]{0:T(128)}, u32[]{:S(2)}) copy-start(s32[2]{0:T(128)} %fusion.192) | copy-start | bytes 28
  239.2 29.9 %all-to-all-start.7 = ((bf16[16,5,4096]{2,1,0:T(8,128)(2,1)}), bf16[16,5,4096]{2,1,0:T(8,128)(2,1)}, u32[]{:S(2)}, u32[]{:S(2)}) async-start(bf16[16,5,4096]{2,1,0:T(8,128)(2,1)} %copy.78), calls=%async_computation.7 | async-start | bytes 2097152 | tf_op jit(solution)/shard_map/all_to_all | solution.py:78
  246.1 240.9 %all-reduce.7.cloned.1.call-start = ((), (), s32[]{:S(2)}) async-start(), calls=%async_computation.8 | async-start | bytes 4194304
  390.0 101.2 %copy-start.20 = (f32[4096]{0:T(1024)S(1)}, f32[4096]{0:T(1024)}, u32[]{:S(2)}) copy-start(f32[4096]{0:T(1024)} %param.25) | copy-start | bytes 49156
  (21 other events, 82.0 us)
Sparse Core Ops, SparseCore 0:
  390.2 96.7 all-reduce.6
where the time goes:
time: 503 us; the launch traced here: 500 us
  waiting for transfers between devices  160 us (32%)
  matrix products  107 us (21%)
  blocking collectives  84.8 us (17%)
  starting transfers between devices  55.2 us (11%)
  local copies, waits for them, and re-layouts  48.1 us (10%)
  other arithmetic  29.9 us (6%)
  between operations  15.1 us (3%)
    unnamed x2, waiting for transfers between devices  93.5 us
    all_gather x4, blocking collectives, local(): lax.all_gather(draft_input, ('expert', 'tensor'), axis=0, tiled=True)  84.8 us
    all_to_all x4, waiting for transfers between devices, local(): lax.all_to_all(outgoing, ('expert', 'tensor'), split_axis=0, concat_axis=...  37.9 us
    all_to_all x4, waiting for transfers between devices, local(): lax.all_to_all(processed, ('expert', 'tensor'), split_axis=0, concat_axis...  28.1 us
    all_to_all x4, starting transfers between devices, local(): lax.all_to_all(processed, ('expert', 'tensor'), split_axis=0, concat_axis...  27.7 us
    all_to_all x4, starting transfers between devices, local(): lax.all_to_all(outgoing, ('expert', 'tensor'), split_axis=0, concat_axis=...  27.2 us
    dot_general x4, matrix products, local(): jnp.dot(flat_rows, up_weight[0], preferred_element_type=jnp.float32)  18.6 us
    dot_general x4, matrix products, local(): jnp.dot(flat_rows, gate_weight[0], preferred_element_type=jnp.float32)  17 us
  transfers between devices with their start and end apart: 9, of which 8 were waited for; matrix products, arithmetic and copies ran while one was open for 27% of the time, Pallas kernels for 0%

commit v1 on v0

v1 whole, which is shorter than its diff:
```python
import functools

import jax
import jax.numpy as jnp
from jax import lax
from jax.experimental import pallas as pl
from jax.experimental.pallas import tpu as pltpu
from jax.sharding import PartitionSpec as P

EPSILON = 1e-06
BF = jnp.bfloat16
F32 = jnp.float32
LANES = 128
VMEM_LIMIT = 48 * 1024 * 1024


def fdot(a, b):
    return jnp.dot(a, b, preferred_element_type=F32)


def iota(shape, axis):
    return lax.broadcasted_iota(jnp.int32, shape, axis)


def accepted_column(accepted_ref, size, axis, per_round, chunk):
    shape = (size, 1) if axis == 0 else (1, size)
    request = lax.rem(iota(shape, axis), chunk)
    found = jnp.zeros(shape, jnp.int32)
    for number in range(chunk):
        value = accepted_ref[number // per_round, number % per_round]
        found = jnp.where(request == number, value, found)
    return found


def sources(accepted_ref, size, axis, per_round, chunk, draft):
    shape = (size, 1) if axis == 0 else (1, size)
    place = iota(shape, axis)
    request = lax.rem(place, chunk)
    layer = lax.div(place, chunk)
    wanted = accepted_column(accepted_ref, size, axis, per_round, chunk)
    other = layer - 1
    inside = jnp.where(layer == 0, wanted, other + (other >= wanted).astype(jnp.int32))
    return lax.div(request, per_round), lax.rem(request, per_round) * draft + inside


def prep_kernel(sizes, accepted_ref, hidden_ref, ids_ref, gain_ref, router_ref, *outs):
    rounds, rows, experts, top, per_round, draft = sizes
    chunk = rounds * per_round
    total = rounds * rows
    width = hidden_ref.shape[2]
    ext_refs, hid_refs = outs[: len(outs) // 2], outs[len(outs) // 2 :]
    source_round, source_row = sources(accepted_ref, total, 0, per_round, chunk, draft)
    lane = iota((rows, LANES), 1)
    moved = None
    for number in range(rounds):
        raw = hidden_ref[number]
        values = raw.astype(F32)
        mean_square = jnp.mean(values * values, axis=-1, keepdims=True)
        normed = (values * lax.rsqrt(mean_square + EPSILON) * gain_ref[...]).astype(BF)
        logits = fdot(normed, router_ref[...])
        ids = ids_ref[number]
        expert = iota((rows, experts), 1)
        named = ids[:, 0:1] == expert
        for k in range(1, top):
            named = named | (ids[:, k : k + 1] == expert)
        powers = jnp.where(named, jnp.exp(logits), 0.0)
        share = powers / jnp.sum(powers, axis=1, keepdims=True)
        high = share.astype(BF)
        rest = (share - high.astype(F32)).astype(BF)
        place = (
            (source_round == number) & (source_row == iota((total, rows), 1))
        ).astype(BF)
        parts = [fdot(place, normed), fdot(place, raw), fdot(place, high), fdot(place, rest)]
        moved = parts if moved is None else [a + b for a, b in zip(moved, parts)]
    normed, raw, high, rest = [part.astype(BF) for part in moved]
    pad = jnp.zeros((total, LANES - 2 * experts), BF)
    tail = jnp.concatenate([high, rest] + ([pad] if 2 * experts < LANES else []), axis=1)
    first = 0
    for ext_ref, hid_ref in zip(ext_refs, hid_refs):
        count = ext_ref.shape[0]
        ext_ref[:, :width] = normed[first : first + count]
        ext_ref[:, width:] = tail[first : first + count]
        hid_ref[...] = raw[first : first + count]
        first += count


def prep(hidden, ids, accepted, gain, router, counts):
    rounds, rows, width = hidden.shape
    sizes = (rounds, rows, router.shape[1], ids.shape[2], accepted.shape[1], rows // accepted.shape[1])
    vmem = pl.BlockSpec(memory_space=pltpu.VMEM)
    return pl.pallas_call(
        functools.partial(prep_kernel, sizes),
        out_shape=[jax.ShapeDtypeStruct((count, width + LANES), BF) for count in counts]
        + [jax.ShapeDtypeStruct((count, width), BF) for count in counts],
        in_specs=[pl.BlockSpec(memory_space=pltpu.SMEM)] + [vmem] * 4,
        out_specs=[vmem] * (2 * len(counts)),
        compiler_params=pltpu.CompilerParams(vmem_limit_bytes=VMEM_LIMIT),
        name="prep",
    )(accepted, hidden, ids, gain.reshape(1, width), router)


def unit_kernel(gated, steps, mark_ref, x_ref, gate_ref, up_ref, down_ref, out_ref, acc_ref):
    step = pl.program_id(1)
    width = out_ref.shape[1]
    x = x_ref[:, :width]
    gate = fdot(x, gate_ref[...])
    up = fdot(x, up_ref[...])
    active = (gate / (1.0 + jnp.exp(-gate)) * up).astype(BF)
    term = fdot(active, down_ref[...])

    @pl.when(step == 0)
    def _():
        acc_ref[...] = term

    @pl.when(step > 0)
    def _():
        acc_ref[...] += term

    @pl.when(step == steps - 1)
    def _():
        total = acc_ref[...]
        if gated:
            share = jnp.sum(x_ref[:, width:].astype(F32) * mark_ref[...], axis=1, keepdims=True)
            total = total * share
        out_ref[...] = total.astype(BF)


def units(x, mark, gate, up, down, gated, tile):
    count, columns = x.shape
    hidden, width = down.shape
    rows = min(count, 256)
    tile = min(tile, hidden)
    if hidden % tile:
        tile = hidden
    steps = hidden // tile
    return pl.pallas_call(
        functools.partial(unit_kernel, gated, steps),
        grid=(count // rows, steps),
        out_shape=jax.ShapeDtypeStruct((count, width), BF),
        in_specs=[
            pl.BlockSpec((1, LANES), lambda m, f: (0, 0)),
            pl.BlockSpec((rows, columns), lambda m, f: (m, 0)),
            pl.BlockSpec((width, tile), lambda m, f: (0, f)),
            pl.BlockSpec((width, tile), lambda m, f: (0, f)),
            pl.BlockSpec((tile, width), lambda m, f: (f, 0)),
        ],
        out_specs=pl.BlockSpec((rows, width), lambda m, f: (m, 0)),
        scratch_shapes=[pltpu.VMEM((rows, width), F32)],
        compiler_params=pltpu.CompilerParams(vmem_limit_bytes=VMEM_LIMIT),
        cost_estimate=pl.CostEstimate(
            flops=6 * count * hidden * width,
            bytes_accessed=2 * (3 * hidden * width + 2 * count * width),
            transcendentals=count * hidden,
        ),
        name="experts" if gated else "drafter",
    )(mark, x, gate, up, down)


def mid_kernel(hid_ref, gain_ref, *refs):
    verified_ref, draft_ref = refs[-2:]
    total = hid_ref[...].astype(F32) + sum(ref[...].astype(F32) for ref in refs[:-2])
    verified = total.astype(BF)
    verified_ref[...] = verified
    values = verified.astype(F32)
    mean_square = jnp.mean(values * values, axis=-1, keepdims=True)
    draft_ref[...] = (values * lax.rsqrt(mean_square + EPSILON) * gain_ref[...]).astype(BF)


def mid(hid, parts, gain):
    return pl.pallas_call(
        mid_kernel,
        out_shape=[jax.ShapeDtypeStruct(hid.shape, BF)] * 2,
        compiler_params=pltpu.CompilerParams(vmem_limit_bytes=VMEM_LIMIT),
        name="accepted_norm",
    )(hid, gain.reshape(1, -1), *parts)


def last_kernel(hid_ref, gain_ref, *refs):
    out_ref = refs[-1]
    total = hid_ref[...].astype(F32) + sum(ref[...].astype(F32) for ref in refs[:-1])
    mean_square = jnp.mean(total * total, axis=-1, keepdims=True)
    out_ref[...] = (total * lax.rsqrt(mean_square + EPSILON) * gain_ref[...]).astype(BF)


def last(hid, parts, gain):
    return pl.pallas_call(
        last_kernel,
        out_shape=jax.ShapeDtypeStruct(hid.shape, BF),
        compiler_params=pltpu.CompilerParams(vmem_limit_bytes=VMEM_LIMIT),
        name="draft_norm",
    )(hid, gain.reshape(1, -1), *parts)


def merge_kernel(sizes, groups, accepted_ref, *refs):
    rounds, rows, per_round, draft = sizes
    chunk = rounds * per_round
    out_ref = refs[-1]
    pieces = []
    first = 0
    for group in groups:
        members = refs[first : first + group]
        first += group
        if group == 1:
            pieces.append(members[0][...])
        else:
            pieces.append(sum(ref[...].astype(F32) for ref in members).astype(BF))
    total = rounds * rows
    source_round, source_row = sources(accepted_ref, total, 1, per_round, chunk, draft)
    for number in range(rounds):
        place = (
            (source_round == number) & (source_row == iota((rows, total), 0))
        ).astype(BF)
        result = None
        first = 0
        for piece in pieces:
            count = piece.shape[0]
            term = fdot(place[:, first : first + count], piece)
            result = term if result is None else result + term
            first += count
        out_ref[number] = result.astype(BF)


def merge(accepted, groups, shape, draft):
    rounds, rows, width = shape
    sizes = (rounds, rows, accepted.shape[1], draft)
    vmem = pl.BlockSpec(memory_space=pltpu.VMEM)
    flat = [array for group in groups for array in group]
    return pl.pallas_call(
        functools.partial(merge_kernel, sizes, [len(group) for group in groups]),
        out_shape=jax.ShapeDtypeStruct(shape, BF),
        in_specs=[pl.BlockSpec(memory_space=pltpu.SMEM)] + [vmem] * len(flat),
        out_specs=vmem,
        compiler_params=pltpu.CompilerParams(vmem_limit_bytes=VMEM_LIMIT),
        name="merge",
    )(accepted, *flat)


class Links:
    def __init__(self, lines, columns):
        self.lines = lines
        self.columns = columns

    def line(self, x, shift):
        n = self.lines
        return lax.ppermute(x, "expert", [(i, (i + shift) % n) for i in range(n)])

    def cross(self, x, bit):
        return lax.ppermute(x, "tensor", [(i, i ^ bit) for i in range(self.columns)])

    def gather(self, x):
        blocks = [x] + [self.line(x, shift) for shift in range(1, self.lines)]
        bit = self.columns // 2
        while bit > 1:
            blocks = blocks + [self.cross(block, bit) for block in blocks]
            bit //= 2
        whole = jnp.concatenate(blocks, axis=0)
        if bit == 1:
            whole = jnp.concatenate([whole, self.cross(whole, 1)], axis=0)
        return whole

    def scatter(self, whole):
        bit = 1
        while bit < self.columns:
            half = whole.shape[0] // 2
            keep, send = whole[:half], whole[half:]
            whole = (keep.astype(F32) + self.cross(send, bit).astype(F32)).astype(BF)
            bit *= 2
        size = whole.shape[0] // self.lines
        terms = [whole[:size]]
        for shift in range(1, self.lines):
            block = whole[shift * size : (shift + 1) * size]
            terms.append(self.line(block, -shift))
        return terms


def local(
    lines,
    columns,
    subs,
    hidden_rows,
    expert_ids,
    accepted,
    norm_gain,
    router,
    gate_weight,
    up_weight,
    down_weight,
    draft_gain,
    draft_gate,
    draft_up,
    draft_down,
    final_gain,
):
    rounds, rows, width = hidden_rows.shape
    experts = router.shape[1]
    requests = accepted.shape[1]
    draft = rows // requests
    chunk = rounds * requests
    links = Links(lines, columns)
    me = lax.axis_index("expert") * columns + lax.axis_index("tensor")
    lane = jnp.arange(LANES, dtype=jnp.int32)[None, :]
    mark = ((lane == me) | (lane == me + experts)).astype(F32)
    others = rounds * rows - chunk
    counts = [chunk, others // 2, others - others // 2]
    outs = prep(hidden_rows, expert_ids, accepted, norm_gain, router, counts)
    exts, hids = outs[:3], outs[3:]

    def routed(ext):
        whole = links.gather(ext)
        out = units(whole, mark, gate_weight[0], up_weight[0], down_weight[0], True, 256)
        terms = links.scatter(out)
        if subs > 1:
            total = sum(term.astype(F32) for term in terms)
            terms = [lax.psum(total, "sub")]
        return terms

    first = routed(exts[0])
    features, draft_in = mid(hids[0], first, draft_gain)
    second = routed(exts[1])
    whole = links.gather(draft_in)
    out = units(whole, mark, draft_gate, draft_up, draft_down, False, 128)
    third = routed(exts[2])
    draft_out = last(features, links.scatter(out), final_gain)
    verified = merge(
        accepted,
        [[features], [hids[1]] + second, [hids[2]] + third],
        hidden_rows.shape,
        draft,
    )
    return verified, draft_out.reshape(rounds, requests, width)


def solution(mesh):
    placed = (
        P(None, ("groups", "expert", "tensor"), None),
        P(None, ("groups", "expert", "tensor"), None),
        P(None, ("groups", "expert", "tensor")),
        P(),
        P(),
        P(("expert", "tensor"), None, "sub"),
        P(("expert", "tensor"), None, "sub"),
        P(("expert", "tensor"), "sub", None),
        P(),
        P(None, ("expert", "tensor")),
        P(None, ("expert", "tensor")),
        P(("expert", "tensor"), None),
        P(),
    )
    body = functools.partial(
        local, mesh.shape["expert"], mesh.shape["tensor"], mesh.shape["sub"]
    )
    return jax.shard_map(
        body,
        mesh=mesh,
        in_specs=placed,
        out_specs=(
            P(None, ("groups", "expert", "tensor"), None),
            P(None, ("groups", "expert", "tensor"), None),
        ),
        check_vma=False,
    )
```

time: 503 us -> 197 us (0.39)
  matrix products: 107 us -> 0 us
  waiting for transfers between devices: 160 us -> 74.5 us
  blocking collectives: 84.8 us -> 0 us
  Pallas kernels: 0 us -> 40.5 us
  other arithmetic: 29.9 us -> 1.11 us
  local copies, waits for them, and re-layouts: 48.1 us -> 24 us
  between operations: 15.1 us -> 1.18 us
    dot_general x44 -> x0, matrix products: 107 us -> none  [the longest x4 18.6 us: local(): jnp.dot(flat_rows, up_weight[0], preferred_element_type=jnp.float32)]
    unnamed x2 -> x0, waiting for transfers between devices: 93.5 us -> none
    all_gather x4 -> x0, blocking collectives: 84.8 us -> none  [local(): lax.all_gather(draft_input, ('expert', 'tensor'), axis=0, tiled=True)]
    ppermute x0 -> x52, waiting for transfers between devices: none -> 74.5 us  [the longest x28 55.8 us: cross(): lax.ppermute(x, 'tensor', [(i, i ^ bit) for i in range(self.columns)])]
    all_to_all x8 -> x0, waiting for transfers between devices: 66 us -> none  [the longest x4 37.9 us: local(): lax.all_to_all(outgoing, ('expert', 'tensor'), split_axis=0, concat_axis=...]
    ppermute x0 -> x52, starting transfers between devices: none -> 55.1 us  [the longest x24 31.5 us: line(): return lax.ppermute(x, 'expert', [(i, (i + shift) % n) for i in range(n)])]
    all_to_all x8 -> x0, starting transfers between devices: 54.9 us -> none  [the longest x4 27.7 us: local(): lax.all_to_all(processed, ('expert', 'tensor'), split_axis=0, concat_axis...]
    pallas_call x0 -> x8, Pallas kernels: none -> 40.5 us  [the longest x4 36.1 us: units(): pl.pallas_call(functools.partial(unit_kernel, gated, steps), grid=(count...]
  transfers between devices with their start and end apart: 9 -> 52, of which waited for: 8 -> 23; matrix products, arithmetic and copies ran while one was open for 27% -> 9% of each run, Pallas kernels for 0% -> 19%
where the time goes in v1:
time: 197 us; the launch traced here: 196 us
  waiting for transfers between devices  74.5 us (38%)
  starting transfers between devices  55.1 us (28%)
  Pallas kernels  40.5 us (21%)
  local copies, waits for them, and re-layouts  24 us (12%)
    ppermute x28, waiting for transfers between devices, cross(): lax.ppermute(x, 'tensor', [(i, i ^ bit) for i in range(self.columns)])  55.8 us
    pallas_call x4, Pallas kernels, units(): pl.pallas_call(functools.partial(unit_kernel, gated, steps), grid=(count...  36.1 us
    ppermute x24, starting transfers between devices, line(): return lax.ppermute(x, 'expert', [(i, (i + shift) % n) for i in range(n)])  31.5 us
    ppermute x28, starting transfers between devices, cross(): lax.ppermute(x, 'tensor', [(i, i ^ bit) for i in range(self.columns)])  23.6 us
    unnamed x64, local copies, waits for them, and re-layouts  21.1 us
    ppermute x24, waiting for transfers between devices, line(): return lax.ppermute(x, 'expert', [(i, (i + shift) % n) for i in range(n)])  18.7 us
  transfers between devices with their start and end apart: 52, of which 23 were waited for; matrix products, arithmetic and copies ran while one was open for 9% of the time, Pallas kernels for 19%

profile of v1, /device:TPU:0, one launch (start us, length us, event | category | flops | bytes accessed | tf_op | source)
XLA Modules:
  0.0 196.4 jit_solution(11371452943615620362)
XLA Ops:
  3.2 2.9 %prep.1 = (bf16[8,4224]{1,0:T(8,128)(2,1)}, bf16[16,4224]{1,0:T(8,128)(2,1)S(1)}, bf16[16,4224]{1,0:T(8,128)(2,1)S(1)}, bf16[8,4096]{1,0:T(8,128)(2,1)S(1)}, bf1...) custom-call(s32[4,2]{1,0:T(4,128)S(1)} %copy.19.accepted_ref, bf16[4,10,4096]{2,1,0:T(8,128)(2,1)S(1)} %copy.16.hidden_ref, ...), custom_call_target="tpu_custom_call" | custom-call | tf_op jit(solution)/shard_map/prep/pallas_call | solution.py:91
  8.1 3.0 %collective-permute-start = (bf16[8,4224]{1,0:T(8,128)(2,1)}, bf16[8,4224]{1,0:T(8,128)(2,1)}, u32[]{:S(2)}, u32[]{:S(2)}) collective-permute-start(bf16[8,4224]{1,0:T(8,128)(2,1)} %get-tuple-element.11), channel_id=1, source_target_pairs={{0,4},{4,8},{8,12},{12,0},{1,5},{5,9},{9,13},{13,1},{2,6},{6,10},{... | collective-permute-start | bytes 202760 | tf_op jit(solution)/shard_map/ppermute | solution.py:245
  11.1 2.6 %collective-permute-start.1 = (bf16[8,4224]{1,0:T(8,128)(2,1)}, bf16[8,4224]{1,0:T(8,128)(2,1)}, u32[]{:S(2)}, u32[]{:S(2)}) collective-permute-start(bf16[8,4224]{1,0:T(8,128)(2,1)} %get-tuple-element.11), channel_id=1, source_target_pairs={{0,8},{4,12},{8,0},{12,4},{1,9},{5,13},{9,1},{13,5},{2,10},{6,14},... | collective-permute-start | bytes 202760 | tf_op jit(solution)/shard_map/ppermute | solution.py:245
  21.4 2.8 %collective-permute-start.28 = (bf16[16,4224]{1,0:T(8,128)(2,1)S(1)}, bf16[16,4224]{1,0:T(8,128)(2,1)S(1)}, u32[]{:S(2)}, u32[]{:S(2)}) collective-permute-start(bf16[16,4224]{1,0:T(8,128)(2,1)S(1)} %get-tuple-element.16), channel_id=1, source_target_pairs={{0,12},{4,0},{8,4},{12,8},{1,13},{5,1},{9,5},{13,9},{2,14},{6,2},{... | collective-permute-start | bytes 405512 | tf_op jit(solution)/shard_map/ppermute | solution.py:245
  33.1 2.9 %collective-permute-start.15 = (bf16[16,4224]{1,0:T(8,128)(2,1)S(1)}, bf16[16,4224]{1,0:T(8,128)(2,1)S(1)}, u32[]{:S(2)}, u32[]{:S(2)}) collective-permute-start(bf16[16,4224]{1,0:T(8,128)(2,1)S(1)} %get-tuple-element.14), channel_id=1, source_target_pairs={{0,12},{4,0},{8,4},{12,8},{1,13},{5,1},{9,5},{13,9},{2,14},{6,2},{... | collective-permute-start | bytes 405512 | tf_op jit(solution)/shard_map/ppermute | solution.py:245
  39.0 2.4 %collective-permute-done.4 = bf16[8,4224]{1,0:T(8,128)(2,1)S(1)} collective-permute-done((bf16[8,4224]{1,0:T(8,128)(2,1)}, bf16[8,4224]{1,0:T(8,128)(2,1)S(1)}, u32[]{:S(2)}, u32[]{:S(2)}) %collective-permute-start.4) | collective-permute-done | bytes 67616 | tf_op jit(solution)/shard_map/ppermute | solution.py:248
  42.9 3.0 %collective-permute-done.5 = bf16[8,4224]{1,0:T(8,128)(2,1)S(1)} collective-permute-done((bf16[8,4224]{1,0:T(8,128)(2,1)}, bf16[8,4224]{1,0:T(8,128)(2,1)S(1)}, u32[]{:S(2)}, u32[]{:S(2)}) %collective-permute-start.5) | collective-permute-done | bytes 67616 | tf_op jit(solution)/shard_map/ppermute | solution.py:248
  47.4 3.0 %collective-permute-done.6 = bf16[8,4224]{1,0:T(8,128)(2,1)S(1)} collective-permute-done((bf16[8,4224]{1,0:T(8,128)(2,1)}, bf16[8,4224]{1,0:T(8,128)(2,1)S(1)}, u32[]{:S(2)}, u32[]{:S(2)}) %collective-permute-start.6) | collective-permute-done | bytes 67616 | tf_op jit(solution)/shard_map/ppermute | solution.py:248
  65.8 2.2 %collective-permute-done.17 = bf16[16,4224]{1,0:T(8,128)(2,1)S(1)} collective-permute-done((bf16[16,4224]{1,0:T(8,128)(2,1)S(1)}, bf16[16,4224]{1,0:T(8,128)(2,1)S(1)}, u32[]{:S(2)}, u32[]{:S(2)}) %collective-permute-start.17) | collective-permute-done | bytes 135200 | tf_op jit(solution)/shard_map/ppermute | solution.py:248
  68.1 2.9 %collective-permute-done.18 = bf16[16,4224]{1,0:T(8,128)(2,1)S(1)} collective-permute-done((bf16[16,4224]{1,0:T(8,128)(2,1)S(1)}, bf16[16,4224]{1,0:T(8,128)(2,1)S(1)}, u32[]{:S(2)}, u32[]{:S(2)}) %collective-permute-start.18) | collective-permute-done | bytes 135200 | tf_op jit(solution)/shard_map/ppermute | solution.py:248
  71.0 8.7 %experts.3 = bf16[128,4096]{1,0:T(8,128)(2,1)S(1)} custom-call(f32[1,128]{1,0:T(1,128)S(1)} %or_convert_fusion.mark_ref, bf16[128,4224]{1,0:T(8,128)(2,1)S(1)} %constant_dynamic-update-slice_fusion.8.x_ref, bf16[4096,768]{1,0:T(8,128)(2,1)} %bitcast.9, bf16[4096,768]{1,0:T(8,128)(2,1)} %bitcast.12, bf16[768,4096]{1,0:T(8,128)(2,1)} %bitcast.15), custom_call_target="tpu_custom_call" | custom-call | flops 2415919104 | bytes 20971520 | tf_op jit(solution)/shard_map/experts/pallas_call | solution.py:136
  83.0 7.4 %collective-permute-done.9 = bf16[32,4096]{1,0:T(8,128)(2,1)S(1)} collective-permute-done((bf16[32,4096]{1,0:T(8,128)(2,1)S(1)}, bf16[32,4096]{1,0:T(8,128)(2,1)S(1)}, u32[]{:S(2)}, u32[]{:S(2)}) %collective-permute-start.9) | collective-permute-done | bytes 262176 | tf_op jit(solution)/shard_map/ppermute | solution.py:248
  90.5 2.3 %collective-permute-start.11 = (bf16[8,4096]{1,0:T(8,128)(2,1)S(1)}, bf16[8,4096]{1,0:T(8,128)(2,1)S(1)}, u32[]{:S(2)}, u32[]{:S(2)}) collective-permute-start(bf16[8,4096]{1,0:T(8,128)(2,1)S(1)} %get-tuple-element.33), channel_id=1, source_target_pairs={{0,8},{4,12},{8,0},{12,4},{1,9},{5,13},{9,1},{13,5},{2,10},{6,14},... | collective-permute-start | bytes 196616 | tf_op jit(solution)/shard_map/ppermute | solution.py:245
  93.7 10.6 %experts.5 = bf16[256,4096]{1,0:T(8,128)(2,1)S(1)} custom-call(f32[1,128]{1,0:T(1,128)S(1)} %or_convert_fusion.mark_ref, bf16[256,4224]{1,0:T(8,128)(2,1)S(1)} %constant_dynamic-update-slice_fusion.42.x_ref, bf16[4096,768]{1,0:T(8,128)(2,1)} %bitcast.10, bf16[4096,768]{1,0:T(8,128)(2,1)} %bitcast.13, bf16[768,4096]{1,0:T(8,128)(2,1)} %bitcast.16), custom_call_target="tpu_custom_call" | custom-call | flops 4831838208 | bytes 23068672 | tf_op jit(solution)/shard_map/experts/pallas_call | solution.py:136
  105.8 3.2 %collective-permute-start.40 = (bf16[8,4096]{1,0:T(8,128)(2,1)S(1)}, bf16[8,4096]{1,0:T(8,128)(2,1)S(1)}, u32[]{:S(2)}, u32[]{:S(2)}) collective-permute-start(bf16[8,4096]{1,0:T(8,128)(2,1)S(1)} %get-tuple-element.17), channel_id=1, source_target_pairs={{0,8},{4,12},{8,0},{12,4},{1,9},{5,13},{9,1},{13,5},{2,10},{6,14},... | collective-permute-start | bytes 196616 | tf_op jit(solution)/shard_map/ppermute | solution.py:245
  110.2 2.1 %collective-permute-done.39 = bf16[8,4096]{1,0:T(8,128)(2,1)S(1)} collective-permute-done((bf16[8,4096]{1,0:T(8,128)(2,1)S(1)}, bf16[8,4096]{1,0:T(8,128)(2,1)S(1)}, u32[]{:S(2)}, u32[]{:S(2)}) %collective-permute-start.39) | collective-permute-done | bytes 65568 | tf_op jit(solution)/shard_map/ppermute | solution.py:245
  121.5 10.6 %experts.4 = bf16[256,4096]{1,0:T(8,128)(2,1)S(1)} custom-call(f32[1,128]{1,0:T(1,128)S(1)} %or_convert_fusion.mark_ref, bf16[256,4224]{1,0:T(8,128)(2,1)S(1)} %constant_dynamic-update-slice_fusion.25.x_ref, bf16[4096,768]{1,0:T(8,128)(2,1)} %bitcast.11, bf16[4096,768]{1,0:T(8,128)(2,1)} %bitcast.14, bf16[768,4096]{1,0:T(8,128)(2,1)} %bitcast.17), custom_call_target="tpu_custom_call" | custom-call | flops 4831838208 | bytes 23068672 | tf_op jit(solution)/shard_map/experts/pallas_call | solution.py:136
  134.0 6.1 %drafter.1 = bf16[128,4096]{1,0:T(8,128)(2,1)S(1)} custom-call(f32[1,128]{1,0:T(1,128)S(1)} %or_convert_fusion.mark_ref, bf16[128,4096]{1,0:T(8,128)(2,1)S(1)} %constant_dynamic-update-slice_fusion.59.x_ref, bf16[4096,384]{1,0:T(8,128)(2,1)S(1)} %copy-done, bf16[4096,384]{1,0:T(8,128)(2,1)} %up_ref.1, bf16[384,4096]{1,0:T(8,128)(2,1)} %down_ref.1), custom_call_target="tpu_custom_call" | custom-call | flops 1207959552 | bytes 11534336 | tf_op jit(solution)/shard_map/drafter/pallas_call | solution.py:136
  144.5 11.4 %collective-permute-done.35 = bf16[64,4096]{1,0:T(8,128)(2,1)S(1)} collective-permute-done((bf16[64,4096]{1,0:T(8,128)(2,1)S(1)}, bf16[64,4096]{1,0:T(8,128)(2,1)S(1)}, u32[]{:S(2)}, u32[]{:S(2)}) %collective-permute-start.35) | collective-permute-done | bytes 524320 | tf_op jit(solution)/shard_map/ppermute | solution.py:248
  158.6 8.6 %collective-permute-done.22 = bf16[64,4096]{1,0:T(8,128)(2,1)S(1)} collective-permute-done((bf16[64,4096]{1,0:T(8,128)(2,1)S(1)}, bf16[64,4096]{1,0:T(8,128)(2,1)S(1)}, u32[]{:S(2)}, u32[]{:S(2)}) %collective-permute-start.22) | collective-permute-done | bytes 524320 | tf_op jit(solution)/shard_map/ppermute | solution.py:248
  167.2 4.5 %collective-permute-done.48 = bf16[32,4096]{1,0:T(8,128)(2,1)S(1)} collective-permute-done((bf16[32,4096]{1,0:T(8,128)(2,1)S(1)}, bf16[32,4096]{1,0:T(8,128)(2,1)S(1)}, u32[]{:S(2)}, u32[]{:S(2)}) %collective-permute-start.48) | collective-permute-done | bytes 262176 | tf_op jit(solution)/shard_map/ppermute | solution.py:248
  177.4 5.1 %collective-permute-done.50.refs_2_ = bf16[8,4096]{1,0:T(8,128)(2,1)S(1)} collective-permute-done((bf16[8,4096]{1,0:T(8,128)(2,1)S(1)}, bf16[8,4096]{1,0:T(8,128)(2,1)S(1)}, u32[]{:S(2)}, u32[]{:S(2)}) %collective-permute-start.50) | collective-permute-done | bytes 65568 | tf_op jit(solution)/shard_map/ppermute | solution.py:245
  185.4 2.1 %collective-permute-done.23.refs_3_ = bf16[16,4096]{1,0:T(8,128)(2,1)S(1)} collective-permute-done((bf16[16,4096]{1,0:T(8,128)(2,1)S(1)}, bf16[16,4096]{1,0:T(8,128)(2,1)S(1)}, u32[]{:S(2)}, u32[]{:S(2)}) %collective-permute-start.23) | collective-permute-done | bytes 131104 | tf_op jit(solution)/shard_map/ppermute | solution.py:245
  187.5 6.7 %collective-permute-done.24.refs_4_ = bf16[16,4096]{1,0:T(8,128)(2,1)S(1)} collective-permute-done((bf16[16,4096]{1,0:T(8,128)(2,1)S(1)}, bf16[16,4096]{1,0:T(8,128)(2,1)S(1)}, u32[]{:S(2)}, u32[]{:S(2)}) %collective-permute-start.24) | collective-permute-done | bytes 131104 | tf_op jit(solution)/shard_map/ppermute | solution.py:245
  (182 shorter events, 78.0 us)
Async XLA Ops:
  13.7 12.1 %collective-permute-start.2 = (bf16[8,4224]{1,0:T(8,128)(2,1)}, bf16[8,4224]{1,0:T(8,128)(2,1)}, u32[]{:S(2)}, u32[]{:S(2)}) collective-permute-start(bf16[8,4224]{1,0:T(8,128)(2,1)} %get-tuple-element.11), channel_id=1, source_target_pairs={{0,12},{4,0},{8,4},{12,8},{1,13},{5,1},{9,5},{13,9},{2,14},{6,2},{... | collective-permute-start | bytes 202760 | tf_op jit(solution)/shard_map/ppermute | solution.py:245
  15.0 12.8 %collective-permute-start.3 = (bf16[8,4224]{1,0:T(8,128)(2,1)}, bf16[8,4224]{1,0:T(8,128)(2,1)}, u32[]{:S(2)}, u32[]{:S(2)}) collective-permute-start(bf16[8,4224]{1,0:T(8,128)(2,1)} %get-tuple-element.11), channel_id=1, source_target_pairs={{0,2},{1,3},{2,0},{3,1},{4,6},{5,7},{6,4},{7,5},{8,10},{9,11},{10,... | collective-permute-start | bytes 202760 | tf_op jit(solution)/shard_map/ppermute | solution.py:248
  16.5 14.0 %collective-permute-start.26 = (bf16[16,4224]{1,0:T(8,128)(2,1)S(1)}, bf16[16,4224]{1,0:T(8,128)(2,1)}, u32[]{:S(2)}, u32[]{:S(2)}) collective-permute-start(bf16[16,4224]{1,0:T(8,128)(2,1)S(1)} %get-tuple-element.16), channel_id=1, source_target_pairs={{0,4},{4,8},{8,12},{12,0},{1,5},{5,9},{9,13},{13,1},{2,6},{6,10},{... | collective-permute-start | bytes 405512 | tf_op jit(solution)/shard_map/ppermute | solution.py:245
  19.5 13.6 %collective-permute-start.27 = (bf16[16,4224]{1,0:T(8,128)(2,1)S(1)}, bf16[16,4224]{1,0:T(8,128)(2,1)S(1)}, u32[]{:S(2)}, u32[]{:S(2)}) collective-permute-start(bf16[16,4224]{1,0:T(8,128)(2,1)S(1)} %get-tuple-element.16), channel_id=1, source_target_pairs={{0,8},{4,12},{8,0},{12,4},{1,9},{5,13},{9,1},{13,5},{2,10},{6,14},... | collective-permute-start | bytes 405512 | tf_op jit(solution)/shard_map/ppermute | solution.py:245
  21.4 15.3 %collective-permute-start.28 = (bf16[16,4224]{1,0:T(8,128)(2,1)S(1)}, bf16[16,4224]{1,0:T(8,128)(2,1)S(1)}, u32[]{:S(2)}, u32[]{:S(2)}) collective-permute-start(bf16[16,4224]{1,0:T(8,128)(2,1)S(1)} %get-tuple-element.16), channel_id=1, source_target_pairs={{0,12},{4,0},{8,4},{12,8},{1,13},{5,1},{9,5},{13,9},{2,14},{6,2},{... | collective-permute-start | bytes 405512 | tf_op jit(solution)/shard_map/ppermute | solution.py:245
  25.8 26.2 %collective-permute-start.29 = (bf16[16,4224]{1,0:T(8,128)(2,1)S(1)}, bf16[16,4224]{1,0:T(8,128)(2,1)S(1)}, u32[]{:S(2)}, u32[]{:S(2)}) collective-permute-start(bf16[16,4224]{1,0:T(8,128)(2,1)S(1)} %get-tuple-element.16), channel_id=1, source_target_pairs={{0,2},{1,3},{2,0},{3,1},{4,6},{5,7},{6,4},{7,5},{8,10},{9,11},{10,... | collective-permute-start | bytes 405512 | tf_op jit(solution)/shard_map/ppermute | solution.py:248
  27.8 24.9 %collective-permute-start.13 = (bf16[16,4224]{1,0:T(8,128)(2,1)S(1)}, bf16[16,4224]{1,0:T(8,128)(2,1)S(1)}, u32[]{:S(2)}, u32[]{:S(2)}) collective-permute-start(bf16[16,4224]{1,0:T(8,128)(2,1)S(1)} %get-tuple-element.14), channel_id=1, source_target_pairs={{0,4},{4,8},{8,12},{12,0},{1,5},{5,9},{9,13},{13,1},{2,6},{6,10},{... | collective-permute-start | bytes 405512 | tf_op jit(solution)/shard_map/ppermute | solution.py:245
  30.5 22.8 %collective-permute-start.14 = (bf16[16,4224]{1,0:T(8,128)(2,1)S(1)}, bf16[16,4224]{1,0:T(8,128)(2,1)S(1)}, u32[]{:S(2)}, u32[]{:S(2)}) collective-permute-start(bf16[16,4224]{1,0:T(8,128)(2,1)S(1)} %get-tuple-element.14), channel_id=1, source_target_pairs={{0,8},{4,12},{8,0},{12,4},{1,9},{5,13},{9,1},{13,5},{2,10},{6,14},... | collective-permute-start | bytes 405512 | tf_op jit(solution)/shard_map/ppermute | solution.py:245
  33.1 21.8 %collective-permute-start.15 = (bf16[16,4224]{1,0:T(8,128)(2,1)S(1)}, bf16[16,4224]{1,0:T(8,128)(2,1)S(1)}, u32[]{:S(2)}, u32[]{:S(2)}) collective-permute-start(bf16[16,4224]{1,0:T(8,128)(2,1)S(1)} %get-tuple-element.14), channel_id=1, source_target_pairs={{0,12},{4,0},{8,4},{12,8},{1,13},{5,1},{9,5},{13,9},{2,14},{6,2},{... | collective-permute-start | bytes 405512 | tf_op jit(solution)/shard_map/ppermute | solution.py:245
  51.9 19.0 %collective-permute-start.7 = (bf16[64,4224]{1,0:T(8,128)(2,1)S(1)}, bf16[64,4224]{1,0:T(8,128)(2,1)S(1)}, u32[]{:S(2)}, u32[]{:S(2)}) collective-permute-start(bf16[64,4224]{1,0:T(8,128)(2,1)S(1)} %get-tuple-element.68), channel_id=1, source_target_pairs={{0,1},{1,0},{2,3},{3,2},{4,5},{5,4},{6,7},{7,6},{8,9},{9,8},{10,11... | collective-permute-start | bytes 1622024 | tf_op jit(solution)/shard_map/ppermute | solution.py:248
  55.5 12.5 %collective-permute-start.17 = (bf16[16,4224]{1,0:T(8,128)(2,1)S(1)}, bf16[16,4224]{1,0:T(8,128)(2,1)S(1)}, u32[]{:S(2)}, u32[]{:S(2)}) collective-permute-start(bf16[16,4224]{1,0:T(8,128)(2,1)S(1)} %collective-permute-done.13), channel_id=1, source_target_pairs={{0,2},{1,3},{2,0},{3,1},{4,6},{5,7},{6,4},{7,5},{8,10},{9,11},{10,... | collective-permute-start | bytes 405512 | tf_op jit(solution)/shard_map/ppermute | solution.py:248
  62.3 17.6 %collective-permute-start.19 = (bf16[16,4224]{1,0:T(8,128)(2,1)S(1)}, bf16[16,4224]{1,0:T(8,128)(2,1)S(1)}, u32[]{:S(2)}, u32[]{:S(2)}) collective-permute-start(bf16[16,4224]{1,0:T(8,128)(2,1)S(1)} %collective-permute-done.15), channel_id=1, source_target_pairs={{0,2},{1,3},{2,0},{3,1},{4,6},{5,7},{6,4},{7,5},{8,10},{9,11},{10,... | collective-permute-start | bytes 405512 | tf_op jit(solution)/shard_map/ppermute | solution.py:248
  65.8 17.0 %collective-permute-start.33 = (bf16[128,4224]{1,0:T(8,128)(2,1)S(1)}, bf16[128,4224]{1,0:T(8,128)(2,1)S(1)}, u32[]{:S(2)}, u32[]{:S(2)}) collective-permute-start(bf16[128,4224]{1,0:T(8,128)(2,1)S(1)} %get-tuple-element.36), channel_id=1, source_target_pairs={{0,1},{1,0},{2,3},{3,2},{4,5},{5,4},{6,7},{7,6},{8,9},{9,8},{10,11... | collective-permute-start | bytes 3244040 | tf_op jit(solution)/shard_map/ppermute | solution.py:248
  80.0 41.4 %collective-permute-start.20 = (bf16[128,4224]{1,0:T(8,128)(2,1)S(1)}, bf16[128,4224]{1,0:T(8,128)(2,1)S(1)}, u32[]{:S(2)}, u32[]{:S(2)}) collective-permute-start(bf16[128,4224]{1,0:T(8,128)(2,1)S(1)} %get-tuple-element.52), channel_id=1, source_target_pairs={{0,1},{1,0},{2,3},{3,2},{4,5},{5,4},{6,7},{7,6},{8,9},{9,8},{10,11... | collective-permute-start | bytes 3244040 | tf_op jit(solution)/shard_map/ppermute | solution.py:248
  90.5 14.1 %collective-permute-start.10 = (bf16[8,4096]{1,0:T(8,128)(2,1)S(1)}, bf16[8,4096]{1,0:T(8,128)(2,1)S(1)}, u32[]{:S(2)}, u32[]{:S(2)}) collective-permute-start(bf16[8,4096]{1,0:T(8,128)(2,1)S(1)} %get-tuple-element.34), channel_id=1, source_target_pairs={{0,12},{4,0},{8,4},{12,8},{1,13},{5,1},{9,5},{13,9},{2,14},{6,2},{... | collective-permute-start | bytes 196616 | tf_op jit(solution)/shard_map/ppermute | solution.py:245
  90.5 14.0 %collective-permute-start.11 = (bf16[8,4096]{1,0:T(8,128)(2,1)S(1)}, bf16[8,4096]{1,0:T(8,128)(2,1)S(1)}, u32[]{:S(2)}, u32[]{:S(2)}) collective-permute-start(bf16[8,4096]{1,0:T(8,128)(2,1)S(1)} %get-tuple-element.33), channel_id=1, source_target_pairs={{0,8},{4,12},{8,0},{12,4},{1,9},{5,13},{9,1},{13,5},{2,10},{6,14},... | collective-permute-start | bytes 196616 | tf_op jit(solution)/shard_map/ppermute | solution.py:245
  104.5 36.2 %collective-permute-start.34 = (bf16[128,4096]{1,0:T(8,128)(2,1)S(1)}, bf16[128,4096]{1,0:T(8,128)(2,1)S(1)}, u32[]{:S(2)}, u32[]{:S(2)}) collective-permute-start(bf16[128,4096]{1,0:T(8,128)(2,1)S(1)} %slice.145), channel_id=1, source_target_pairs={{0,1},{1,0},{2,3},{3,2},{4,5},{5,4},{6,7},{7,6},{8,9},{9,8},{10,11... | collective-permute-start | bytes 3145736 | tf_op jit(solution)/shard_map/ppermute | solution.py:248
  141.0 14.9 %collective-permute-start.35 = (bf16[64,4096]{1,0:T(8,128)(2,1)S(1)}, bf16[64,4096]{1,0:T(8,128)(2,1)S(1)}, u32[]{:S(2)}, u32[]{:S(2)}) collective-permute-start(bf16[64,4096]{1,0:T(8,128)(2,1)S(1)} %slice.147), channel_id=1, source_target_pairs={{0,2},{1,3},{2,0},{3,1},{4,6},{5,7},{6,4},{7,5},{8,10},{9,11},{10,... | collective-permute-start | bytes 1572872 | tf_op jit(solution)/shard_map/ppermute | solution.py:248
  142.2 24.9 %collective-permute-start.22 = (bf16[64,4096]{1,0:T(8,128)(2,1)S(1)}, bf16[64,4096]{1,0:T(8,128)(2,1)S(1)}, u32[]{:S(2)}, u32[]{:S(2)}) collective-permute-start(bf16[64,4096]{1,0:T(8,128)(2,1)S(1)} %slice.139), channel_id=1, source_target_pairs={{0,2},{1,3},{2,0},{3,1},{4,6},{5,7},{6,4},{7,5},{8,10},{9,11},{10,... | collective-permute-start | bytes 1572872 | tf_op jit(solution)/shard_map/ppermute | solution.py:248
  143.6 28.2 %collective-permute-start.48 = (bf16[32,4096]{1,0:T(8,128)(2,1)S(1)}, bf16[32,4096]{1,0:T(8,128)(2,1)S(1)}, u32[]{:S(2)}, u32[]{:S(2)}) collective-permute-start(bf16[32,4096]{1,0:T(8,128)(2,1)S(1)} %slice.155), channel_id=1, source_target_pairs={{0,2},{1,3},{2,0},{3,1},{4,6},{5,7},{6,4},{7,5},{8,10},{9,11},{10,... | collective-permute-start | bytes 786440 | tf_op jit(solution)/shard_map/ppermute | solution.py:248
  156.7 25.8 %collective-permute-start.36 = (bf16[16,4096]{1,0:T(8,128)(2,1)S(1)}, bf16[16,4096]{1,0:T(8,128)(2,1)S(1)}, u32[]{:S(2)}, u32[]{:S(2)}) collective-permute-start(bf16[16,4096]{1,0:T(8,128)(2,1)S(1)} %get-tuple-element.22), channel_id=1, source_target_pairs={{0,12},{4,0},{8,4},{12,8},{1,13},{5,1},{9,5},{13,9},{2,14},{6,2},{... | collective-permute-start | bytes 393224 | tf_op jit(solution)/shard_map/ppermute | solution.py:245
  158.6 26.9 %collective-permute-start.37 = (bf16[16,4096]{1,0:T(8,128)(2,1)}, bf16[16,4096]{1,0:T(8,128)(2,1)S(1)}, u32[]{:S(2)}, u32[]{:S(2)}) collective-permute-start(bf16[16,4096]{1,0:T(8,128)(2,1)} %get-tuple-element.21), channel_id=1, source_target_pairs={{0,8},{4,12},{8,0},{12,4},{1,9},{5,13},{9,1},{13,5},{2,10},{6,14},... | collective-permute-start | bytes 393224 | tf_op jit(solution)/shard_map/ppermute | solution.py:245
  182.5 11.8 %collective-permute-start.24 = (bf16[16,4096]{1,0:T(8,128)(2,1)S(1)}, bf16[16,4096]{1,0:T(8,128)(2,1)S(1)}, u32[]{:S(2)}, u32[]{:S(2)}) collective-permute-start(bf16[16,4096]{1,0:T(8,128)(2,1)S(1)} %get-tuple-element.25), channel_id=1, source_target_pairs={{0,8},{4,12},{8,0},{12,4},{1,9},{5,13},{9,1},{13,5},{2,10},{6,14},... | collective-permute-start | bytes 393224 | tf_op jit(solution)/shard_map/ppermute | solution.py:245
  182.5 11.7 %collective-permute-start.25 = (bf16[16,4096]{1,0:T(8,128)(2,1)S(1)}, bf16[16,4096]{1,0:T(8,128)(2,1)S(1)}, u32[]{:S(2)}, u32[]{:S(2)}) collective-permute-start(bf16[16,4096]{1,0:T(8,128)(2,1)S(1)} %get-tuple-element.24), channel_id=1, source_target_pairs={{0,4},{4,8},{8,12},{12,0},{1,5},{5,9},{9,13},{13,1},{2,6},{6,10},{... | collective-permute-start | bytes 393224 | tf_op jit(solution)/shard_map/ppermute | solution.py:245
  (44 other events, 319.8 us)

commit v2 on v0

v2 whole, which is shorter than its diff:
```python
import functools

import jax
import jax.numpy as jnp
from jax import lax
from jax.experimental import pallas as pl
from jax.experimental.pallas import tpu as pltpu
from jax.sharding import PartitionSpec as P

EPSILON = 1e-06
BF = jnp.bfloat16
F32 = jnp.float32
LANES = 128
MIB = 1024 * 1024
SMALL = pltpu.CompilerParams(vmem_limit_bytes=16 * MIB)
BLOCK_ROWS = 256
CUT = 2
ANYWHERE = pl.BlockSpec(memory_space=pl.ANY)
HBM = pl.BlockSpec(memory_space=pltpu.HBM)
SCALARS = pl.BlockSpec(memory_space=pltpu.SMEM)
VECTORS = pl.BlockSpec(memory_space=pltpu.VMEM)


def fdot(a, b):
    return jnp.dot(a, b, preferred_element_type=F32)


def fdot_t(a, b):
    return lax.dot_general(a, b, (((1,), (1,)), ((), ())), preferred_element_type=F32)


def iota(shape, axis):
    return lax.broadcasted_iota(jnp.int32, shape, axis)


def rms(values):
    return values * lax.rsqrt(jnp.mean(values * values, axis=-1, keepdims=True) + EPSILON)


def struct(rows, columns):
    return jax.ShapeDtypeStruct((rows, columns), BF)


def accepted_vector(accepted_ref, request, rounds):
    place = iota((rounds, 1), 0)
    found = jnp.zeros((rounds, 1), jnp.int32)
    for number in range(rounds):
        found = jnp.where(place == number, accepted_ref[request, number], found)
    return found


def reorder(layers, accepted_ref, hidden_ref, ids_ref, gain_ref, router_ref, ext_ref, hid_ref):
    rows, rounds, width = hidden_ref.shape
    requests = accepted_ref.shape[0]
    draft = rows // requests
    top, experts = ids_ref.shape[1], router_ref.shape[0]
    chunk = rounds * requests
    taken = [accepted_vector(accepted_ref, request, rounds) for request in range(requests)]
    pieces = []
    for layer in layers:
        for request in range(requests):
            first = request * draft
            if layer == 0:
                found = hidden_ref[first].astype(F32)
                for inside in range(1, draft):
                    found = jnp.where(
                        taken[request] == inside, hidden_ref[first + inside].astype(F32), found
                    )
            else:
                found = jnp.where(
                    taken[request] >= layer,
                    hidden_ref[first + layer - 1].astype(F32),
                    hidden_ref[first + layer].astype(F32),
                )
            pieces.append(found)
    raw = jnp.concatenate(pieces, axis=0)
    hid_ref[...] = raw.astype(BF)
    normed = (rms(raw) * gain_ref[...]).astype(BF)
    ext_ref[:, :width] = normed
    count = len(layers) * chunk
    logits = fdot_t(normed, router_ref[...])
    place = iota((count, rows), 0)
    source = iota((count, rows), 1)
    wanted = jnp.full((count, rows), -1, jnp.int32)
    for number, layer in enumerate(layers):
        for request in range(requests):
            for turn in range(rounds):
                value = accepted_ref[request, turn]
                if layer > 0:
                    value = jnp.where(value >= layer, layer - 1, layer)
                row = number * chunk + request * rounds + turn
                wanted = jnp.where(place == row, value + request * draft, wanted)
    chosen = wanted == source
    named = None
    for turn in range(rounds):
        ids = ids_ref[turn]
        expert = iota((experts, rows), 0)
        hot = ids[0:1] == expert
        for k in range(1, top):
            hot = hot | (ids[k : k + 1] == expert)
        pick = (chosen & (lax.rem(place, rounds) == turn)).astype(F32).astype(BF)
        term = fdot_t(pick, hot.astype(F32).astype(BF))
        named = term if named is None else named + term
    powers = jnp.where(named > 0.5, jnp.exp(logits), 0.0)
    share = powers / jnp.sum(powers, axis=1, keepdims=True)
    high = share.astype(BF).astype(F32)
    tail = [high, share - high]
    if 2 * experts < LANES:
        tail.append(jnp.zeros((count, LANES - 2 * experts), F32))
    ext_ref[:, width:] = jnp.concatenate(tail, axis=1).astype(BF)


def prep_kernel(groups, columns, experts, *refs):
    sources, outs, targets, sems = refs[:5], refs[5:-6], refs[-6:-1], refs[-1]
    moves = [
        pltpu.make_async_copy(source, target, sems.at[number])
        for number, (source, target) in enumerate(zip(sources, targets))
    ]
    for move in moves:
        move.start()
    me = lax.axis_index("expert") * columns + lax.axis_index("tensor")
    lane = iota((1, LANES), 1)
    outs[-1][...] = ((lane == me) | (lane == me + experts)).astype(F32)
    for move in moves:
        move.wait()
    for number, layers in enumerate(groups):
        reorder(layers, *targets, outs[2 * number], outs[2 * number + 1])


def prep(inputs, groups, columns):
    accepted, hidden = inputs[:2]
    rows, rounds, width = hidden.shape
    shapes = []
    for layers in groups:
        count = len(layers) * rounds * accepted.shape[0]
        shapes += [struct(count, width + LANES), struct(count, width)]
    shapes.append(jax.ShapeDtypeStruct((1, LANES), F32))
    return pl.pallas_call(
        functools.partial(prep_kernel, groups, columns, inputs[-1].shape[0]),
        out_shape=shapes,
        in_specs=[HBM] * 5,
        out_specs=[VECTORS] * len(shapes),
        scratch_shapes=[pltpu.SMEM(accepted.shape, jnp.int32)]
        + [pltpu.VMEM(array.shape, array.dtype) for array in inputs[1:]]
        + [pltpu.SemaphoreType.DMA((5,))],
        compiler_params=pltpu.CompilerParams(vmem_limit_bytes=56 * MIB),
        name="prep",
    )(*inputs)


def hold(arrays, after):
    held = pl.pallas_call(
        lambda *refs: None,
        out_shape=[struct(*array.shape) for array in arrays],
        in_specs=[ANYWHERE] * (len(arrays) + len(after)),
        out_specs=[ANYWHERE] * len(arrays),
        input_output_aliases={number: number for number in range(len(arrays))},
        compiler_params=SMALL,
        name="hold",
    )(*arrays, *after)
    return list(held)


def pack_kernel(count, cut, *refs):
    whole = jnp.concatenate([ref[...] for ref in refs[:count]], axis=0)
    rows = whole.shape[0] // cut
    for number, out_ref in enumerate(refs[-cut:]):
        out_ref[...] = whole[number * rows : (number + 1) * rows]


def pack(blocks, after, cut=1):
    rows, width = sum(block.shape[0] for block in blocks), blocks[0].shape[1]
    outs = pl.pallas_call(
        functools.partial(pack_kernel, len(blocks), cut),
        out_shape=[struct(rows // cut, width)] * cut,
        in_specs=[VECTORS] * len(blocks) + [ANYWHERE] * len(after),
        out_specs=[VECTORS] * cut,
        compiler_params=SMALL,
        name="pack",
    )(*blocks, *after)
    return outs[0] if cut == 1 else list(outs)


def cut_kernel(count, first, rows, *refs):
    blocks = [ref[...] for ref in refs[:count]]
    refs[-1][...] = jnp.concatenate([block[first : first + rows] for block in blocks], axis=0)


def cut(blocks, first, rows, after, near=()):
    width = blocks[0].shape[1]
    count = len(blocks)
    return pl.pallas_call(
        functools.partial(cut_kernel, count, first, rows),
        out_shape=struct(count * rows, width),
        in_specs=[VECTORS] * count + [ANYWHERE] * len(after) + [VECTORS] * len(near),
        out_specs=VECTORS,
        compiler_params=SMALL,
        name="cut",
    )(*blocks, *after, *near)


def add_kernel(*refs):
    refs[-1][...] = sum(ref[...].astype(F32) for ref in refs[:-1]).astype(BF)


def add(arrays):
    return pl.pallas_call(
        add_kernel,
        out_shape=struct(*arrays[0].shape),
        compiler_params=SMALL,
        name="add",
    )(*arrays)


def fold_kernel(comes, parts, keep_ref, *refs):
    come_refs, out_refs = refs[:comes], refs[-parts:]
    rows = out_refs[0].shape[0]
    come = jnp.concatenate([ref[...] for ref in come_refs], axis=0).astype(F32)
    total = keep_ref[...].astype(F32) + come
    for number, out_ref in enumerate(out_refs):
        out_ref[...] = total[number * rows : (number + 1) * rows].astype(BF)


def fold(keep, comes, parts, after):
    rows, width = keep.shape
    return pl.pallas_call(
        functools.partial(fold_kernel, len(comes), parts),
        out_shape=[struct(rows // parts, width)] * parts,
        in_specs=[VECTORS] * (1 + len(comes)) + [ANYWHERE] * len(after),
        out_specs=[VECTORS] * parts,
        compiler_params=SMALL,
        name="fold",
    )(keep, *comes, *after)


def unit_kernel(gated, parts, group, mark_ref, *refs):
    x_refs, (gate_ref, up_ref, down_ref) = refs[:parts], refs[parts : parts + 3]
    out_refs, (all_ref, active_ref) = refs[-parts - 2 : -2], refs[-2:]
    rows, width = out_refs[0].shape
    hidden = gate_ref.shape[1]
    tile = min(256, hidden)
    columns = min(512, width)
    for first in range(0, parts, group):
        members = list(range(first, min(first + group, parts)))
        count = len(members) * rows
        for place, number in enumerate(members):
            all_ref[place * rows : (place + 1) * rows] = x_refs[number][:, :width]

        for step in range(0, hidden, tile):
            at = slice(step, step + tile)
            gate = fdot(all_ref[:count], gate_ref[:, at])
            up = fdot(all_ref[:count], up_ref[:, at])
            active_ref[:count, at] = (gate / (1.0 + jnp.exp(-gate)) * up).astype(BF)

        share = None
        if gated:
            tail = jnp.concatenate([x_refs[number][:, width:] for number in members], axis=0)
            share = jnp.sum(tail.astype(F32) * mark_ref[...], axis=1, keepdims=True)

        for step in range(0, width, columns):
            at = slice(step, step + columns)
            total = fdot(active_ref[:count], down_ref[:, at])
            if gated:
                total = total * share
            for place, number in enumerate(members):
                out_refs[number][:, at] = total[place * rows : (place + 1) * rows].astype(BF)


def units(pieces, mark, weights, gated, after):
    parts = len(pieces)
    rows = pieces[0].shape[0]
    hidden, width = weights[2].shape
    group = max(1, min(parts, BLOCK_ROWS // rows))
    outs = pl.pallas_call(
        functools.partial(unit_kernel, gated, parts, group),
        out_shape=[struct(rows, width)] * parts,
        in_specs=[VECTORS] * (4 + parts) + [ANYWHERE] * len(after),
        out_specs=[VECTORS] * parts,
        scratch_shapes=[
            pltpu.VMEM((rows * group, width), BF),
            pltpu.VMEM((rows * group, hidden), BF),
        ],
        compiler_params=SMALL,
        name="experts" if gated else "drafter",
    )(mark, *pieces, *weights, *after)
    return list(outs)


def mid_kernel(count, hid_ref, gain_ref, *refs):
    verified_ref, draft_ref = refs[-2:]
    total = hid_ref[...].astype(F32) + sum(ref[...].astype(F32) for ref in refs[:count])
    verified = total.astype(BF)
    verified_ref[...] = verified
    draft_ref[...] = (rms(verified.astype(F32)) * gain_ref[...]).astype(BF)


def mid(hid, parts, gain, after):
    return pl.pallas_call(
        functools.partial(mid_kernel, len(parts)),
        out_shape=[struct(*hid.shape)] * 2,
        in_specs=[VECTORS] * (2 + len(parts)) + [ANYWHERE] * len(after),
        out_specs=[VECTORS] * 2,
        compiler_params=SMALL,
        name="accepted_norm",
    )(hid, gain, *parts, *after)


def last_kernel(hid_ref, gain_ref, *refs):
    out_ref = refs[-1]
    total = hid_ref[...].astype(F32) + sum(ref[...].astype(F32) for ref in refs[:-1])
    result = (rms(total) * gain_ref[...]).astype(BF).astype(F32)
    requests, rounds, _ = out_ref.shape
    for request in range(requests):
        out_ref[request] = result[request * rounds : (request + 1) * rounds].astype(BF)


def last(hid, parts, gain, requests, rounds):
    return pl.pallas_call(
        last_kernel,
        out_shape=jax.ShapeDtypeStruct((requests, rounds, hid.shape[1]), BF),
        compiler_params=SMALL,
        name="draft_norm",
    )(hid, gain, *parts)


def merge_kernel(groups, accepted_ref, *refs):
    out_ref = refs[-1]
    rows, rounds, _ = out_ref.shape
    requests = accepted_ref.shape[0]
    draft = rows // requests
    chunk = rounds * requests
    layers = []
    first = 0
    for group in groups:
        members = refs[first : first + group]
        first += group
        total = sum(ref[...].astype(F32) for ref in members).astype(BF).astype(F32)
        layers += [total[at : at + chunk] for at in range(0, total.shape[0], chunk)]
    for request in range(requests):
        taken = accepted_vector(accepted_ref, request, rounds)
        held = [layer[request * rounds : (request + 1) * rounds] for layer in layers]
        for inside in range(draft):
            found = held[0]
            if inside < draft - 1:
                found = jnp.where(taken > inside, held[inside + 1], found)
            if inside > 0:
                found = jnp.where(taken < inside, held[inside], found)
            out_ref[request * draft + inside] = found.astype(BF)


def merge(accepted, groups, rows, rounds):
    flat = [array for group in groups for array in group]
    return pl.pallas_call(
        functools.partial(merge_kernel, [len(group) for group in groups]),
        out_shape=jax.ShapeDtypeStruct((rows, rounds, flat[0].shape[1]), BF),
        in_specs=[SCALARS] + [VECTORS] * len(flat),
        out_specs=VECTORS,
        compiler_params=SMALL,
        name="merge",
    )(accepted, *flat)


class Links:

    def __init__(self, lines, columns):
        self.lines = lines
        self.columns = columns

    def line(self, x, bits):
        return lax.ppermute(x, "expert", [(i, i ^ bits) for i in range(self.lines)])

    def far(self, x):
        return lax.ppermute(x, "tensor", [(i, i ^ 2) for i in range(self.columns)])

    def near(self, x):
        return lax.ppermute(x, "tensor", [(i, i ^ 1) for i in range(self.columns)])

    def widen(self, x, bit, after):
        return pack([x, self.line(x, bit)], after)

    def sides(self, x, after):
        own = pack([x, self.far(x)], after, CUT)
        return own + [self.near(piece) for piece in own]

    def meet(self, pieces):
        comes = [self.near(piece) for piece in pieces[CUT:]]
        return [fold(keep, [come], 1, [])[0] for keep, come in zip(pieces, comes)]


def bits_of(size):
    return [1 << bit for bit in reversed(range(size.bit_length() - 1))]


def local(
    lines,
    columns,
    subs,
    hidden_rows,
    expert_ids,
    accepted,
    norm_gain,
    router,
    gate_weight,
    up_weight,
    down_weight,
    draft_gain,
    draft_gate,
    draft_up,
    draft_down,
    final_gain,
):
    rounds, rows, width = hidden_rows.shape
    requests = accepted.shape[1]
    draft = rows // requests
    links = Links(lines, columns)
    accepted = accepted.T
    inputs = (
        accepted,
        hidden_rows.transpose(1, 0, 2),
        expert_ids.transpose(0, 2, 1),
        norm_gain.reshape(1, width),
        router.T,
    )

    def over_sub(terms):
        if subs > 1:
            terms = [lax.psum(sum(term.astype(F32) for term in terms), "sub")]
        return terms

    weights = [gate_weight[0], up_weight[0], down_weight[0]]
    draft_weights = [draft_gate, draft_up, draft_down]
    bits = bits_of(lines)
    chunk = rounds * requests
    others = rounds * rows - chunk
    ext, hid, mark = prep(inputs, [list(range(draft))], columns)
    hid, rest_hid = hid[:chunk], hid[chunk:]

    lined, offsets = [ext], [0]
    for bit in bits:
        lined = lined + [links.line(block, bit) for block in lined]
        offsets = offsets + [offset | bit for offset in offsets]
    crossed = [links.far(block) for block in lined]
    head = [cut(lined, 0, chunk, [], weights[:1]), cut(crossed, 0, chunk, [], weights[1:])]
    head += [links.near(piece) for piece in head]
    line_rest = cut(lined, chunk, others, head[2:])
    cross_rest = cut(crossed, chunk, others, head[2:])
    cross_other = links.near(cross_rest)
    line_other = links.near(line_rest)

    halves = links.meet(units(head, mark, weights, True, []))
    cross_keep, cross_send = units([cross_rest, cross_other], mark, weights, True, [halves[1]])
    steps = []
    keep, come = halves[0], links.far(halves[1])
    for place, bit in enumerate(reversed(bits)):
        waits = [cross_keep] if place == 0 else [line_keep] if place == 1 else []
        keep, send = fold(keep, [come], 2, waits)
        come = links.line(send, bit)
        steps.append(send)
        if place == 0:
            line_keep, line_send = units(
                [line_rest, line_other], mark, weights, True, [send]
            )
    cross_come = links.near(hold([cross_send], [steps[0]])[0])
    line_come = links.near(hold([line_send], [steps[1]])[0])
    features, draft_in = mid(
        hid, over_sub([keep, come]), draft_gain.reshape(1, width), []
    )
    cross_parts = fold(cross_keep, [cross_come], lines, [])
    line_parts = fold(line_keep, [line_come], lines, [])

    held = {}
    for place in reversed(range(lines)):
        held[offsets[place]] = [line_parts[place], links.far(cross_parts[place])]
    summed = {}
    for bit in reversed(bits):
        for offset in reversed(offsets):
            if offset & bit and offset < 2 * bit * (lines // bit) and not offset & (bit - 1):
                summed[offset] = add(held[offset])
                held[offset ^ bit].append(links.line(summed[offset], bit))
    rest_terms = held[0]
    a = draft_in
    for place, bit in enumerate(bits):
        a = links.widen(a, bit, (([cross_parts[0]], [summed[lines - 1], held[lines // 2][1]])[place] if place < 2 else []))
    own = pack([a, links.far(a)], [summed[lines // 2], summed[1]], CUT)
    pieces = own + [links.near(piece) for piece in own]
    halves = links.meet(units(pieces, mark, draft_weights, False, []))
    keep, come = halves[0], links.far(halves[1])
    for bit in reversed(bits):
        keep, send = fold(keep, [come], 2, [])
        come = links.line(send, bit)
    terms = [keep, come]
    draft_out = last(features, terms, final_gain.reshape(1, width), requests, rounds)
    verified = merge(
        accepted,
        [[features], [rest_hid] + over_sub(rest_terms)],
        rows,
        rounds,
    )
    return verified.transpose(1, 0, 2), draft_out.transpose(1, 0, 2)


def solution(mesh):
    placed = (
        P(None, ("groups", "expert", "tensor"), None),
        P(None, ("groups", "expert", "tensor"), None),
        P(None, ("groups", "expert", "tensor")),
        P(),
        P(),
        P(("expert", "tensor"), None, "sub"),
        P(("expert", "tensor"), None, "sub"),
        P(("expert", "tensor"), "sub", None),
        P(),
        P(None, ("expert", "tensor")),
        P(None, ("expert", "tensor")),
        P(("expert", "tensor"), None),
        P(),
    )
    body = functools.partial(
        local, mesh.shape["expert"], mesh.shape["tensor"], mesh.shape["sub"]
    )
    return jax.shard_map(
        body,
        mesh=mesh,
        in_specs=placed,
        out_specs=(
            P(None, ("groups", "expert", "tensor"), None),
            P(None, ("groups", "expert", "tensor"), None),
        ),
        check_vma=False,
    )
```

time: 503 us -> 140 us (0.28)
  matrix products: 107 us -> 0 us
  waiting for transfers between devices: 160 us -> 74 us
  blocking collectives: 84.8 us -> 0 us
  local copies, waits for them, and re-layouts: 48.1 us -> 8.87 us
  other arithmetic: 29.9 us -> 0.01 us
  Pallas kernels: 0 us -> 21.2 us
  starting transfers between devices: 55.2 us -> 34.9 us
  between operations: 15.1 us -> 1 us
    dot_general x44 -> x0, matrix products: 107 us -> none  [the longest x4 18.6 us: local(): jnp.dot(flat_rows, up_weight[0], preferred_element_type=jnp.float32)]
    unnamed x2 -> x0, waiting for transfers between devices: 93.5 us -> none
    all_gather x4 -> x0, blocking collectives: 84.8 us -> none  [local(): lax.all_gather(draft_input, ('expert', 'tensor'), axis=0, tiled=True)]
    ppermute x0 -> x35, waiting for transfers between devices: none -> 74 us  [the longest x12 38.3 us: line(): return lax.ppermute(x, 'expert', [(i, i ^ bits) for i in range(self.lines)])]
    all_to_all x8 -> x0, waiting for transfers between devices: 66 us -> none  [the longest x4 37.9 us: local(): lax.all_to_all(outgoing, ('expert', 'tensor'), split_axis=0, concat_axis=...]
    all_to_all x8 -> x0, starting transfers between devices: 54.9 us -> none  [the longest x4 27.7 us: local(): lax.all_to_all(processed, ('expert', 'tensor'), split_axis=0, concat_axis...]
    ppermute x0 -> x35, starting transfers between devices: none -> 34.9 us  [the longest x12 18.4 us: line(): return lax.ppermute(x, 'expert', [(i, i ^ bits) for i in range(self.lines)])]
    pallas_call x0 -> x30, Pallas kernels: none -> 21.2 us  [the longest x4 15.2 us: units(): pl.pallas_call(functools.partial(unit_kernel, gated, parts, group), out_s...]
  transfers between devices with their start and end apart: 9 -> 35, of which waited for: 8 -> 19; matrix products, arithmetic and copies ran while one was open for 27% -> 0% of each run, Pallas kernels for 0% -> 12%
where the time goes in v2:
time: 140 us
  waiting for transfers between devices  74 us (53%)
  starting transfers between devices  34.9 us (25%)
  Pallas kernels  21.2 us (15%)
  local copies, waits for them, and re-layouts  8.87 us (6%)
    ppermute x12, waiting for transfers between devices, line(): return lax.ppermute(x, 'expert', [(i, i ^ bits) for i in range(self.lines)])  38.3 us
    ppermute x11, waiting for transfers between devices, far(): return lax.ppermute(x, 'tensor', [(i, i ^ 2) for i in range(self.columns)])  30.7 us
    ppermute x12, starting transfers between devices, line(): return lax.ppermute(x, 'expert', [(i, i ^ bits) for i in range(self.lines)])  18.4 us
    pallas_call x4, Pallas kernels, units(): pl.pallas_call(functools.partial(unit_kernel, gated, parts, group), out_s...  15.2 us
    ppermute x11, starting transfers between devices, far(): return lax.ppermute(x, 'tensor', [(i, i ^ 2) for i in range(self.columns)])  13.6 us
    unnamed x33, local copies, waits for them, and re-layouts  8.84 us
    ppermute x12, waiting for transfers between devices, near(): return lax.ppermute(x, 'tensor', [(i, i ^ 1) for i in range(self.columns)])  4.99 us
  transfers between devices with their start and end apart: 35, of which 19 were waited for; matrix products, arithmetic and copies ran while one was open for 0% of the time, Pallas kernels for 12%

profile of v2, /device:TPU:0, one launch (start us, length us, event | category | flops | bytes accessed | tf_op | source)
XLA Modules:
  0.0 140.0 jit_solution(323698077377003916)
XLA Ops:
  0.6 2.7 %prep.1 = (bf16[40,4224]{1,0:T(8,128)(2,1)}, bf16[40,4096]{1,0:T(8,128)(2,1)}, f32[1,128]{1,0:T(1,128)}) custom-call(s32[2,4]{1,0:T(2,128)} %bitcast.29, bf16[10,4,4096]{2,1,0:T(4,128)(2,1)} %bitcast.31, s32[4,8,10]{2,1,0:T(8,128)} %bitcast.34, f32[1,4096]{1,0:T(1,128)} %bitcast.35, bf16[16,4096]{1,0:T(8,128)(2,1)} %bitcast.33), custom_call_target="tpu_custom_call" | custom-call | tf_op jit(solution)/shard_map/prep/pallas_call | solution.py:138
  3.3 4.1 %collective-permute-start = (bf16[40,4224]{1,0:T(8,128)(2,1)}, bf16[40,4224]{1,0:T(8,128)(2,1)S(1)}, u32[]{:S(2)}, u32[]{:S(2)}) collective-permute-start(bf16[40,4224]{1,0:T(8,128)(2,1)} %get-tuple-element.39.refs_0_), channel_id=1, source_target_pairs={{0,8},{4,12},{8,0},{12,4},{1,9},{5,13},{9,1},{13,5},{2,10},{6,14},... | collective-permute-start | bytes 1013768 | tf_op jit(solution)/shard_map/ppermute | solution.py:370
  9.0 13.9 %collective-permute-done.refs_1_ = bf16[40,4224]{1,0:T(8,128)(2,1)S(1)} collective-permute-done((bf16[40,4224]{1,0:T(8,128)(2,1)}, bf16[40,4224]{1,0:T(8,128)(2,1)S(1)}, u32[]{:S(2)}, u32[]{:S(2)}) %collective-permute-start) | collective-permute-done | bytes 337952 | tf_op jit(solution)/shard_map/ppermute | solution.py:370
  27.1 4.8 %collective-permute-done.2.refs_3_ = bf16[40,4224]{1,0:T(8,128)(2,1)S(1)} collective-permute-done((bf16[40,4224]{1,0:T(8,128)(2,1)S(1)}, bf16[40,4224]{1,0:T(8,128)(2,1)S(1)}, u32[]{:S(2)}, u32[]{:S(2)}) %collective-permute-start.2) | collective-permute-done | bytes 337952 | tf_op jit(solution)/shard_map/ppermute | solution.py:370
  33.2 2.8 %copy-done = bf16[1,4096,768]{2,1,0:T(8,128)(2,1)S(1)} copy-done((bf16[1,4096,768]{2,1,0:T(8,128)(2,1)S(1)}, bf16[1,4096,768]{2,1,0:T(8,128)(2,1)}, u32[]{:S(2)}) %copy-start) | copy-done | bytes 6291480
  37.1 12.0 %collective-permute-done.5.refs_2_ = bf16[40,4224]{1,0:T(8,128)(2,1)S(1)} collective-permute-done((bf16[40,4224]{1,0:T(8,128)(2,1)S(1)}, bf16[40,4224]{1,0:T(8,128)(2,1)S(1)}, u32[]{:S(2)}, u32[]{:S(2)}) %collective-permute-start.5) | collective-permute-done | bytes 337952 | tf_op jit(solution)/shard_map/ppermute | solution.py:373
  49.1 6.0 %collective-permute-done.6.refs_3_ = bf16[40,4224]{1,0:T(8,128)(2,1)S(1)} collective-permute-done((bf16[40,4224]{1,0:T(8,128)(2,1)S(1)}, bf16[40,4224]{1,0:T(8,128)(2,1)S(1)}, u32[]{:S(2)}, u32[]{:S(2)}) %collective-permute-start.6) | collective-permute-done | bytes 337952 | tf_op jit(solution)/shard_map/ppermute | solution.py:373
  55.1 2.9 %copy-done.2 = bf16[1,768,4096]{2,1,0:T(8,128)(2,1)S(1)} copy-done((bf16[1,768,4096]{2,1,0:T(8,128)(2,1)S(1)}, bf16[1,768,4096]{2,1,0:T(8,128)(2,1)}, u32[]{:S(2)}) %copy-start.2) | copy-done | bytes 6291480
  61.9 2.7 %experts.3 = (bf16[32,4096]{1,0:T(8,128)(2,1)S(1)}, bf16[32,4096]{1,0:T(8,128)(2,1)S(1)}, bf16[32,4096]{1,0:T(8,128)(2,1)S(1)}, bf16[32,4096]{1,0:T(8,128)(2,1)S(1)}) custom-call(f32[1,128]{1,0:T(1,128)S(1)} %copy-done.11, bf16[32,4224]{1,0:T(8,128)(2,1)S(1)} %cut.4.refs_0_, bf16[32,4224]{1,0:T(8,128)(2,1)S(1)} %cut.5.refs_1_, ...), custom_call_target="tpu_custom_call" | custom-call | tf_op jit(solution)/shard_map/experts/pallas_call | solution.py:274
  68.0 5.2 %experts.4 = (bf16[128,4096]{1,0:T(8,128)(2,1)S(1)}, bf16[128,4096]{1,0:T(8,128)(2,1)S(1)}) custom-call(f32[1,128]{1,0:T(1,128)S(1)} %copy-done.11, bf16[128,4224]{1,0:T(8,128)(2,1)S(1)} %cut.6.refs_0_, bf16[128,4224]{1,0:T(8,128)(2,1)S(1)} %collective-permute-done.12.refs_1_, bf16[4096,768]{1,0:T(8,128)(2,1)S(1)} %bitcast.16, ...), custom_call_target="tpu_custom_call" | custom-call | tf_op jit(solution)/shard_map/experts/pallas_call | solution.py:274
  73.2 1.6 %collective-permute-done.11.refs_0_ = bf16[32,4096]{1,0:T(8,128)(2,1)S(1)} collective-permute-done((bf16[32,4096]{1,0:T(8,128)(2,1)S(1)}, bf16[32,4096]{1,0:T(8,128)(2,1)S(1)}, u32[]{:S(2)}, u32[]{:S(2)}) %collective-permute-start.11) | collective-permute-done | bytes 262176 | tf_op jit(solution)/shard_map/ppermute | solution.py:373
  75.5 5.3 %experts.5 = (bf16[128,4096]{1,0:T(8,128)(2,1)S(1)}, bf16[128,4096]{1,0:T(8,128)(2,1)S(1)}) custom-call(f32[1,128]{1,0:T(1,128)S(1)} %copy-done.11, bf16[128,4224]{1,0:T(8,128)(2,1)S(1)} %cut.7.refs_0_, bf16[128,4224]{1,0:T(8,128)(2,1)S(1)} %collective-permute-done.14.refs_1_, bf16[4096,768]{1,0:T(8,128)(2,1)S(1)} %bitcast.17, ...), custom_call_target="tpu_custom_call" | custom-call | tf_op jit(solution)/shard_map/experts/pallas_call | solution.py:274
  81.1 3.2 %collective-permute-start.15 = (bf16[8,4096]{1,0:T(8,128)(2,1)S(1)}, bf16[8,4096]{1,0:T(8,128)(2,1)S(1)}, u32[]{:S(2)}, u32[]{:S(2)}) collective-permute-start(bf16[8,4096]{1,0:T(8,128)(2,1)S(1)} %get-tuple-element.49.refs_1_), channel_id=1, source_target_pairs={{0,8},{4,12},{8,0},{12,4},{1,9},{5,13},{9,1},{13,5},{2,10},{6,14},... | collective-permute-start | bytes 196616 | tf_op jit(solution)/shard_map/ppermute | solution.py:370
  86.7 1.7 %collective-permute-done.15.refs_1_ = bf16[8,4096]{1,0:T(8,128)(2,1)S(1)} collective-permute-done((bf16[8,4096]{1,0:T(8,128)(2,1)S(1)}, bf16[8,4096]{1,0:T(8,128)(2,1)S(1)}, u32[]{:S(2)}, u32[]{:S(2)}) %collective-permute-start.15) | collective-permute-done | bytes 65568 | tf_op jit(solution)/shard_map/ppermute | solution.py:370
  90.0 5.2 %collective-permute-done.25.refs_1_ = bf16[8,4096]{1,0:T(8,128)(2,1)S(1)} collective-permute-done((bf16[8,4096]{1,0:T(8,128)(2,1)S(1)}, bf16[8,4096]{1,0:T(8,128)(2,1)S(1)}, u32[]{:S(2)}, u32[]{:S(2)}) %collective-permute-start.25) | collective-permute-done | bytes 65568 | tf_op jit(solution)/shard_map/ppermute | solution.py:370
  97.2 2.0 %collective-permute-start.23 = (bf16[32,4096]{1,0:T(8,128)(2,1)S(1)}, bf16[32,4096]{1,0:T(8,128)(2,1)S(1)}, u32[]{:S(2)}, u32[]{:S(2)}) collective-permute-start(bf16[32,4096]{1,0:T(8,128)(2,1)S(1)} %add.4.refs_2_), channel_id=1, source_target_pairs={{0,4},{4,0},{8,12},{12,8},{1,5},{5,1},{9,13},{13,9},{2,6},{6,2},{1... | collective-permute-start | bytes 786440 | tf_op jit(solution)/shard_map/ppermute | solution.py:370
  99.2 2.4 %collective-permute-done.26.refs_1_ = bf16[16,4096]{1,0:T(8,128)(2,1)S(1)} collective-permute-done((bf16[16,4096]{1,0:T(8,128)(2,1)S(1)}, bf16[16,4096]{1,0:T(8,128)(2,1)S(1)}, u32[]{:S(2)}, u32[]{:S(2)}) %collective-permute-start.26) | collective-permute-done | bytes 131104 | tf_op jit(solution)/shard_map/ppermute | solution.py:370
  103.3 1.7 %collective-permute-done.19.refs_1_ = bf16[32,4096]{1,0:T(8,128)(2,1)S(1)} collective-permute-done((bf16[32,4096]{1,0:T(8,128)(2,1)S(1)}, bf16[32,4096]{1,0:T(8,128)(2,1)S(1)}, u32[]{:S(2)}, u32[]{:S(2)}) %collective-permute-start.19) | collective-permute-done | bytes 262176 | tf_op jit(solution)/shard_map/ppermute | solution.py:373
  105.8 4.1 %collective-permute-done.27.refs_1_ = bf16[32,4096]{1,0:T(8,128)(2,1)S(1)} collective-permute-done((bf16[32,4096]{1,0:T(8,128)(2,1)S(1)}, bf16[32,4096]{1,0:T(8,128)(2,1)S(1)}, u32[]{:S(2)}, u32[]{:S(2)}) %collective-permute-start.27) | collective-permute-done | bytes 262176 | tf_op jit(solution)/shard_map/ppermute | solution.py:373
  111.9 1.9 %drafter.1 = (bf16[32,4096]{1,0:T(8,128)(2,1)S(1)}, bf16[32,4096]{1,0:T(8,128)(2,1)S(1)}, bf16[32,4096]{1,0:T(8,128)(2,1)S(1)}, bf16[32,4096]{1,0:T(8,128)(2,1)S(1)}) custom-call(f32[1,128]{1,0:T(1,128)S(1)} %copy-done.11, bf16[32,4096]{1,0:T(8,128)(2,1)S(1)} %get-tuple-element.62.refs_0_, bf16[32,4096]{1,0:T(8,128)(2,1)S(1)} %get-tuple-element.63.refs_1_, ...), custom_call_target="tpu_custom_call" | custom-call | tf_op jit(solution)/shard_map/drafter/pallas_call | solution.py:274
  119.5 5.2 %collective-permute-done.32.refs_0_ = bf16[32,4096]{1,0:T(8,128)(2,1)S(1)} collective-permute-done((bf16[32,4096]{1,0:T(8,128)(2,1)S(1)}, bf16[32,4096]{1,0:T(8,128)(2,1)S(1)}, u32[]{:S(2)}, u32[]{:S(2)}) %collective-permute-start.32) | collective-permute-done | bytes 262176 | tf_op jit(solution)/shard_map/ppermute | solution.py:373
  126.4 7.5 %collective-permute-done.33.refs_0_ = bf16[16,4096]{1,0:T(8,128)(2,1)S(1)} collective-permute-done((bf16[16,4096]{1,0:T(8,128)(2,1)S(1)}, bf16[16,4096]{1,0:T(8,128)(2,1)S(1)}, u32[]{:S(2)}, u32[]{:S(2)}) %collective-permute-start.33) | collective-permute-done | bytes 131104 | tf_op jit(solution)/shard_map/ppermute | solution.py:370
  135.4 1.6 %merge.1 = bf16[10,4,4096]{2,1,0:T(4,128)(2,1)} custom-call(s32[2,4]{1,0:T(2,128)S(1)} %bitcast.30, bf16[8,4096]{1,0:T(8,128)(2,1)S(1)} %get-tuple-element.50.refs_0_.hid_ref, bf16[32,4096]{1,0:T(8,128)(2,1)S(1)} %slice.7.refs_1_, bf16[32,4096]{1,0:T(8,128)(2,1)S(1)} %get-tuple-element.52.refs_2_, bf16[32,4096]{1,0:T(8,128)(2,1)S(1)} %collective-permute-done.18.refs_3_, ...), custom_call_target="tpu_custom_call" | custom-call | tf_op jit(solution)/shard_map/merge/pallas_call | solution.py:353
  137.0 2.1 %collective-permute-done.34.refs_1_ = bf16[8,4096]{1,0:T(8,128)(2,1)S(1)} collective-permute-done((bf16[8,4096]{1,0:T(8,128)(2,1)S(1)}, bf16[8,4096]{1,0:T(8,128)(2,1)S(1)}, u32[]{:S(2)}, u32[]{:S(2)}) %collective-permute-start.34) | collective-permute-done | bytes 65568 | tf_op jit(solution)/shard_map/ppermute | solution.py:370
  (112 shorter events, 36.2 us)
Async XLA Ops:
  3.3 19.6 %collective-permute-start = (bf16[40,4224]{1,0:T(8,128)(2,1)}, bf16[40,4224]{1,0:T(8,128)(2,1)S(1)}, u32[]{:S(2)}, u32[]{:S(2)}) collective-permute-start(bf16[40,4224]{1,0:T(8,128)(2,1)} %get-tuple-element.39.refs_0_), channel_id=1, source_target_pairs={{0,8},{4,12},{8,0},{12,4},{1,9},{5,13},{9,1},{13,5},{2,10},{6,14},... | collective-permute-start | bytes 1013768 | tf_op jit(solution)/shard_map/ppermute | solution.py:370
  7.4 18.2 %collective-permute-start.1 = (bf16[40,4224]{1,0:T(8,128)(2,1)}, bf16[40,4224]{1,0:T(8,128)(2,1)S(1)}, u32[]{:S(2)}, u32[]{:S(2)}) collective-permute-start(bf16[40,4224]{1,0:T(8,128)(2,1)} %get-tuple-element.39.refs_0_), channel_id=1, source_target_pairs={{0,4},{4,0},{8,12},{12,8},{1,5},{5,1},{9,13},{13,9},{2,6},{6,2},{1... | collective-permute-start | bytes 1013768 | tf_op jit(solution)/shard_map/ppermute | solution.py:370
  22.9 9.1 %collective-permute-start.2 = (bf16[40,4224]{1,0:T(8,128)(2,1)S(1)}, bf16[40,4224]{1,0:T(8,128)(2,1)S(1)}, u32[]{:S(2)}, u32[]{:S(2)}) collective-permute-start(bf16[40,4224]{1,0:T(8,128)(2,1)S(1)} %collective-permute-done.refs_1_), channel_id=1, source_target_pairs={{0,4},{4,0},{8,12},{12,8},{1,5},{5,1},{9,13},{13,9},{2,6},{6,2},{1... | collective-permute-start | bytes 1013768 | tf_op jit(solution)/shard_map/ppermute | solution.py:370
  23.6 13.5 %collective-permute-start.3 = (bf16[40,4224]{1,0:T(8,128)(2,1)}, bf16[40,4224]{1,0:T(8,128)(2,1)S(1)}, u32[]{:S(2)}, u32[]{:S(2)}) collective-permute-start(bf16[40,4224]{1,0:T(8,128)(2,1)} %get-tuple-element.39.refs_0_), channel_id=1, source_target_pairs={{0,2},{1,3},{2,0},{3,1},{4,6},{5,7},{6,4},{7,5},{8,10},{9,11},{10,... | collective-permute-start | bytes 1013768 | tf_op jit(solution)/shard_map/ppermute | solution.py:373
  25.1 24.0 %collective-permute-start.4 = (bf16[40,4224]{1,0:T(8,128)(2,1)S(1)}, bf16[40,4224]{1,0:T(8,128)(2,1)S(1)}, u32[]{:S(2)}, u32[]{:S(2)}) collective-permute-start(bf16[40,4224]{1,0:T(8,128)(2,1)S(1)} %collective-permute-done.refs_1_), channel_id=1, source_target_pairs={{0,2},{1,3},{2,0},{3,1},{4,6},{5,7},{6,4},{7,5},{8,10},{9,11},{10,... | collective-permute-start | bytes 1013768 | tf_op jit(solution)/shard_map/ppermute | solution.py:373
  25.6 23.5 %collective-permute-start.5 = (bf16[40,4224]{1,0:T(8,128)(2,1)S(1)}, bf16[40,4224]{1,0:T(8,128)(2,1)S(1)}, u32[]{:S(2)}, u32[]{:S(2)}) collective-permute-start(bf16[40,4224]{1,0:T(8,128)(2,1)S(1)} %collective-permute-done.1.refs_2_), channel_id=1, source_target_pairs={{0,2},{1,3},{2,0},{3,1},{4,6},{5,7},{6,4},{7,5},{8,10},{9,11},{10,... | collective-permute-start | bytes 1013768 | tf_op jit(solution)/shard_map/ppermute | solution.py:373
  31.9 23.2 %collective-permute-start.6 = (bf16[40,4224]{1,0:T(8,128)(2,1)S(1)}, bf16[40,4224]{1,0:T(8,128)(2,1)S(1)}, u32[]{:S(2)}, u32[]{:S(2)}) collective-permute-start(bf16[40,4224]{1,0:T(8,128)(2,1)S(1)} %collective-permute-done.2.refs_3_), channel_id=1, source_target_pairs={{0,2},{1,3},{2,0},{3,1},{4,6},{5,7},{6,4},{7,5},{8,10},{9,11},{10,... | collective-permute-start | bytes 1013768 | tf_op jit(solution)/shard_map/ppermute | solution.py:373
  37.0 21.2 %collective-permute-start.7 = (bf16[32,4224]{1,0:T(8,128)(2,1)S(1)}, bf16[32,4224]{1,0:T(8,128)(2,1)S(1)}, u32[]{:S(2)}, u32[]{:S(2)}) collective-permute-start(bf16[32,4224]{1,0:T(8,128)(2,1)S(1)} %cut.4.refs_0_), channel_id=1, source_target_pairs={{0,1},{1,0},{2,3},{3,2},{4,5},{5,4},{6,7},{7,6},{8,9},{9,8},{10,11... | collective-permute-start | bytes 811016 | tf_op jit(solution)/shard_map/ppermute | solution.py:376
  59.8 8.2 %collective-permute-start.12 = (bf16[128,4224]{1,0:T(8,128)(2,1)S(1)}, bf16[128,4224]{1,0:T(8,128)(2,1)S(1)}, u32[]{:S(2)}, u32[]{:S(2)}) collective-permute-start(bf16[128,4224]{1,0:T(8,128)(2,1)S(1)} %cut.6.refs_0_), channel_id=1, source_target_pairs={{0,1},{1,0},{2,3},{3,2},{4,5},{5,4},{6,7},{7,6},{8,9},{9,8},{10,11... | collective-permute-start | bytes 3244040 | tf_op jit(solution)/shard_map/ppermute | solution.py:376
  60.1 15.4 %collective-permute-start.14 = (bf16[128,4224]{1,0:T(8,128)(2,1)S(1)}, bf16[128,4224]{1,0:T(8,128)(2,1)S(1)}, u32[]{:S(2)}, u32[]{:S(2)}) collective-permute-start(bf16[128,4224]{1,0:T(8,128)(2,1)S(1)} %cut.7.refs_0_), channel_id=1, source_target_pairs={{0,1},{1,0},{2,3},{3,2},{4,5},{5,4},{6,7},{7,6},{8,9},{9,8},{10,11... | collective-permute-start | bytes 3244040 | tf_op jit(solution)/shard_map/ppermute | solution.py:376
  66.4 8.4 %collective-permute-start.11 = (bf16[32,4096]{1,0:T(8,128)(2,1)S(1)}, bf16[32,4096]{1,0:T(8,128)(2,1)S(1)}, u32[]{:S(2)}, u32[]{:S(2)}) collective-permute-start(bf16[32,4096]{1,0:T(8,128)(2,1)S(1)} %fold.11.refs_5_), channel_id=1, source_target_pairs={{0,2},{1,3},{2,0},{3,1},{4,6},{5,7},{6,4},{7,5},{8,10},{9,11},{10,... | collective-permute-start | bytes 786440 | tf_op jit(solution)/shard_map/ppermute | solution.py:373
  74.8 9.5 %collective-permute-start.17 = (bf16[128,4096]{1,0:T(8,128)(2,1)S(1)}, bf16[128,4096]{1,0:T(8,128)(2,1)S(1)}, u32[]{:S(2)}, u32[]{:S(2)}) collective-permute-start(bf16[128,4096]{1,0:T(8,128)(2,1)S(1)} %hold.3), channel_id=1, source_target_pairs={{0,1},{1,0},{2,3},{3,2},{4,5},{5,4},{6,7},{7,6},{8,9},{9,8},{10,11... | collective-permute-start | bytes 3145736 | tf_op jit(solution)/shard_map/ppermute | solution.py:376
  80.9 16.0 %collective-permute-start.16 = (bf16[128,4096]{1,0:T(8,128)(2,1)S(1)}, bf16[128,4096]{1,0:T(8,128)(2,1)S(1)}, u32[]{:S(2)}, u32[]{:S(2)}) collective-permute-start(bf16[128,4096]{1,0:T(8,128)(2,1)S(1)} %hold.2), channel_id=1, source_target_pairs={{0,1},{1,0},{2,3},{3,2},{4,5},{5,4},{6,7},{7,6},{8,9},{9,8},{10,11... | collective-permute-start | bytes 3145736 | tf_op jit(solution)/shard_map/ppermute | solution.py:376
  81.1 7.2 %collective-permute-start.15 = (bf16[8,4096]{1,0:T(8,128)(2,1)S(1)}, bf16[8,4096]{1,0:T(8,128)(2,1)S(1)}, u32[]{:S(2)}, u32[]{:S(2)}) collective-permute-start(bf16[8,4096]{1,0:T(8,128)(2,1)S(1)} %get-tuple-element.49.refs_1_), channel_id=1, source_target_pairs={{0,8},{4,12},{8,0},{12,4},{1,9},{5,13},{9,1},{13,5},{2,10},{6,14},... | collective-permute-start | bytes 196616 | tf_op jit(solution)/shard_map/ppermute | solution.py:370
  84.6 12.6 %collective-permute-start.22 = (bf16[32,4096]{1,0:T(8,128)(2,1)S(1)}, bf16[32,4096]{1,0:T(8,128)(2,1)S(1)}, u32[]{:S(2)}, u32[]{:S(2)}) collective-permute-start(bf16[32,4096]{1,0:T(8,128)(2,1)S(1)} %get-tuple-element.60), channel_id=1, source_target_pairs={{0,2},{1,3},{2,0},{3,1},{4,6},{5,7},{6,4},{7,5},{8,10},{9,11},{10,... | collective-permute-start | bytes 786440 | tf_op jit(solution)/shard_map/ppermute | solution.py:373
  86.1 15.6 %collective-permute-start.21 = (bf16[32,4096]{1,0:T(8,128)(2,1)S(1)}, bf16[32,4096]{1,0:T(8,128)(2,1)S(1)}, u32[]{:S(2)}, u32[]{:S(2)}) collective-permute-start(bf16[32,4096]{1,0:T(8,128)(2,1)S(1)} %get-tuple-element.58), channel_id=1, source_target_pairs={{0,2},{1,3},{2,0},{3,1},{4,6},{5,7},{6,4},{7,5},{8,10},{9,11},{10,... | collective-permute-start | bytes 786440 | tf_op jit(solution)/shard_map/ppermute | solution.py:373
  95.3 9.7 %collective-permute-start.19 = (bf16[32,4096]{1,0:T(8,128)(2,1)S(1)}, bf16[32,4096]{1,0:T(8,128)(2,1)S(1)}, u32[]{:S(2)}, u32[]{:S(2)}) collective-permute-start(bf16[32,4096]{1,0:T(8,128)(2,1)S(1)} %get-tuple-element.56), channel_id=1, source_target_pairs={{0,2},{1,3},{2,0},{3,1},{4,6},{5,7},{6,4},{7,5},{8,10},{9,11},{10,... | collective-permute-start | bytes 786440 | tf_op jit(solution)/shard_map/ppermute | solution.py:373
  97.2 8.4 %collective-permute-start.23 = (bf16[32,4096]{1,0:T(8,128)(2,1)S(1)}, bf16[32,4096]{1,0:T(8,128)(2,1)S(1)}, u32[]{:S(2)}, u32[]{:S(2)}) collective-permute-start(bf16[32,4096]{1,0:T(8,128)(2,1)S(1)} %add.4.refs_2_), channel_id=1, source_target_pairs={{0,4},{4,0},{8,12},{12,8},{1,5},{5,1},{9,13},{13,9},{2,6},{6,2},{1... | collective-permute-start | bytes 786440 | tf_op jit(solution)/shard_map/ppermute | solution.py:370
  101.7 8.2 %collective-permute-start.27 = (bf16[32,4096]{1,0:T(8,128)(2,1)S(1)}, bf16[32,4096]{1,0:T(8,128)(2,1)S(1)}, u32[]{:S(2)}, u32[]{:S(2)}) collective-permute-start(bf16[32,4096]{1,0:T(8,128)(2,1)S(1)} %pack.4.refs_0_), channel_id=1, source_target_pairs={{0,2},{1,3},{2,0},{3,1},{4,6},{5,7},{6,4},{7,5},{8,10},{9,11},{10,... | collective-permute-start | bytes 786440 | tf_op jit(solution)/shard_map/ppermute | solution.py:373
  115.5 9.2 %collective-permute-start.32 = (bf16[32,4096]{1,0:T(8,128)(2,1)S(1)}, bf16[32,4096]{1,0:T(8,128)(2,1)S(1)}, u32[]{:S(2)}, u32[]{:S(2)}) collective-permute-start(bf16[32,4096]{1,0:T(8,128)(2,1)S(1)} %fold.17), channel_id=1, source_target_pairs={{0,2},{1,3},{2,0},{3,1},{4,6},{5,7},{6,4},{7,5},{8,10},{9,11},{10,... | collective-permute-start | bytes 786440 | tf_op jit(solution)/shard_map/ppermute | solution.py:373
  117.1 18.3 %collective-permute-start.18 = (bf16[32,4096]{1,0:T(8,128)(2,1)S(1)}, bf16[32,4096]{1,0:T(8,128)(2,1)S(1)}, u32[]{:S(2)}, u32[]{:S(2)}) collective-permute-start(bf16[32,4096]{1,0:T(8,128)(2,1)S(1)} %get-tuple-element.54.refs_2_), channel_id=1, source_target_pairs={{0,2},{1,3},{2,0},{3,1},{4,6},{5,7},{6,4},{7,5},{8,10},{9,11},{10,... | collective-permute-start | bytes 786440 | tf_op jit(solution)/shard_map/ppermute | solution.py:373
  117.6 17.7 %collective-permute-start.20 = (bf16[32,4096]{1,0:T(8,128)(2,1)S(1)}, bf16[32,4096]{1,0:T(8,128)(2,1)S(1)}, u32[]{:S(2)}, u32[]{:S(2)}) collective-permute-start(bf16[32,4096]{1,0:T(8,128)(2,1)S(1)} %add.3.refs_3_), channel_id=1, source_target_pairs={{0,4},{4,0},{8,12},{12,8},{1,5},{5,1},{9,13},{13,9},{2,6},{6,2},{1... | collective-permute-start | bytes 786440 | tf_op jit(solution)/shard_map/ppermute | solution.py:370
  119.1 16.2 %collective-permute-start.24 = (bf16[32,4096]{1,0:T(8,128)(2,1)S(1)}, bf16[32,4096]{1,0:T(8,128)(2,1)S(1)}, u32[]{:S(2)}, u32[]{:S(2)}) collective-permute-start(bf16[32,4096]{1,0:T(8,128)(2,1)S(1)} %add.5.refs_2_), channel_id=1, source_target_pairs={{0,8},{4,12},{8,0},{12,4},{1,9},{5,13},{9,1},{13,5},{2,10},{6,14},... | collective-permute-start | bytes 786440 | tf_op jit(solution)/shard_map/ppermute | solution.py:370
  124.8 9.1 %collective-permute-start.33 = (bf16[16,4096]{1,0:T(8,128)(2,1)S(1)}, bf16[16,4096]{1,0:T(8,128)(2,1)S(1)}, u32[]{:S(2)}, u32[]{:S(2)}) collective-permute-start(bf16[16,4096]{1,0:T(8,128)(2,1)S(1)} %get-tuple-element.69), channel_id=1, source_target_pairs={{0,4},{4,0},{8,12},{12,8},{1,5},{5,1},{9,13},{13,9},{2,6},{6,2},{1... | collective-permute-start | bytes 393224 | tf_op jit(solution)/shard_map/ppermute | solution.py:370
  (27 other events, 208.1 us)

commit v3 on v2

--- a/solution.py
+++ b/solution.py
@@ -199,17 +199,50 @@
     )(*blocks, *after, *near)
 
 
-def add_kernel(*refs):
-    refs[-1][...] = sum(ref[...].astype(F32) for ref in refs[:-1]).astype(BF)
-
-
-def add(arrays):
-    return pl.pallas_call(
-        add_kernel,
-        out_shape=struct(*arrays[0].shape),
+def stage_kernel(count, *refs):
+    sources, targets, sems = refs[:count], refs[-count - 1 : -1], refs[-1]
+    moves = [
+        pltpu.make_async_copy(source, target, sems.at[number])
+        for number, (source, target) in enumerate(zip(sources, targets))
+    ]
+    for move in moves:
+        move.start()
+    for move in moves:
+        move.wait()
+
+
+def stage(arrays, limit, after):
+    count = len(arrays)
+    outs = pl.pallas_call(
+        functools.partial(stage_kernel, count),
+        out_shape=[struct(*array.shape) for array in arrays],
+        in_specs=[HBM] * count + [ANYWHERE] * len(after),
+        out_specs=[VECTORS] * count,
+        scratch_shapes=[pltpu.SemaphoreType.DMA((count,))],
+        compiler_params=pltpu.CompilerParams(vmem_limit_bytes=limit * MIB),
+        name="stage",
+    )(*arrays, *after)
+    return list(outs)
+
+
+def add_kernel(count, parts, *refs):
+    total = sum(ref[...].astype(F32) for ref in refs[:count]).astype(BF)
+    rows = total.shape[0] // parts
+    for number, out_ref in enumerate(refs[-parts:]):
+        out_ref[...] = total[number * rows : (number + 1) * rows]
+
+
+def add(arrays, after=(), parts=1):
+    rows, width = arrays[0].shape
+    outs = pl.pallas_call(
+        functools.partial(add_kernel, len(arrays), parts),
+        out_shape=[struct(rows // parts, width)] * parts,
+        in_specs=[VECTORS] * len(arrays) + [ANYWHERE] * len(after),
+        out_specs=[VECTORS] * parts,
         compiler_params=SMALL,
         name="add",
-    )(*arrays)
+    )(*arrays, *after)
+    return outs[0] if parts == 1 else list(outs)
 
 
 def fold_kernel(comes, parts, keep_ref, *refs):
@@ -286,23 +319,30 @@
     return list(outs)
 
 
-def mid_kernel(count, hid_ref, gain_ref, *refs):
+def mid_kernel(swapped, hid_ref, other_ref, gain_ref, held_ref, *refs):
     verified_ref, draft_ref = refs[-2:]
-    total = hid_ref[...].astype(F32) + sum(ref[...].astype(F32) for ref in refs[:count])
-    verified = total.astype(BF)
+    rows = hid_ref.shape[0]
+    held = held_ref[...].astype(F32)
+    own, other = held[:rows], held[rows:]
+    if swapped:
+        come = refs[0][...].astype(F32)
+        own, other = own + come[rows:], other + come[:rows]
+    verified = (hid_ref[...].astype(F32) + own).astype(BF)
     verified_ref[...] = verified
-    draft_ref[...] = (rms(verified.astype(F32)) * gain_ref[...]).astype(BF)
-
-
-def mid(hid, parts, gain, after):
+    beside = (other_ref[...].astype(F32) + other).astype(BF)
+    both = jnp.concatenate([verified.astype(F32), beside.astype(F32)], axis=0)
+    draft_ref[...] = (rms(both) * gain_ref[...]).astype(BF)
+
+
+def mid(hid, other, sums, gain, after):
     return pl.pallas_call(
-        functools.partial(mid_kernel, len(parts)),
-        out_shape=[struct(*hid.shape)] * 2,
-        in_specs=[VECTORS] * (2 + len(parts)) + [ANYWHERE] * len(after),
+        functools.partial(mid_kernel, len(sums) > 1),
+        out_shape=[struct(*hid.shape), struct(2 * hid.shape[0], hid.shape[1])],
+        in_specs=[VECTORS] * (3 + len(sums)) + [ANYWHERE] * len(after),
         out_specs=[VECTORS] * 2,
         compiler_params=SMALL,
         name="accepted_norm",
-    )(hid, gain, *parts, *after)
+    )(hid, other, gain, *sums, *after)
 
 
 def last_kernel(hid_ref, gain_ref, *refs):
@@ -375,16 +415,21 @@
     def near(self, x):
         return lax.ppermute(x, "tensor", [(i, i ^ 1) for i in range(self.columns)])
 
-    def widen(self, x, bit, after):
-        return pack([x, self.line(x, bit)], after)
-
-    def sides(self, x, after):
-        own = pack([x, self.far(x)], after, CUT)
-        return own + [self.near(piece) for piece in own]
-
     def meet(self, pieces):
-        comes = [self.near(piece) for piece in pieces[CUT:]]
-        return [fold(keep, [come], 1, [])[0] for keep, come in zip(pieces, comes)]
+        comes = [self.near(piece) for piece in pieces[2:]]
+        return [fold(keep, [come], 2, []) for keep, come in zip(pieces, comes)]
+
+    def meet_line(self, halves, first_waits, second_waits):
+        (keep_even, keep_odd), (send_even, send_odd) = halves
+        bits = bits_of(self.lines)
+        odd = add([keep_odd, self.far(send_odd)], first_waits)
+        come_even = self.far(send_even)
+        parts = 1 if len(bits) < 3 else 2
+        held = add([keep_even, come_even, self.line(odd, bits[-1])], second_waits(odd), parts)
+        for place, bit in enumerate(reversed(bits[1:-1])):
+            keep, send = held
+            held = add([keep, self.line(send, bit)], [], 1 if place == len(bits) - 3 else 2)
+        return held
 
 
 def bits_of(size):
@@ -434,13 +479,18 @@
     others = rounds * rows - chunk
     ext, hid, mark = prep(inputs, [list(range(draft))], columns)
     hid, rest_hid = hid[:chunk], hid[chunk:]
-
-    lined, offsets = [ext], [0]
+    hid_beside = links.line(hid, bits[0])
+
+    lined, offsets, crossed = [ext], [0], [links.far(ext)]
     for bit in bits:
-        lined = lined + [links.line(block, bit) for block in lined]
+        came = [links.line(block, bit) for block in lined]
+        if bit == bits[0]:
+            came = hold(came, crossed[-1:])
+        lined = lined + came
         offsets = offsets + [offset | bit for offset in offsets]
-    crossed = [links.far(block) for block in lined]
-    head = [cut(lined, 0, chunk, [], weights[:1]), cut(crossed, 0, chunk, [], weights[1:])]
+        crossed = crossed + [links.far(block) for block in came]
+    weights = stage(weights, 36, [lined[-1]])
+    head = [cut(lined, 0, chunk, [weights[0]], []), cut(crossed, 0, chunk, [hid_beside])]
     head += [links.near(piece) for piece in head]
     line_rest = cut(lined, chunk, others, head[2:])
     cross_rest = cut(crossed, chunk, others, head[2:])
@@ -448,47 +498,48 @@
     line_other = links.near(line_rest)
 
     halves = links.meet(units(head, mark, weights, True, []))
-    cross_keep, cross_send = units([cross_rest, cross_other], mark, weights, True, [halves[1]])
-    steps = []
-    keep, come = halves[0], links.far(halves[1])
-    for place, bit in enumerate(reversed(bits)):
-        waits = [cross_keep] if place == 0 else [line_keep] if place == 1 else []
-        keep, send = fold(keep, [come], 2, waits)
-        come = links.line(send, bit)
-        steps.append(send)
-        if place == 0:
-            line_keep, line_send = units(
-                [line_rest, line_other], mark, weights, True, [send]
-            )
-    cross_come = links.near(hold([cross_send], [steps[0]])[0])
-    line_come = links.near(hold([line_send], [steps[1]])[0])
-    features, draft_in = mid(
-        hid, over_sub([keep, come]), draft_gain.reshape(1, width), []
-    )
-    cross_parts = fold(cross_keep, [cross_come], lines, [])
+    cross_keep, cross_send = units([cross_rest, cross_other], mark, weights, True, [halves[1][1]])
+    lines_done = []
+
+    def second_waits(odd):
+        cross_come = links.near(hold([cross_send], [odd])[0])
+        parts = fold(cross_keep, [cross_come], lines, [])
+        lines_done.extend([odd, parts])
+        lines_done.extend(units([line_rest, line_other], mark, weights, True, [odd]))
+        return [lines_done[2]]
+
+    held = links.meet_line(halves, [cross_keep], second_waits)
+    odd, cross_parts, line_keep, line_send = lines_done
+    come = links.line(held, bits[0])
+    line_come = links.near(hold([line_send], [held])[0])
+    sums = [held, come]
+    if subs > 1:
+        come = jnp.concatenate([come[chunk:], come[:chunk]], axis=0)
+        sums = [lax.psum(held.astype(F32) + come.astype(F32), "sub")]
     line_parts = fold(line_keep, [line_come], lines, [])
 
-    held = {}
+    blocks = {}
     for place in reversed(range(lines)):
-        held[offsets[place]] = [line_parts[place], links.far(cross_parts[place])]
+        blocks[offsets[place]] = [line_parts[place], links.far(cross_parts[place])]
     summed = {}
     for bit in reversed(bits):
         for offset in reversed(offsets):
             if offset & bit and offset < 2 * bit * (lines // bit) and not offset & (bit - 1):
-                summed[offset] = add(held[offset])
-                held[offset ^ bit].append(links.line(summed[offset], bit))
-    rest_terms = held[0]
-    a = draft_in
-    for place, bit in enumerate(bits):
-        a = links.widen(a, bit, (([cross_parts[0]], [summed[lines - 1], held[lines // 2][1]])[place] if place < 2 else []))
-    own = pack([a, links.far(a)], [summed[lines // 2], summed[1]], CUT)
+                summed[offset] = add(blocks[offset])
+                blocks[offset ^ bit].append(links.line(summed[offset], bit))
+    rest_terms = blocks[0]
+    features, draft_in = mid(hid, hid_beside, sums, draft_gain.reshape(1, width), [summed[lines - 1], blocks[lines // 2][1]])
+    a_lined = [draft_in]
+    for bit in bits[1:]:
+        a_lined = a_lined + [links.line(block, bit) for block in a_lined]
+    a_crossed = [links.far(block) for block in a_lined]
+    own = [pack(a_lined, [summed[1]]), pack(a_crossed, [])]
     pieces = own + [links.near(piece) for piece in own]
-    halves = links.meet(units(pieces, mark, draft_weights, False, []))
-    keep, come = halves[0], links.far(halves[1])
-    for bit in reversed(bits):
-        keep, send = fold(keep, [come], 2, [])
-        come = links.line(send, bit)
-    terms = [keep, come]
+    halves = links.meet(units(pieces, mark, draft_weights, False, [summed[lines // 2]]))
+    held = links.meet_line(halves, [], lambda odd: [])
+    keep, send = add([held], [], 2)
+    terms = [keep, links.line(send, bits[0])]
+
     draft_out = last(features, terms, final_gain.reshape(1, width), requests, rounds)
     verified = merge(
         accepted,

time: 140 us -> 126 us (0.900)
  waiting for transfers between devices: 74 us -> 52.3 us
  Pallas kernels: 21.2 us -> 30.4 us
  local copies, waits for them, and re-layouts: 8.87 us -> 1.62 us
  starting transfers between devices: 34.9 us -> 40 us
    ppermute x12, waiting for transfers between devices: 38.3 us -> 28 us  [line(): return lax.ppermute(x, 'expert', [(i, i ^ bits) for i in range(self.lines)])]
    ppermute x11 -> x14, waiting for transfers between devices: 30.7 us -> 20.7 us  [far(): return lax.ppermute(x, 'tensor', [(i, i ^ 2) for i in range(self.columns)])]
    pallas_call x4 -> x10, Pallas kernels: 0.38 us -> 9.71 us  [the longest x1 9.11 us: stage(): pl.pallas_call(functools.partial(stage_kernel, count), out_shape=[struct(...]
    unnamed x33 -> x23, local copies, waits for them, and re-layouts: 8.84 us -> 0.76 us
    ppermute x12, starting transfers between devices: 18.4 us -> 22.3 us  [line(): return lax.ppermute(x, 'expert', [(i, i ^ bits) for i in range(self.lines)])]
    ppermute x11 -> x14, starting transfers between devices: 13.6 us -> 15.5 us  [far(): return lax.ppermute(x, 'tensor', [(i, i ^ 2) for i in range(self.columns)])]
  transfers between devices with their start and end apart: 35 -> 38, of which waited for: 19 -> 17; matrix products, arithmetic and copies ran while one was open for 0% -> 1% of each run, Pallas kernels for 12% -> 20%
where the time goes in v3:
time: 126 us; the launch traced here: 125 us
  waiting for transfers between devices  52.3 us (42%)
  starting transfers between devices  40 us (32%)
  Pallas kernels  30.4 us (24%)
  local copies, waits for them, and re-layouts  1.62 us (1%)
    ppermute x12, waiting for transfers between devices, line(): return lax.ppermute(x, 'expert', [(i, i ^ bits) for i in range(self.lines)])  28 us
    ppermute x12, starting transfers between devices, line(): return lax.ppermute(x, 'expert', [(i, i ^ bits) for i in range(self.lines)])  22.3 us
    ppermute x14, waiting for transfers between devices, far(): return lax.ppermute(x, 'tensor', [(i, i ^ 2) for i in range(self.columns)])  20.7 us
    ppermute x14, starting transfers between devices, far(): return lax.ppermute(x, 'tensor', [(i, i ^ 2) for i in range(self.columns)])  15.5 us
    pallas_call x4, Pallas kernels, units(): pl.pallas_call(functools.partial(unit_kernel, gated, parts, group), out_s...  15.3 us
    pallas_call x1, Pallas kernels, stage(): pl.pallas_call(functools.partial(stage_kernel, count), out_shape=[struct(...  9.11 us
    ppermute x12, waiting for transfers between devices, near(): return lax.ppermute(x, 'tensor', [(i, i ^ 1) for i in range(self.columns)])  3.6 us
    pallas_call x1, Pallas kernels, prep(): pl.pallas_call(functools.partial(prep_kernel, groups, columns, inputs[-1]...  2.65 us
  transfers between devices with their start and end apart: 38, of which 17 were waited for; matrix products, arithmetic and copies ran while one was open for 1% of the time, Pallas kernels for 20%

profile of v3, /device:TPU:0, one launch (start us, length us, event | category | flops | bytes accessed | tf_op | source)
XLA Modules:
  0.0 125.4 jit_solution(16923413264179141502)
XLA Ops:
  0.6 2.7 %prep.1 = (bf16[40,4224]{1,0:T(8,128)(2,1)}, bf16[40,4096]{1,0:T(8,128)(2,1)}, f32[1,128]{1,0:T(1,128)}) custom-call(s32[2,4]{1,0:T(2,128)} %bitcast.17, bf16[10,4,4096]{2,1,0:T(4,128)(2,1)} %bitcast.22, s32[4,8,10]{2,1,0:T(8,128)} %bitcast.25, f32[1,4096]{1,0:T(1,128)} %bitcast.26, bf16[16,4096]{1,0:T(8,128)(2,1)} %bitcast.24), custom_call_target="tpu_custom_call" | custom-call | tf_op jit(solution)/shard_map/prep/pallas_call | solution.py:138
  3.3 3.0 %collective-permute-start.2 = (bf16[40,4224]{1,0:T(8,128)(2,1)}, bf16[40,4224]{1,0:T(8,128)(2,1)S(1)}, u32[]{:S(2)}, u32[]{:S(2)}) collective-permute-start(bf16[40,4224]{1,0:T(8,128)(2,1)} %get-tuple-element.42.refs_0_), channel_id=1, source_target_pairs={{0,2},{1,3},{2,0},{3,1},{4,6},{5,7},{6,4},{7,5},{8,10},{9,11},{10,... | collective-permute-start | bytes 1013768 | tf_op jit(solution)/shard_map/ppermute | solution.py:413
  6.3 2.6 %collective-permute-start.1 = (bf16[40,4224]{1,0:T(8,128)(2,1)}, bf16[40,4224]{1,0:T(8,128)(2,1)S(1)}, u32[]{:S(2)}, u32[]{:S(2)}) collective-permute-start(bf16[40,4224]{1,0:T(8,128)(2,1)} %get-tuple-element.42.refs_0_), channel_id=1, source_target_pairs={{0,8},{4,12},{8,0},{12,4},{1,9},{5,13},{9,1},{13,5},{2,10},{6,14},... | collective-permute-start | bytes 1013768 | tf_op jit(solution)/shard_map/ppermute | solution.py:410
  10.5 4.0 %collective-permute-done.2.refs_1_.refs_0_ = bf16[40,4224]{1,0:T(8,128)(2,1)S(1)} collective-permute-done((bf16[40,4224]{1,0:T(8,128)(2,1)}, bf16[40,4224]{1,0:T(8,128)(2,1)S(1)}, u32[]{:S(2)}, u32[]{:S(2)}) %collective-permute-start.2) | collective-permute-done | bytes 337952 | tf_op jit(solution)/shard_map/ppermute | solution.py:413
  14.4 9.7 %collective-permute-done.1.refs_0_ = bf16[40,4224]{1,0:T(8,128)(2,1)S(1)} collective-permute-done((bf16[40,4224]{1,0:T(8,128)(2,1)}, bf16[40,4224]{1,0:T(8,128)(2,1)S(1)}, u32[]{:S(2)}, u32[]{:S(2)}) %collective-permute-start.1) | collective-permute-done | bytes 337952 | tf_op jit(solution)/shard_map/ppermute | solution.py:410
  26.8 6.1 %collective-permute-done.4.refs_3_ = bf16[40,4224]{1,0:T(8,128)(2,1)S(1)} collective-permute-done((bf16[40,4224]{1,0:T(8,128)(2,1)S(1)}, bf16[40,4224]{1,0:T(8,128)(2,1)S(1)}, u32[]{:S(2)}, u32[]{:S(2)}) %collective-permute-start.4) | collective-permute-done | bytes 337952 | tf_op jit(solution)/shard_map/ppermute | solution.py:410
  34.3 3.3 %collective-permute-start = (bf16[8,4096]{1,0:T(8,128)(2,1)S(1)}, bf16[8,4096]{1,0:T(8,128)(2,1)S(1)}, u32[]{:S(2)}, u32[]{:S(2)}) collective-permute-start(bf16[8,4096]{1,0:T(8,128)(2,1)S(1)} %slice.6.hid_ref), channel_id=1, source_target_pairs={{0,8},{4,12},{8,0},{12,4},{1,9},{5,13},{9,1},{13,5},{2,10},{6,14},... | collective-permute-start | bytes 196616 | tf_op jit(solution)/shard_map/ppermute | solution.py:410
  37.6 9.1 %stage.1 = (bf16[4096,768]{1,0:T(8,128)(2,1)S(1)}, bf16[4096,768]{1,0:T(8,128)(2,1)S(1)}, bf16[768,4096]{1,0:T(8,128)(2,1)}) custom-call(bf16[4096,768]{1,0:T(8,128)(2,1)} %bitcast.19, bf16[4096,768]{1,0:T(8,128)(2,1)} %bitcast.20, bf16[768,4096]{1,0:T(8,128)(2,1)} %bitcast.21, bf16[40,4224]{1,0:T(8,128)(2,1)S(1)} %collective-permute-done.4.refs_3_), custom_call_target="tpu_custom_call" | custom-call | tf_op jit(solution)/shard_map/stage/pallas_call | solution.py:216
  46.9 2.0 %collective-permute-done.7.refs_3_ = bf16[40,4224]{1,0:T(8,128)(2,1)S(1)} collective-permute-done((bf16[40,4224]{1,0:T(8,128)(2,1)S(1)}, bf16[40,4224]{1,0:T(8,128)(2,1)S(1)}, u32[]{:S(2)}, u32[]{:S(2)}) %collective-permute-start.7) | collective-permute-done | bytes 337952 | tf_op jit(solution)/shard_map/ppermute | solution.py:413
  51.3 2.8 %experts.3 = (bf16[32,4096]{1,0:T(8,128)(2,1)S(1)}, bf16[32,4096]{1,0:T(8,128)(2,1)S(1)}, bf16[32,4096]{1,0:T(8,128)(2,1)S(1)}, bf16[32,4096]{1,0:T(8,128)(2,1)S(1)}) custom-call(f32[1,128]{1,0:T(1,128)S(1)} %copy-done.6, bf16[32,4224]{1,0:T(8,128)(2,1)S(1)} %cut.4.refs_0_, bf16[32,4224]{1,0:T(8,128)(2,1)S(1)} %cut.5.refs_1_, ...), custom_call_target="tpu_custom_call" | custom-call | tf_op jit(solution)/shard_map/experts/pallas_call | solution.py:307
  56.5 5.2 %experts.4 = (bf16[128,4096]{1,0:T(8,128)(2,1)S(1)}, bf16[128,4096]{1,0:T(8,128)(2,1)S(1)}) custom-call(f32[1,128]{1,0:T(1,128)S(1)} %copy-done.6, bf16[128,4224]{1,0:T(8,128)(2,1)S(1)} %cut.6.refs_0_, bf16[128,4224]{1,0:T(8,128)(2,1)S(1)} %collective-permute-done.14.refs_1_, bf16[4096,768]{1,0:T(8,128)(2,1)S(1)} %get-tuple-element.43.refs_4_.refs_2_, ...), custom_call_target="tpu_custom_call" | custom-call | tf_op jit(solution)/shard_map/experts/pallas_call | solution.py:307
  63.6 5.4 %experts.5 = (bf16[128,4096]{1,0:T(8,128)(2,1)S(1)}, bf16[128,4096]{1,0:T(8,128)(2,1)S(1)}) custom-call(f32[1,128]{1,0:T(1,128)S(1)} %copy-done.6, bf16[128,4224]{1,0:T(8,128)(2,1)S(1)} %cut.7.refs_0_, bf16[128,4224]{1,0:T(8,128)(2,1)S(1)} %collective-permute-done.16.refs_1_, bf16[4096,768]{1,0:T(8,128)(2,1)S(1)} %get-tuple-element.43.refs_4_.refs_2_, ...), custom_call_target="tpu_custom_call" | custom-call | tf_op jit(solution)/shard_map/experts/pallas_call | solution.py:307
  71.6 3.3 %collective-permute-start.17 = (bf16[16,4096]{1,0:T(8,128)(2,1)S(1)}, bf16[16,4096]{1,0:T(8,128)(2,1)S(1)}, u32[]{:S(2)}, u32[]{:S(2)}) collective-permute-start(bf16[16,4096]{1,0:T(8,128)(2,1)S(1)} %add.9.refs_1_.held_ref), channel_id=1, source_target_pairs={{0,8},{4,12},{8,0},{12,4},{1,9},{5,13},{9,1},{13,5},{2,10},{6,14},... | collective-permute-start | bytes 393224 | tf_op jit(solution)/shard_map/ppermute | solution.py:410
  75.7 3.0 %collective-permute-done.20.refs_1_ = bf16[32,4096]{1,0:T(8,128)(2,1)S(1)} collective-permute-done((bf16[32,4096]{1,0:T(8,128)(2,1)S(1)}, bf16[32,4096]{1,0:T(8,128)(2,1)S(1)}, u32[]{:S(2)}, u32[]{:S(2)}) %collective-permute-start.20) | collective-permute-done | bytes 262176 | tf_op jit(solution)/shard_map/ppermute | solution.py:413
  78.7 2.5 %collective-permute-done.17.refs_0_ = bf16[16,4096]{1,0:T(8,128)(2,1)S(1)} collective-permute-done((bf16[16,4096]{1,0:T(8,128)(2,1)S(1)}, bf16[16,4096]{1,0:T(8,128)(2,1)S(1)}, u32[]{:S(2)}, u32[]{:S(2)}) %collective-permute-start.17) | collective-permute-done | bytes 131104 | tf_op jit(solution)/shard_map/ppermute | solution.py:410
  81.2 3.0 %collective-permute-done.21.refs_2_.refs_1_ = bf16[32,4096]{1,0:T(8,128)(2,1)S(1)} collective-permute-done((bf16[32,4096]{1,0:T(8,128)(2,1)S(1)}, bf16[32,4096]{1,0:T(8,128)(2,1)S(1)}, u32[]{:S(2)}, u32[]{:S(2)}) %collective-permute-start.21) | collective-permute-done | bytes 262176 | tf_op jit(solution)/shard_map/ppermute | solution.py:413
  86.8 2.7 %collective-permute-done.27.refs_1_ = bf16[16,4096]{1,0:T(8,128)(2,1)S(1)} collective-permute-done((bf16[16,4096]{1,0:T(8,128)(2,1)S(1)}, bf16[16,4096]{1,0:T(8,128)(2,1)S(1)}, u32[]{:S(2)}, u32[]{:S(2)}) %collective-permute-start.27) | collective-permute-done | bytes 131104 | tf_op jit(solution)/shard_map/ppermute | solution.py:410
  92.7 2.4 %collective-permute-done.29.refs_1_ = bf16[16,4096]{1,0:T(8,128)(2,1)S(1)} collective-permute-done((bf16[16,4096]{1,0:T(8,128)(2,1)S(1)}, bf16[16,4096]{1,0:T(8,128)(2,1)S(1)}, u32[]{:S(2)}, u32[]{:S(2)}) %collective-permute-start.29) | collective-permute-done | bytes 131104 | tf_op jit(solution)/shard_map/ppermute | solution.py:413
  95.2 1.9 %collective-permute-done.25.refs_2_ = bf16[32,4096]{1,0:T(8,128)(2,1)S(1)} collective-permute-done((bf16[32,4096]{1,0:T(8,128)(2,1)S(1)}, bf16[32,4096]{1,0:T(8,128)(2,1)S(1)}, u32[]{:S(2)}, u32[]{:S(2)}) %collective-permute-start.25) | collective-permute-done | bytes 262176 | tf_op jit(solution)/shard_map/ppermute | solution.py:410
  97.2 2.0 %drafter.1 = (bf16[32,4096]{1,0:T(8,128)(2,1)S(1)}, bf16[32,4096]{1,0:T(8,128)(2,1)S(1)}, bf16[32,4096]{1,0:T(8,128)(2,1)S(1)}, bf16[32,4096]{1,0:T(8,128)(2,1)S(1)}) custom-call(f32[1,128]{1,0:T(1,128)S(1)} %copy-done.6, bf16[32,4096]{1,0:T(8,128)(2,1)S(1)} %pack.2.refs_0_, bf16[32,4096]{1,0:T(8,128)(2,1)S(1)} %pack.3.refs_1_, ...), custom_call_target="tpu_custom_call" | custom-call | tf_op jit(solution)/shard_map/drafter/pallas_call | solution.py:307
  104.2 3.3 %collective-permute-start.26 = (bf16[32,4096]{1,0:T(8,128)(2,1)S(1)}, bf16[32,4096]{1,0:T(8,128)(2,1)S(1)}, u32[]{:S(2)}, u32[]{:S(2)}) collective-permute-start(bf16[32,4096]{1,0:T(8,128)(2,1)S(1)} %add.12.refs_7_), channel_id=1, source_target_pairs={{0,8},{4,12},{8,0},{12,4},{1,9},{5,13},{9,1},{13,5},{2,10},{6,14},... | collective-permute-start | bytes 786440 | tf_op jit(solution)/shard_map/ppermute | solution.py:410
  109.3 5.6 %collective-permute-done.34.refs_1_ = bf16[16,4096]{1,0:T(8,128)(2,1)S(1)} collective-permute-done((bf16[16,4096]{1,0:T(8,128)(2,1)S(1)}, bf16[16,4096]{1,0:T(8,128)(2,1)S(1)}, u32[]{:S(2)}, u32[]{:S(2)}) %collective-permute-start.34) | collective-permute-done | bytes 131104 | tf_op jit(solution)/shard_map/ppermute | solution.py:413
  114.9 4.3 %collective-permute-done.36.refs_2_ = bf16[16,4096]{1,0:T(8,128)(2,1)S(1)} collective-permute-done((bf16[16,4096]{1,0:T(8,128)(2,1)S(1)}, bf16[16,4096]{1,0:T(8,128)(2,1)S(1)}, u32[]{:S(2)}, u32[]{:S(2)}) %collective-permute-start.36) | collective-permute-done | bytes 131104 | tf_op jit(solution)/shard_map/ppermute | solution.py:410
  119.3 2.9 %collective-permute-start.37 = (bf16[8,4096]{1,0:T(8,128)(2,1)S(1)}, bf16[8,4096]{1,0:T(8,128)(2,1)S(1)}, u32[]{:S(2)}, u32[]{:S(2)}) collective-permute-start(bf16[8,4096]{1,0:T(8,128)(2,1)S(1)} %get-tuple-element.77), channel_id=1, source_target_pairs={{0,8},{4,12},{8,0},{12,4},{1,9},{5,13},{9,1},{13,5},{2,10},{6,14},... | collective-permute-start | bytes 196616 | tf_op jit(solution)/shard_map/ppermute | solution.py:410
  (110 shorter events, 31.9 us)
Async XLA Ops:
  3.3 11.1 %collective-permute-start.2 = (bf16[40,4224]{1,0:T(8,128)(2,1)}, bf16[40,4224]{1,0:T(8,128)(2,1)S(1)}, u32[]{:S(2)}, u32[]{:S(2)}) collective-permute-start(bf16[40,4224]{1,0:T(8,128)(2,1)} %get-tuple-element.42.refs_0_), channel_id=1, source_target_pairs={{0,2},{1,3},{2,0},{3,1},{4,6},{5,7},{6,4},{7,5},{8,10},{9,11},{10,... | collective-permute-start | bytes 1013768 | tf_op jit(solution)/shard_map/ppermute | solution.py:413
  6.3 17.9 %collective-permute-start.1 = (bf16[40,4224]{1,0:T(8,128)(2,1)}, bf16[40,4224]{1,0:T(8,128)(2,1)S(1)}, u32[]{:S(2)}, u32[]{:S(2)}) collective-permute-start(bf16[40,4224]{1,0:T(8,128)(2,1)} %get-tuple-element.42.refs_0_), channel_id=1, source_target_pairs={{0,8},{4,12},{8,0},{12,4},{1,9},{5,13},{9,1},{13,5},{2,10},{6,14},... | collective-permute-start | bytes 1013768 | tf_op jit(solution)/shard_map/ppermute | solution.py:410
  8.9 16.5 %collective-permute-start.3 = (bf16[40,4224]{1,0:T(8,128)(2,1)}, bf16[40,4224]{1,0:T(8,128)(2,1)S(1)}, u32[]{:S(2)}, u32[]{:S(2)}) collective-permute-start(bf16[40,4224]{1,0:T(8,128)(2,1)} %get-tuple-element.42.refs_0_), channel_id=1, source_target_pairs={{0,4},{4,0},{8,12},{12,8},{1,5},{5,1},{9,13},{13,9},{2,6},{6,2},{1... | collective-permute-start | bytes 1013768 | tf_op jit(solution)/shard_map/ppermute | solution.py:410
  24.2 8.8 %collective-permute-start.4 = (bf16[40,4224]{1,0:T(8,128)(2,1)S(1)}, bf16[40,4224]{1,0:T(8,128)(2,1)S(1)}, u32[]{:S(2)}, u32[]{:S(2)}) collective-permute-start(bf16[40,4224]{1,0:T(8,128)(2,1)S(1)} %hold.3.refs_1_), channel_id=1, source_target_pairs={{0,4},{4,0},{8,12},{12,8},{1,5},{5,1},{9,13},{13,9},{2,6},{6,2},{1... | collective-permute-start | bytes 1013768 | tf_op jit(solution)/shard_map/ppermute | solution.py:410
  24.8 22.1 %collective-permute-start.5 = (bf16[40,4224]{1,0:T(8,128)(2,1)S(1)}, bf16[40,4224]{1,0:T(8,128)(2,1)S(1)}, u32[]{:S(2)}, u32[]{:S(2)}) collective-permute-start(bf16[40,4224]{1,0:T(8,128)(2,1)S(1)} %hold.3.refs_1_), channel_id=1, source_target_pairs={{0,2},{1,3},{2,0},{3,1},{4,6},{5,7},{6,4},{7,5},{8,10},{9,11},{10,... | collective-permute-start | bytes 1013768 | tf_op jit(solution)/shard_map/ppermute | solution.py:413
  25.4 21.5 %collective-permute-start.6 = (bf16[40,4224]{1,0:T(8,128)(2,1)S(1)}, bf16[40,4224]{1,0:T(8,128)(2,1)S(1)}, u32[]{:S(2)}, u32[]{:S(2)}) collective-permute-start(bf16[40,4224]{1,0:T(8,128)(2,1)S(1)} %collective-permute-done.3.refs_2_), channel_id=1, source_target_pairs={{0,2},{1,3},{2,0},{3,1},{4,6},{5,7},{6,4},{7,5},{8,10},{9,11},{10,... | collective-permute-start | bytes 1013768 | tf_op jit(solution)/shard_map/ppermute | solution.py:413
  32.9 15.9 %collective-permute-start.7 = (bf16[40,4224]{1,0:T(8,128)(2,1)S(1)}, bf16[40,4224]{1,0:T(8,128)(2,1)S(1)}, u32[]{:S(2)}, u32[]{:S(2)}) collective-permute-start(bf16[40,4224]{1,0:T(8,128)(2,1)S(1)} %collective-permute-done.4.refs_3_), channel_id=1, source_target_pairs={{0,2},{1,3},{2,0},{3,1},{4,6},{5,7},{6,4},{7,5},{8,10},{9,11},{10,... | collective-permute-start | bytes 1013768 | tf_op jit(solution)/shard_map/ppermute | solution.py:413
  34.3 12.6 %collective-permute-start = (bf16[8,4096]{1,0:T(8,128)(2,1)S(1)}, bf16[8,4096]{1,0:T(8,128)(2,1)S(1)}, u32[]{:S(2)}, u32[]{:S(2)}) collective-permute-start(bf16[8,4096]{1,0:T(8,128)(2,1)S(1)} %slice.6.hid_ref), channel_id=1, source_target_pairs={{0,8},{4,12},{8,0},{12,4},{1,9},{5,13},{9,1},{13,5},{2,10},{6,14},... | collective-permute-start | bytes 196616 | tf_op jit(solution)/shard_map/ppermute | solution.py:410
  50.9 12.7 %collective-permute-start.16 = (bf16[128,4224]{1,0:T(8,128)(2,1)S(1)}, bf16[128,4224]{1,0:T(8,128)(2,1)S(1)}, u32[]{:S(2)}, u32[]{:S(2)}) collective-permute-start(bf16[128,4224]{1,0:T(8,128)(2,1)S(1)} %cut.7.refs_0_), channel_id=1, source_target_pairs={{0,1},{1,0},{2,3},{3,2},{4,5},{5,4},{6,7},{7,6},{8,9},{9,8},{10,11... | collective-permute-start | bytes 3244040 | tf_op jit(solution)/shard_map/ppermute | solution.py:416
  61.7 7.5 %collective-permute-start.19 = (bf16[128,4096]{1,0:T(8,128)(2,1)S(1)}, bf16[128,4096]{1,0:T(8,128)(2,1)S(1)}, u32[]{:S(2)}, u32[]{:S(2)}) collective-permute-start(bf16[128,4096]{1,0:T(8,128)(2,1)S(1)} %hold.5), channel_id=1, source_target_pairs={{0,1},{1,0},{2,3},{3,2},{4,5},{5,4},{6,7},{7,6},{8,9},{9,8},{10,11... | collective-permute-start | bytes 3145736 | tf_op jit(solution)/shard_map/ppermute | solution.py:416
  61.8 7.2 %collective-permute-start.12 = (bf16[16,4096]{1,0:T(8,128)(2,1)S(1)}, bf16[16,4096]{1,0:T(8,128)(2,1)S(1)}, u32[]{:S(2)}, u32[]{:S(2)}) collective-permute-start(bf16[16,4096]{1,0:T(8,128)(2,1)S(1)} %get-tuple-element.51), channel_id=1, source_target_pairs={{0,2},{1,3},{2,0},{3,1},{4,6},{5,7},{6,4},{7,5},{8,10},{9,11},{10,... | collective-permute-start | bytes 393224 | tf_op jit(solution)/shard_map/ppermute | solution.py:413
  69.5 9.2 %collective-permute-start.20 = (bf16[32,4096]{1,0:T(8,128)(2,1)S(1)}, bf16[32,4096]{1,0:T(8,128)(2,1)S(1)}, u32[]{:S(2)}, u32[]{:S(2)}) collective-permute-start(bf16[32,4096]{1,0:T(8,128)(2,1)S(1)} %get-tuple-element.59), channel_id=1, source_target_pairs={{0,2},{1,3},{2,0},{3,1},{4,6},{5,7},{6,4},{7,5},{8,10},{9,11},{10,... | collective-permute-start | bytes 786440 | tf_op jit(solution)/shard_map/ppermute | solution.py:413
  70.7 13.5 %collective-permute-start.21 = (bf16[32,4096]{1,0:T(8,128)(2,1)S(1)}, bf16[32,4096]{1,0:T(8,128)(2,1)S(1)}, u32[]{:S(2)}, u32[]{:S(2)}) collective-permute-start(bf16[32,4096]{1,0:T(8,128)(2,1)S(1)} %get-tuple-element.60), channel_id=1, source_target_pairs={{0,2},{1,3},{2,0},{3,1},{4,6},{5,7},{6,4},{7,5},{8,10},{9,11},{10,... | collective-permute-start | bytes 786440 | tf_op jit(solution)/shard_map/ppermute | solution.py:413
  71.6 9.7 %collective-permute-start.17 = (bf16[16,4096]{1,0:T(8,128)(2,1)S(1)}, bf16[16,4096]{1,0:T(8,128)(2,1)S(1)}, u32[]{:S(2)}, u32[]{:S(2)}) collective-permute-start(bf16[16,4096]{1,0:T(8,128)(2,1)S(1)} %add.9.refs_1_.held_ref), channel_id=1, source_target_pairs={{0,8},{4,12},{8,0},{12,4},{1,9},{5,13},{9,1},{13,5},{2,10},{6,14},... | collective-permute-start | bytes 393224 | tf_op jit(solution)/shard_map/ppermute | solution.py:410
  74.8 16.9 %collective-permute-start.23 = (bf16[32,4096]{1,0:T(8,128)(2,1)S(1)}, bf16[32,4096]{1,0:T(8,128)(2,1)S(1)}, u32[]{:S(2)}, u32[]{:S(2)}) collective-permute-start(bf16[32,4096]{1,0:T(8,128)(2,1)S(1)} %get-tuple-element.65), channel_id=1, source_target_pairs={{0,2},{1,3},{2,0},{3,1},{4,6},{5,7},{6,4},{7,5},{8,10},{9,11},{10,... | collective-permute-start | bytes 786440 | tf_op jit(solution)/shard_map/ppermute | solution.py:413
  86.3 6.4 %collective-permute-start.28 = (bf16[16,4096]{1,0:T(8,128)(2,1)S(1)}, bf16[16,4096]{1,0:T(8,128)(2,1)S(1)}, u32[]{:S(2)}, u32[]{:S(2)}) collective-permute-start(bf16[16,4096]{1,0:T(8,128)(2,1)S(1)} %get-tuple-element.67.refs_0_), channel_id=1, source_target_pairs={{0,2},{1,3},{2,0},{3,1},{4,6},{5,7},{6,4},{7,5},{8,10},{9,11},{10,... | collective-permute-start | bytes 393224 | tf_op jit(solution)/shard_map/ppermute | solution.py:413
  90.7 6.4 %collective-permute-start.25 = (bf16[32,4096]{1,0:T(8,128)(2,1)S(1)}, bf16[32,4096]{1,0:T(8,128)(2,1)S(1)}, u32[]{:S(2)}, u32[]{:S(2)}) collective-permute-start(bf16[32,4096]{1,0:T(8,128)(2,1)S(1)} %add.10.refs_1_), channel_id=1, source_target_pairs={{0,4},{4,0},{8,12},{12,8},{1,5},{5,1},{9,13},{13,9},{2,6},{6,2},{1... | collective-permute-start | bytes 786440 | tf_op jit(solution)/shard_map/ppermute | solution.py:410
  99.3 8.2 %collective-permute-start.32 = (bf16[32,4096]{1,0:T(8,128)(2,1)S(1)}, bf16[32,4096]{1,0:T(8,128)(2,1)S(1)}, u32[]{:S(2)}, u32[]{:S(2)}) collective-permute-start(bf16[32,4096]{1,0:T(8,128)(2,1)S(1)} %get-tuple-element.69), channel_id=1, source_target_pairs={{0,1},{1,0},{2,3},{3,2},{4,5},{5,4},{6,7},{7,6},{8,9},{9,8},{10,11... | collective-permute-start | bytes 786440 | tf_op jit(solution)/shard_map/ppermute | solution.py:416
  100.9 8.0 %collective-permute-start.35 = (bf16[16,4096]{1,0:T(8,128)(2,1)S(1)}, bf16[16,4096]{1,0:T(8,128)(2,1)S(1)}, u32[]{:S(2)}, u32[]{:S(2)}) collective-permute-start(bf16[16,4096]{1,0:T(8,128)(2,1)S(1)} %get-tuple-element.75), channel_id=1, source_target_pairs={{0,2},{1,3},{2,0},{3,1},{4,6},{5,7},{6,4},{7,5},{8,10},{9,11},{10,... | collective-permute-start | bytes 393224 | tf_op jit(solution)/shard_map/ppermute | solution.py:413
  101.8 20.4 %collective-permute-start.22 = (bf16[32,4096]{1,0:T(8,128)(2,1)S(1)}, bf16[32,4096]{1,0:T(8,128)(2,1)S(1)}, u32[]{:S(2)}, u32[]{:S(2)}) collective-permute-start(bf16[32,4096]{1,0:T(8,128)(2,1)S(1)} %get-tuple-element.63), channel_id=1, source_target_pairs={{0,2},{1,3},{2,0},{3,1},{4,6},{5,7},{6,4},{7,5},{8,10},{9,11},{10,... | collective-permute-start | bytes 786440 | tf_op jit(solution)/shard_map/ppermute | solution.py:413
  103.0 19.2 %collective-permute-start.24 = (bf16[32,4096]{1,0:T(8,128)(2,1)S(1)}, bf16[32,4096]{1,0:T(8,128)(2,1)S(1)}, u32[]{:S(2)}, u32[]{:S(2)}) collective-permute-start(bf16[32,4096]{1,0:T(8,128)(2,1)S(1)} %add.11.refs_2_), channel_id=1, source_target_pairs={{0,4},{4,0},{8,12},{12,8},{1,5},{5,1},{9,13},{13,9},{2,6},{6,2},{1... | collective-permute-start | bytes 786440 | tf_op jit(solution)/shard_map/ppermute | solution.py:410
  104.2 18.0 %collective-permute-start.26 = (bf16[32,4096]{1,0:T(8,128)(2,1)S(1)}, bf16[32,4096]{1,0:T(8,128)(2,1)S(1)}, u32[]{:S(2)}, u32[]{:S(2)}) collective-permute-start(bf16[32,4096]{1,0:T(8,128)(2,1)S(1)} %add.12.refs_7_), channel_id=1, source_target_pairs={{0,8},{4,12},{8,0},{12,4},{1,9},{5,13},{9,1},{13,5},{2,10},{6,14},... | collective-permute-start | bytes 786440 | tf_op jit(solution)/shard_map/ppermute | solution.py:410
  107.5 7.4 %collective-permute-start.34 = (bf16[16,4096]{1,0:T(8,128)(2,1)S(1)}, bf16[16,4096]{1,0:T(8,128)(2,1)S(1)}, u32[]{:S(2)}, u32[]{:S(2)}) collective-permute-start(bf16[16,4096]{1,0:T(8,128)(2,1)S(1)} %get-tuple-element.73), channel_id=1, source_target_pairs={{0,2},{1,3},{2,0},{3,1},{4,6},{5,7},{6,4},{7,5},{8,10},{9,11},{10,... | collective-permute-start | bytes 393224 | tf_op jit(solution)/shard_map/ppermute | solution.py:413
  108.9 10.2 %collective-permute-start.36 = (bf16[16,4096]{1,0:T(8,128)(2,1)S(1)}, bf16[16,4096]{1,0:T(8,128)(2,1)S(1)}, u32[]{:S(2)}, u32[]{:S(2)}) collective-permute-start(bf16[16,4096]{1,0:T(8,128)(2,1)S(1)} %add.13), channel_id=1, source_target_pairs={{0,4},{4,0},{8,12},{12,8},{1,5},{5,1},{9,13},{13,9},{2,6},{6,2},{1... | collective-permute-start | bytes 393224 | tf_op jit(solution)/shard_map/ppermute | solution.py:410
  (25 other events, 240.3 us)

commit v4 on v3

--- a/solution.py
+++ b/solution.py
@@ -49,7 +49,7 @@
     return found
 
 
-def reorder(layers, accepted_ref, hidden_ref, ids_ref, gain_ref, router_ref, ext_ref, hid_ref):
+def reorder(layers, accepted_ref, hidden_ref, ids_ref, gain_ref, router_ref, ext_ref, hid_ref, more_ref):
     rows, rounds, width = hidden_ref.shape
     requests = accepted_ref.shape[0]
     draft = rows // requests
@@ -74,7 +74,8 @@
                 )
             pieces.append(found)
     raw = jnp.concatenate(pieces, axis=0)
-    hid_ref[...] = raw.astype(BF)
+    hid_ref[...] = raw[:chunk].astype(BF)
+    more_ref[...] = raw[chunk:].astype(BF)
     normed = (rms(raw) * gain_ref[...]).astype(BF)
     ext_ref[:, :width] = normed
     count = len(layers) * chunk
@@ -124,7 +125,7 @@
     for move in moves:
         move.wait()
     for number, layers in enumerate(groups):
-        reorder(layers, *targets, outs[2 * number], outs[2 * number + 1])
+        reorder(layers, *targets, *outs[3 * number : 3 * number + 3])
 
 
 def prep(inputs, groups, columns):
@@ -133,7 +134,8 @@
     shapes = []
     for layers in groups:
         count = len(layers) * rounds * accepted.shape[0]
-        shapes += [struct(count, width + LANES), struct(count, width)]
+        chunk = rounds * accepted.shape[0]
+        shapes += [struct(count, width + LANES), struct(chunk, width), struct(count - chunk, width)]
     shapes.append(jax.ShapeDtypeStruct((1, LANES), F32))
     return pl.pallas_call(
         functools.partial(prep_kernel, groups, columns, inputs[-1].shape[0]),
@@ -349,15 +351,16 @@
     out_ref = refs[-1]
     total = hid_ref[...].astype(F32) + sum(ref[...].astype(F32) for ref in refs[:-1])
     result = (rms(total) * gain_ref[...]).astype(BF).astype(F32)
-    requests, rounds, _ = out_ref.shape
-    for request in range(requests):
-        out_ref[request] = result[request * rounds : (request + 1) * rounds].astype(BF)
+    rounds, requests, _ = out_ref.shape
+    for turn in range(rounds):
+        members = [result[turn + request * rounds][None] for request in range(requests)]
+        out_ref[turn] = jnp.concatenate(members, axis=0).astype(BF)
 
 
 def last(hid, parts, gain, requests, rounds):
     return pl.pallas_call(
         last_kernel,
-        out_shape=jax.ShapeDtypeStruct((requests, rounds, hid.shape[1]), BF),
+        out_shape=jax.ShapeDtypeStruct((rounds, requests, hid.shape[1]), BF),
         compiler_params=SMALL,
         name="draft_norm",
     )(hid, gain, *parts)
@@ -477,15 +480,17 @@
     bits = bits_of(lines)
     chunk = rounds * requests
     others = rounds * rows - chunk
-    ext, hid, mark = prep(inputs, [list(range(draft))], columns)
-    hid, rest_hid = hid[:chunk], hid[chunk:]
+    ext, hid, rest_hid, mark = prep(inputs, [list(range(draft))], columns)
     hid_beside = links.line(hid, bits[0])
 
     lined, offsets, crossed = [ext], [0], [links.far(ext)]
     for bit in bits:
-        came = [links.line(block, bit) for block in lined]
+        came = [links.line(block, bit) for block in lined[len(lined) > 1 :]]
+        if len(lined) > 1:
+            came = [near_line] + came
         if bit == bits[0]:
-            came = hold(came, crossed[-1:])
+            near_line = links.line(ext, bits[-1])
+            came = hold(came, [crossed[0], near_line])
         lined = lined + came
         offsets = offsets + [offset | bit for offset in offsets]
         crossed = crossed + [links.far(block) for block in came]
@@ -528,15 +533,15 @@
                 summed[offset] = add(blocks[offset])
                 blocks[offset ^ bit].append(links.line(summed[offset], bit))
     rest_terms = blocks[0]
-    features, draft_in = mid(hid, hid_beside, sums, draft_gain.reshape(1, width), [summed[lines - 1], blocks[lines // 2][1]])
+    features, draft_in = mid(hid, hid_beside, sums, draft_gain.reshape(1, width), [summed[lines - 1]])
     a_lined = [draft_in]
     for bit in bits[1:]:
         a_lined = a_lined + [links.line(block, bit) for block in a_lined]
     a_crossed = [links.far(block) for block in a_lined]
-    own = [pack(a_lined, [summed[1]]), pack(a_crossed, [])]
+    own = [pack(a_lined, [blocks[lines // 2][1]]), pack(a_crossed, [summed[1], summed[lines // 2]])]
     pieces = own + [links.near(piece) for piece in own]
-    halves = links.meet(units(pieces, mark, draft_weights, False, [summed[lines // 2]]))
-    held = links.meet_line(halves, [], lambda odd: [])
+    halves = links.meet(units(pieces, mark, draft_weights, False, []))
+    held = links.meet_line(halves, [], lambda odd: [blocks[0][1], blocks[0][2]])
     keep, send = add([held], [], 2)
     terms = [keep, links.line(send, bits[0])]
 
@@ -547,7 +552,7 @@
         rows,
         rounds,
     )
-    return verified.transpose(1, 0, 2), draft_out.transpose(1, 0, 2)
+    return verified.transpose(1, 0, 2), draft_out
 
 
 def solution(mesh):

time: 126 us -> 123 us (0.976)
  local copies, waits for them, and re-layouts: 1.62 us -> 0.06 us
    ppermute x14, waiting for transfers between devices: 20.7 us -> 14.4 us  [far(): return lax.ppermute(x, 'tensor', [(i, i ^ 2) for i in range(self.columns)])]
    ppermute x12, waiting for transfers between devices: 28 us -> 33.1 us  [line(): return lax.ppermute(x, 'expert', [(i, i ^ bits) for i in range(self.lines)])]
    ppermute x12, starting transfers between devices: 22.3 us -> 20.9 us  [line(): return lax.ppermute(x, 'expert', [(i, i ^ bits) for i in range(self.lines)])]
  transfers between devices with their start and end apart: 38 -> 38, of which waited for: 17 -> 15; matrix products, arithmetic and copies ran while one was open for 1% -> 0% of each run, Pallas kernels for 20% -> 21%
where the time goes in v4:
time: 123 us
  waiting for transfers between devices  51.6 us (42%)
  starting transfers between devices  39.5 us (32%)
  Pallas kernels  31.1 us (25%)
    ppermute x12, waiting for transfers between devices, line(): return lax.ppermute(x, 'expert', [(i, i ^ bits) for i in range(self.lines)])  33.1 us
    ppermute x12, starting transfers between devices, line(): return lax.ppermute(x, 'expert', [(i, i ^ bits) for i in range(self.lines)])  20.9 us
    ppermute x14, starting transfers between devices, far(): return lax.ppermute(x, 'tensor', [(i, i ^ 2) for i in range(self.columns)])  16.3 us
    pallas_call x4, Pallas kernels, units(): pl.pallas_call(functools.partial(unit_kernel, gated, parts, group), out_s...  15.3 us
    ppermute x14, waiting for transfers between devices, far(): return lax.ppermute(x, 'tensor', [(i, i ^ 2) for i in range(self.columns)])  14.4 us
    pallas_call x1, Pallas kernels, stage(): pl.pallas_call(functools.partial(stage_kernel, count), out_shape=[struct(...  9.11 us
    ppermute x12, waiting for transfers between devices, near(): return lax.ppermute(x, 'tensor', [(i, i ^ 1) for i in range(self.columns)])  4.08 us
    pallas_call x1, Pallas kernels, prep(): pl.pallas_call(functools.partial(prep_kernel, groups, columns, inputs[-1]...  2.65 us
  transfers between devices with their start and end apart: 38, of which 15 were waited for; matrix products, arithmetic and copies ran while one was open for 0% of the time, Pallas kernels for 21%

profile of v4, /device:TPU:0, one launch (start us, length us, event | category | flops | bytes accessed | tf_op | source)
XLA Modules:
  0.0 123.3 jit_solution(13202075856552727613)
XLA Ops:
  0.6 2.7 %prep.1 = (bf16[40,4224]{1,0:T(8,128)(2,1)}, bf16[8,4096]{1,0:T(8,128)(2,1)}, bf16[32,4096]{1,0:T(8,128)(2,1)}, f32[1,128]{1,0:T(1,128)}) custom-call(s32[2,4]{1,0:T(2,128)} %bitcast.15, bf16[10,4,4096]{2,1,0:T(4,128)(2,1)} %bitcast.20, s32[4,8,10]{2,1,0:T(8,128)} %bitcast.23, f32[1,4096]{1,0:T(1,128)} %bitcast.24, bf16[16,4096]{1,0:T(8,128)(2,1)} %bitcast.22), custom_call_target="tpu_custom_call" | custom-call | tf_op jit(solution)/shard_map/prep/pallas_call | solution.py:140
  3.3 3.1 %collective-permute-start.3 = (bf16[40,4224]{1,0:T(8,128)(2,1)}, bf16[40,4224]{1,0:T(8,128)(2,1)S(1)}, u32[]{:S(2)}, u32[]{:S(2)}) collective-permute-start(bf16[40,4224]{1,0:T(8,128)(2,1)} %get-tuple-element.43.refs_0_), channel_id=1, source_target_pairs={{0,4},{4,0},{8,12},{12,8},{1,5},{5,1},{9,13},{13,9},{2,6},{6,2},{1... | collective-permute-start | bytes 1013768 | tf_op jit(solution)/shard_map/ppermute | solution.py:413
  7.9 2.6 %collective-permute-start.1 = (bf16[40,4224]{1,0:T(8,128)(2,1)}, bf16[40,4224]{1,0:T(8,128)(2,1)S(1)}, u32[]{:S(2)}, u32[]{:S(2)}) collective-permute-start(bf16[40,4224]{1,0:T(8,128)(2,1)} %get-tuple-element.43.refs_0_), channel_id=1, source_target_pairs={{0,8},{4,12},{8,0},{12,4},{1,9},{5,13},{9,1},{13,5},{2,10},{6,14},... | collective-permute-start | bytes 1013768 | tf_op jit(solution)/shard_map/ppermute | solution.py:413
  10.5 10.0 %collective-permute-done.3.refs_2_ = bf16[40,4224]{1,0:T(8,128)(2,1)S(1)} collective-permute-done((bf16[40,4224]{1,0:T(8,128)(2,1)}, bf16[40,4224]{1,0:T(8,128)(2,1)S(1)}, u32[]{:S(2)}, u32[]{:S(2)}) %collective-permute-start.3) | collective-permute-done | bytes 337952 | tf_op jit(solution)/shard_map/ppermute | solution.py:413
  20.4 5.1 %collective-permute-done.1.refs_0_ = bf16[40,4224]{1,0:T(8,128)(2,1)S(1)} collective-permute-done((bf16[40,4224]{1,0:T(8,128)(2,1)}, bf16[40,4224]{1,0:T(8,128)(2,1)S(1)}, u32[]{:S(2)}, u32[]{:S(2)}) %collective-permute-start.1) | collective-permute-done | bytes 337952 | tf_op jit(solution)/shard_map/ppermute | solution.py:413
  27.5 5.2 %collective-permute-done.4.refs_3_ = bf16[40,4224]{1,0:T(8,128)(2,1)S(1)} collective-permute-done((bf16[40,4224]{1,0:T(8,128)(2,1)S(1)}, bf16[40,4224]{1,0:T(8,128)(2,1)S(1)}, u32[]{:S(2)}, u32[]{:S(2)}) %collective-permute-start.4) | collective-permute-done | bytes 337952 | tf_op jit(solution)/shard_map/ppermute | solution.py:413
  34.9 9.1 %stage.1 = (bf16[4096,768]{1,0:T(8,128)(2,1)S(1)}, bf16[4096,768]{1,0:T(8,128)(2,1)S(1)}, bf16[768,4096]{1,0:T(8,128)(2,1)}) custom-call(bf16[4096,768]{1,0:T(8,128)(2,1)} %bitcast.17, bf16[4096,768]{1,0:T(8,128)(2,1)} %bitcast.18, bf16[768,4096]{1,0:T(8,128)(2,1)} %bitcast.19, bf16[40,4224]{1,0:T(8,128)(2,1)S(1)} %collective-permute-done.4.refs_3_), custom_call_target="tpu_custom_call" | custom-call | tf_op jit(solution)/shard_map/stage/pallas_call | solution.py:218
  44.2 3.3 %collective-permute-done.7.refs_3_ = bf16[40,4224]{1,0:T(8,128)(2,1)S(1)} collective-permute-done((bf16[40,4224]{1,0:T(8,128)(2,1)S(1)}, bf16[40,4224]{1,0:T(8,128)(2,1)S(1)}, u32[]{:S(2)}, u32[]{:S(2)}) %collective-permute-start.7) | collective-permute-done | bytes 337952 | tf_op jit(solution)/shard_map/ppermute | solution.py:416
  50.0 2.8 %experts.3 = (bf16[32,4096]{1,0:T(8,128)(2,1)S(1)}, bf16[32,4096]{1,0:T(8,128)(2,1)S(1)}, bf16[32,4096]{1,0:T(8,128)(2,1)S(1)}, bf16[32,4096]{1,0:T(8,128)(2,1)S(1)}) custom-call(f32[1,128]{1,0:T(1,128)S(1)} %copy-done.8, bf16[32,4224]{1,0:T(8,128)(2,1)S(1)} %cut.4.refs_0_, bf16[32,4224]{1,0:T(8,128)(2,1)S(1)} %cut.5.refs_1_, ...), custom_call_target="tpu_custom_call" | custom-call | tf_op jit(solution)/shard_map/experts/pallas_call | solution.py:309
  56.1 5.2 %experts.4 = (bf16[128,4096]{1,0:T(8,128)(2,1)S(1)}, bf16[128,4096]{1,0:T(8,128)(2,1)S(1)}) custom-call(f32[1,128]{1,0:T(1,128)S(1)} %copy-done.8, bf16[128,4224]{1,0:T(8,128)(2,1)S(1)} %cut.6.refs_0_, bf16[128,4224]{1,0:T(8,128)(2,1)S(1)} %collective-permute-done.14.refs_1_, bf16[4096,768]{1,0:T(8,128)(2,1)S(1)} %get-tuple-element.44.refs_4_.refs_2_, ...), custom_call_target="tpu_custom_call" | custom-call | tf_op jit(solution)/shard_map/experts/pallas_call | solution.py:309
  62.3 5.4 %experts.5 = (bf16[128,4096]{1,0:T(8,128)(2,1)S(1)}, bf16[128,4096]{1,0:T(8,128)(2,1)S(1)}) custom-call(f32[1,128]{1,0:T(1,128)S(1)} %copy-done.8, bf16[128,4224]{1,0:T(8,128)(2,1)S(1)} %cut.7.refs_0_, bf16[128,4224]{1,0:T(8,128)(2,1)S(1)} %collective-permute-done.16.refs_1_, bf16[4096,768]{1,0:T(8,128)(2,1)S(1)} %get-tuple-element.44.refs_4_.refs_2_, ...), custom_call_target="tpu_custom_call" | custom-call | tf_op jit(solution)/shard_map/experts/pallas_call | solution.py:309
  69.7 2.1 %collective-permute-start.17 = (bf16[16,4096]{1,0:T(8,128)(2,1)S(1)}, bf16[16,4096]{1,0:T(8,128)(2,1)S(1)}, u32[]{:S(2)}, u32[]{:S(2)}) collective-permute-start(bf16[16,4096]{1,0:T(8,128)(2,1)S(1)} %add.9.refs_1_.held_ref), channel_id=1, source_target_pairs={{0,8},{4,12},{8,0},{12,4},{1,9},{5,13},{9,1},{13,5},{2,10},{6,14},... | collective-permute-start | bytes 393224 | tf_op jit(solution)/shard_map/ppermute | solution.py:413
  74.1 3.2 %collective-permute-done.20.refs_1_ = bf16[32,4096]{1,0:T(8,128)(2,1)S(1)} collective-permute-done((bf16[32,4096]{1,0:T(8,128)(2,1)S(1)}, bf16[32,4096]{1,0:T(8,128)(2,1)S(1)}, u32[]{:S(2)}, u32[]{:S(2)}) %collective-permute-start.20) | collective-permute-done | bytes 262176 | tf_op jit(solution)/shard_map/ppermute | solution.py:416
  77.4 1.8 %collective-permute-start.25 = (bf16[32,4096]{1,0:T(8,128)(2,1)S(1)}, bf16[32,4096]{1,0:T(8,128)(2,1)S(1)}, u32[]{:S(2)}, u32[]{:S(2)}) collective-permute-start(bf16[32,4096]{1,0:T(8,128)(2,1)S(1)} %add.10.refs_1_), channel_id=1, source_target_pairs={{0,4},{4,0},{8,12},{12,8},{1,5},{5,1},{9,13},{13,9},{2,6},{6,2},{1... | collective-permute-start | bytes 786440 | tf_op jit(solution)/shard_map/ppermute | solution.py:413
  81.2 6.5 %collective-permute-done.27.refs_1_ = bf16[16,4096]{1,0:T(8,128)(2,1)S(1)} collective-permute-done((bf16[16,4096]{1,0:T(8,128)(2,1)S(1)}, bf16[16,4096]{1,0:T(8,128)(2,1)S(1)}, u32[]{:S(2)}, u32[]{:S(2)}) %collective-permute-start.27) | collective-permute-done | bytes 131104 | tf_op jit(solution)/shard_map/ppermute | solution.py:413
  89.6 1.8 %collective-permute-done.28.refs_0_ = bf16[16,4096]{1,0:T(8,128)(2,1)S(1)} collective-permute-done((bf16[16,4096]{1,0:T(8,128)(2,1)S(1)}, bf16[16,4096]{1,0:T(8,128)(2,1)S(1)}, u32[]{:S(2)}, u32[]{:S(2)}) %collective-permute-start.28) | collective-permute-done | bytes 131104 | tf_op jit(solution)/shard_map/ppermute | solution.py:416
  91.4 2.4 %collective-permute-done.29.refs_1_ = bf16[16,4096]{1,0:T(8,128)(2,1)S(1)} collective-permute-done((bf16[16,4096]{1,0:T(8,128)(2,1)S(1)}, bf16[16,4096]{1,0:T(8,128)(2,1)S(1)}, u32[]{:S(2)}, u32[]{:S(2)}) %collective-permute-start.29) | collective-permute-done | bytes 131104 | tf_op jit(solution)/shard_map/ppermute | solution.py:416
  95.4 1.9 %drafter.1 = (bf16[32,4096]{1,0:T(8,128)(2,1)S(1)}, bf16[32,4096]{1,0:T(8,128)(2,1)S(1)}, bf16[32,4096]{1,0:T(8,128)(2,1)S(1)}, bf16[32,4096]{1,0:T(8,128)(2,1)S(1)}) custom-call(f32[1,128]{1,0:T(1,128)S(1)} %copy-done.8, bf16[32,4096]{1,0:T(8,128)(2,1)S(1)} %pack.2.refs_0_, bf16[32,4096]{1,0:T(8,128)(2,1)S(1)} %pack.3.refs_1_, ...), custom_call_target="tpu_custom_call" | custom-call | tf_op jit(solution)/shard_map/drafter/pallas_call | solution.py:309
  102.4 2.8 %collective-permute-start.26 = (bf16[32,4096]{1,0:T(8,128)(2,1)S(1)}, bf16[32,4096]{1,0:T(8,128)(2,1)S(1)}, u32[]{:S(2)}, u32[]{:S(2)}) collective-permute-start(bf16[32,4096]{1,0:T(8,128)(2,1)S(1)} %add.12.refs_3_), channel_id=1, source_target_pairs={{0,8},{4,12},{8,0},{12,4},{1,9},{5,13},{9,1},{13,5},{2,10},{6,14},... | collective-permute-start | bytes 786440 | tf_op jit(solution)/shard_map/ppermute | solution.py:413
  106.3 3.7 %collective-permute-done.35.refs_1_ = bf16[16,4096]{1,0:T(8,128)(2,1)S(1)} collective-permute-done((bf16[16,4096]{1,0:T(8,128)(2,1)S(1)}, bf16[16,4096]{1,0:T(8,128)(2,1)S(1)}, u32[]{:S(2)}, u32[]{:S(2)}) %collective-permute-start.35) | collective-permute-done | bytes 131104 | tf_op jit(solution)/shard_map/ppermute | solution.py:416
  110.0 1.8 %collective-permute-start.36 = (bf16[16,4096]{1,0:T(8,128)(2,1)S(1)}, bf16[16,4096]{1,0:T(8,128)(2,1)S(1)}, u32[]{:S(2)}, u32[]{:S(2)}) collective-permute-start(bf16[16,4096]{1,0:T(8,128)(2,1)S(1)} %add.13), channel_id=1, source_target_pairs={{0,4},{4,0},{8,12},{12,8},{1,5},{5,1},{9,13},{13,9},{2,6},{6,2},{1... | collective-permute-start | bytes 393224 | tf_op jit(solution)/shard_map/ppermute | solution.py:413
  111.8 3.4 %collective-permute-done.23.refs_4_ = bf16[32,4096]{1,0:T(8,128)(2,1)S(1)} collective-permute-done((bf16[32,4096]{1,0:T(8,128)(2,1)S(1)}, bf16[32,4096]{1,0:T(8,128)(2,1)S(1)}, u32[]{:S(2)}, u32[]{:S(2)}) %collective-permute-start.23) | collective-permute-done | bytes 262176 | tf_op jit(solution)/shard_map/ppermute | solution.py:413
  115.2 1.9 %collective-permute-done.36.refs_2_ = bf16[16,4096]{1,0:T(8,128)(2,1)S(1)} collective-permute-done((bf16[16,4096]{1,0:T(8,128)(2,1)S(1)}, bf16[16,4096]{1,0:T(8,128)(2,1)S(1)}, u32[]{:S(2)}, u32[]{:S(2)}) %collective-permute-start.36) | collective-permute-done | bytes 131104 | tf_op jit(solution)/shard_map/ppermute | solution.py:413
  117.2 2.6 %collective-permute-start.37 = (bf16[8,4096]{1,0:T(8,128)(2,1)S(1)}, bf16[8,4096]{1,0:T(8,128)(2,1)S(1)}, u32[]{:S(2)}, u32[]{:S(2)}) collective-permute-start(bf16[8,4096]{1,0:T(8,128)(2,1)S(1)} %get-tuple-element.79), channel_id=1, source_target_pairs={{0,8},{4,12},{8,0},{12,4},{1,9},{5,13},{9,1},{13,5},{2,10},{6,14},... | collective-permute-start | bytes 196616 | tf_op jit(solution)/shard_map/ppermute | solution.py:413
  (109 shorter events, 31.9 us)
Async XLA Ops:
  3.3 17.1 %collective-permute-start.3 = (bf16[40,4224]{1,0:T(8,128)(2,1)}, bf16[40,4224]{1,0:T(8,128)(2,1)S(1)}, u32[]{:S(2)}, u32[]{:S(2)}) collective-permute-start(bf16[40,4224]{1,0:T(8,128)(2,1)} %get-tuple-element.43.refs_0_), channel_id=1, source_target_pairs={{0,4},{4,0},{8,12},{12,8},{1,5},{5,1},{9,13},{13,9},{2,6},{6,2},{1... | collective-permute-start | bytes 1013768 | tf_op jit(solution)/shard_map/ppermute | solution.py:413
  6.4 14.0 %collective-permute-start.2 = (bf16[40,4224]{1,0:T(8,128)(2,1)}, bf16[40,4224]{1,0:T(8,128)(2,1)S(1)}, u32[]{:S(2)}, u32[]{:S(2)}) collective-permute-start(bf16[40,4224]{1,0:T(8,128)(2,1)} %get-tuple-element.43.refs_0_), channel_id=1, source_target_pairs={{0,2},{1,3},{2,0},{3,1},{4,6},{5,7},{6,4},{7,5},{8,10},{9,11},{10,... | collective-permute-start | bytes 1013768 | tf_op jit(solution)/shard_map/ppermute | solution.py:416
  7.9 17.6 %collective-permute-start.1 = (bf16[40,4224]{1,0:T(8,128)(2,1)}, bf16[40,4224]{1,0:T(8,128)(2,1)S(1)}, u32[]{:S(2)}, u32[]{:S(2)}) collective-permute-start(bf16[40,4224]{1,0:T(8,128)(2,1)} %get-tuple-element.43.refs_0_), channel_id=1, source_target_pairs={{0,8},{4,12},{8,0},{12,4},{1,9},{5,13},{9,1},{13,5},{2,10},{6,14},... | collective-permute-start | bytes 1013768 | tf_op jit(solution)/shard_map/ppermute | solution.py:413
  25.5 7.2 %collective-permute-start.4 = (bf16[40,4224]{1,0:T(8,128)(2,1)S(1)}, bf16[40,4224]{1,0:T(8,128)(2,1)S(1)}, u32[]{:S(2)}, u32[]{:S(2)}) collective-permute-start(bf16[40,4224]{1,0:T(8,128)(2,1)S(1)} %hold.3.refs_1_), channel_id=1, source_target_pairs={{0,4},{4,0},{8,12},{12,8},{1,5},{5,1},{9,13},{13,9},{2,6},{6,2},{1... | collective-permute-start | bytes 1013768 | tf_op jit(solution)/shard_map/ppermute | solution.py:413
  25.5 18.7 %collective-permute-start.5 = (bf16[40,4224]{1,0:T(8,128)(2,1)S(1)}, bf16[40,4224]{1,0:T(8,128)(2,1)S(1)}, u32[]{:S(2)}, u32[]{:S(2)}) collective-permute-start(bf16[40,4224]{1,0:T(8,128)(2,1)S(1)} %hold.3.refs_1_), channel_id=1, source_target_pairs={{0,2},{1,3},{2,0},{3,1},{4,6},{5,7},{6,4},{7,5},{8,10},{9,11},{10,... | collective-permute-start | bytes 1013768 | tf_op jit(solution)/shard_map/ppermute | solution.py:416
  26.1 18.1 %collective-permute-start.6 = (bf16[40,4224]{1,0:T(8,128)(2,1)S(1)}, bf16[40,4224]{1,0:T(8,128)(2,1)S(1)}, u32[]{:S(2)}, u32[]{:S(2)}) collective-permute-start(bf16[40,4224]{1,0:T(8,128)(2,1)S(1)} %collective-permute-done.3.refs_2_), channel_id=1, source_target_pairs={{0,2},{1,3},{2,0},{3,1},{4,6},{5,7},{6,4},{7,5},{8,10},{9,11},{10,... | collective-permute-start | bytes 1013768 | tf_op jit(solution)/shard_map/ppermute | solution.py:416
  32.7 14.9 %collective-permute-start.7 = (bf16[40,4224]{1,0:T(8,128)(2,1)S(1)}, bf16[40,4224]{1,0:T(8,128)(2,1)S(1)}, u32[]{:S(2)}, u32[]{:S(2)}) collective-permute-start(bf16[40,4224]{1,0:T(8,128)(2,1)S(1)} %collective-permute-done.4.refs_3_), channel_id=1, source_target_pairs={{0,2},{1,3},{2,0},{3,1},{4,6},{5,7},{6,4},{7,5},{8,10},{9,11},{10,... | collective-permute-start | bytes 1013768 | tf_op jit(solution)/shard_map/ppermute | solution.py:416
  33.2 11.0 %collective-permute-start = (bf16[8,4096]{1,0:T(8,128)(2,1)}, bf16[8,4096]{1,0:T(8,128)(2,1)S(1)}, u32[]{:S(2)}, u32[]{:S(2)}) collective-permute-start(bf16[8,4096]{1,0:T(8,128)(2,1)} %get-tuple-element.41.hid_ref), channel_id=1, source_target_pairs={{0,8},{4,12},{8,0},{12,4},{1,9},{5,13},{9,1},{13,5},{2,10},{6,14},... | collective-permute-start | bytes 196616 | tf_op jit(solution)/shard_map/ppermute | solution.py:413
  49.6 12.7 %collective-permute-start.16 = (bf16[128,4224]{1,0:T(8,128)(2,1)S(1)}, bf16[128,4224]{1,0:T(8,128)(2,1)S(1)}, u32[]{:S(2)}, u32[]{:S(2)}) collective-permute-start(bf16[128,4224]{1,0:T(8,128)(2,1)S(1)} %cut.7.refs_0_), channel_id=1, source_target_pairs={{0,1},{1,0},{2,3},{3,2},{4,5},{5,4},{6,7},{7,6},{8,9},{9,8},{10,11... | collective-permute-start | bytes 3244040 | tf_op jit(solution)/shard_map/ppermute | solution.py:419
  54.5 6.8 %collective-permute-start.13 = (bf16[16,4096]{1,0:T(8,128)(2,1)S(1)}, bf16[16,4096]{1,0:T(8,128)(2,1)S(1)}, u32[]{:S(2)}, u32[]{:S(2)}) collective-permute-start(bf16[16,4096]{1,0:T(8,128)(2,1)S(1)} %get-tuple-element.54.refs_5_), channel_id=1, source_target_pairs={{0,2},{1,3},{2,0},{3,1},{4,6},{5,7},{6,4},{7,5},{8,10},{9,11},{10,... | collective-permute-start | bytes 393224 | tf_op jit(solution)/shard_map/ppermute | solution.py:416
  68.2 9.2 %collective-permute-start.20 = (bf16[32,4096]{1,0:T(8,128)(2,1)S(1)}, bf16[32,4096]{1,0:T(8,128)(2,1)S(1)}, u32[]{:S(2)}, u32[]{:S(2)}) collective-permute-start(bf16[32,4096]{1,0:T(8,128)(2,1)S(1)} %get-tuple-element.60), channel_id=1, source_target_pairs={{0,2},{1,3},{2,0},{3,1},{4,6},{5,7},{6,4},{7,5},{8,10},{9,11},{10,... | collective-permute-start | bytes 786440 | tf_op jit(solution)/shard_map/ppermute | solution.py:416
  69.7 9.5 %collective-permute-start.17 = (bf16[16,4096]{1,0:T(8,128)(2,1)S(1)}, bf16[16,4096]{1,0:T(8,128)(2,1)S(1)}, u32[]{:S(2)}, u32[]{:S(2)}) collective-permute-start(bf16[16,4096]{1,0:T(8,128)(2,1)S(1)} %add.9.refs_1_.held_ref), channel_id=1, source_target_pairs={{0,8},{4,12},{8,0},{12,4},{1,9},{5,13},{9,1},{13,5},{2,10},{6,14},... | collective-permute-start | bytes 393224 | tf_op jit(solution)/shard_map/ppermute | solution.py:413
  71.8 17.5 %collective-permute-start.22 = (bf16[32,4096]{1,0:T(8,128)(2,1)S(1)}, bf16[32,4096]{1,0:T(8,128)(2,1)S(1)}, u32[]{:S(2)}, u32[]{:S(2)}) collective-permute-start(bf16[32,4096]{1,0:T(8,128)(2,1)S(1)} %get-tuple-element.66), channel_id=1, source_target_pairs={{0,2},{1,3},{2,0},{3,1},{4,6},{5,7},{6,4},{7,5},{8,10},{9,11},{10,... | collective-permute-start | bytes 786440 | tf_op jit(solution)/shard_map/ppermute | solution.py:416
  73.6 15.8 %collective-permute-start.24 = (bf16[32,4096]{1,0:T(8,128)(2,1)S(1)}, bf16[32,4096]{1,0:T(8,128)(2,1)S(1)}, u32[]{:S(2)}, u32[]{:S(2)}) collective-permute-start(bf16[32,4096]{1,0:T(8,128)(2,1)S(1)} %get-tuple-element.68), channel_id=1, source_target_pairs={{0,2},{1,3},{2,0},{3,1},{4,6},{5,7},{6,4},{7,5},{8,10},{9,11},{10,... | collective-permute-start | bytes 786440 | tf_op jit(solution)/shard_map/ppermute | solution.py:416
  77.4 12.1 %collective-permute-start.25 = (bf16[32,4096]{1,0:T(8,128)(2,1)S(1)}, bf16[32,4096]{1,0:T(8,128)(2,1)S(1)}, u32[]{:S(2)}, u32[]{:S(2)}) collective-permute-start(bf16[32,4096]{1,0:T(8,128)(2,1)S(1)} %add.10.refs_1_), channel_id=1, source_target_pairs={{0,4},{4,0},{8,12},{12,8},{1,5},{5,1},{9,13},{13,9},{2,6},{6,2},{1... | collective-permute-start | bytes 786440 | tf_op jit(solution)/shard_map/ppermute | solution.py:413
  79.4 8.4 %collective-permute-start.27 = (bf16[16,4096]{1,0:T(8,128)(2,1)S(1)}, bf16[16,4096]{1,0:T(8,128)(2,1)S(1)}, u32[]{:S(2)}, u32[]{:S(2)}) collective-permute-start(bf16[16,4096]{1,0:T(8,128)(2,1)S(1)} %get-tuple-element.69.refs_0_), channel_id=1, source_target_pairs={{0,4},{4,0},{8,12},{12,8},{1,5},{5,1},{9,13},{13,9},{2,6},{6,2},{1... | collective-permute-start | bytes 393224 | tf_op jit(solution)/shard_map/ppermute | solution.py:413
  79.8 11.6 %collective-permute-start.28 = (bf16[16,4096]{1,0:T(8,128)(2,1)S(1)}, bf16[16,4096]{1,0:T(8,128)(2,1)S(1)}, u32[]{:S(2)}, u32[]{:S(2)}) collective-permute-start(bf16[16,4096]{1,0:T(8,128)(2,1)S(1)} %get-tuple-element.69.refs_0_), channel_id=1, source_target_pairs={{0,2},{1,3},{2,0},{3,1},{4,6},{5,7},{6,4},{7,5},{8,10},{9,11},{10,... | collective-permute-start | bytes 393224 | tf_op jit(solution)/shard_map/ppermute | solution.py:416
  97.6 7.6 %collective-permute-start.32 = (bf16[32,4096]{1,0:T(8,128)(2,1)S(1)}, bf16[32,4096]{1,0:T(8,128)(2,1)S(1)}, u32[]{:S(2)}, u32[]{:S(2)}) collective-permute-start(bf16[32,4096]{1,0:T(8,128)(2,1)S(1)} %get-tuple-element.71), channel_id=1, source_target_pairs={{0,1},{1,0},{2,3},{3,2},{4,5},{5,4},{6,7},{7,6},{8,9},{9,8},{10,11... | collective-permute-start | bytes 786440 | tf_op jit(solution)/shard_map/ppermute | solution.py:419
  98.0 13.8 %collective-permute-start.21 = (bf16[32,4096]{1,0:T(8,128)(2,1)S(1)}, bf16[32,4096]{1,0:T(8,128)(2,1)S(1)}, u32[]{:S(2)}, u32[]{:S(2)}) collective-permute-start(bf16[32,4096]{1,0:T(8,128)(2,1)S(1)} %get-tuple-element.64), channel_id=1, source_target_pairs={{0,2},{1,3},{2,0},{3,1},{4,6},{5,7},{6,4},{7,5},{8,10},{9,11},{10,... | collective-permute-start | bytes 786440 | tf_op jit(solution)/shard_map/ppermute | solution.py:416
  99.5 10.4 %collective-permute-start.35 = (bf16[16,4096]{1,0:T(8,128)(2,1)S(1)}, bf16[16,4096]{1,0:T(8,128)(2,1)S(1)}, u32[]{:S(2)}, u32[]{:S(2)}) collective-permute-start(bf16[16,4096]{1,0:T(8,128)(2,1)S(1)} %get-tuple-element.77), channel_id=1, source_target_pairs={{0,2},{1,3},{2,0},{3,1},{4,6},{5,7},{6,4},{7,5},{8,10},{9,11},{10,... | collective-permute-start | bytes 393224 | tf_op jit(solution)/shard_map/ppermute | solution.py:416
  100.6 14.6 %collective-permute-start.23 = (bf16[32,4096]{1,0:T(8,128)(2,1)S(1)}, bf16[32,4096]{1,0:T(8,128)(2,1)S(1)}, u32[]{:S(2)}, u32[]{:S(2)}) collective-permute-start(bf16[32,4096]{1,0:T(8,128)(2,1)S(1)} %add.11.refs_2_), channel_id=1, source_target_pairs={{0,4},{4,0},{8,12},{12,8},{1,5},{5,1},{9,13},{13,9},{2,6},{6,2},{1... | collective-permute-start | bytes 786440 | tf_op jit(solution)/shard_map/ppermute | solution.py:413
  102.4 17.5 %collective-permute-start.26 = (bf16[32,4096]{1,0:T(8,128)(2,1)S(1)}, bf16[32,4096]{1,0:T(8,128)(2,1)S(1)}, u32[]{:S(2)}, u32[]{:S(2)}) collective-permute-start(bf16[32,4096]{1,0:T(8,128)(2,1)S(1)} %add.12.refs_3_), channel_id=1, source_target_pairs={{0,8},{4,12},{8,0},{12,4},{1,9},{5,13},{9,1},{13,5},{2,10},{6,14},... | collective-permute-start | bytes 786440 | tf_op jit(solution)/shard_map/ppermute | solution.py:413
  105.2 10.0 %collective-permute-start.34 = (bf16[16,4096]{1,0:T(8,128)(2,1)S(1)}, bf16[16,4096]{1,0:T(8,128)(2,1)S(1)}, u32[]{:S(2)}, u32[]{:S(2)}) collective-permute-start(bf16[16,4096]{1,0:T(8,128)(2,1)S(1)} %get-tuple-element.75), channel_id=1, source_target_pairs={{0,2},{1,3},{2,0},{3,1},{4,6},{5,7},{6,4},{7,5},{8,10},{9,11},{10,... | collective-permute-start | bytes 393224 | tf_op jit(solution)/shard_map/ppermute | solution.py:416
  110.0 7.1 %collective-permute-start.36 = (bf16[16,4096]{1,0:T(8,128)(2,1)S(1)}, bf16[16,4096]{1,0:T(8,128)(2,1)S(1)}, u32[]{:S(2)}, u32[]{:S(2)}) collective-permute-start(bf16[16,4096]{1,0:T(8,128)(2,1)S(1)} %add.13), channel_id=1, source_target_pairs={{0,4},{4,0},{8,12},{12,8},{1,5},{5,1},{9,13},{13,9},{2,6},{6,2},{1... | collective-permute-start | bytes 393224 | tf_op jit(solution)/shard_map/ppermute | solution.py:413
  (26 other events, 255.4 us)
